TPU v7x, 256 devices: a whole 4x4x8 slice. The times are simulated.
256 devices in a mesh: grp: 8 (over z), seq: 32 (over y, x, core).
Axes of the slice: x: 4, y: 4, z: 8, core: 2. Of those that a mesh axis runs over, the one named last changes fastest.
Arguments:
- cache_hidden: bfloat16 [16384, 5120], P(('grp', 'seq')), parts along dimension 0, may hold values from -12 to 12
- group_hidden: bfloat16 [2048, 5120], P(('grp', 'seq')), parts along dimension 0, may hold values from -12 to 12
- proj_weight: bfloat16 [5120, 32, 3, 128], P(None, 'seq'), may hold values from -1 to 1
- row_place: int32 [16384], P(('grp', 'seq')), parts along dimension 0, may hold values from 0 to 2047, as said below
- cache_len: int32 [256], P('grp'), parts along dimension 0, may hold values from 1 to 64, as said below
- group_place: int32 [2048], P(('grp', 'seq')), parts along dimension 0, may hold values from 0 to 255, each once
Outputs:
- attended: bfloat16 [2048, 4096], P(('grp', 'seq')), parts along dimension 0
There are 8 independent parts, one for each index of `grp`. A program takes and returns all parts, laid end to end along the dimension named above; an argument that names none is the same for every part. Nothing has to cross between parts.
Inputs may be any that keep to these rules, and one draw needn't show every extreme that they name: `row_place`: each session position appears exactly once; the 64 rows of every device hold exactly 48 live positions. `cache_len`: the lengths sum to 1536; some owner full. `group_place`: each turn position appears exactly once.
All inputs are finite; a program needn't handle non-finite values.
Results may differ from a plain program's by a relative error of at most 0.009.
Values may be sent and summed in bfloat16 or wider, within the bound.
No kernel may reach another device: no remote copies, remote signals or barrier semaphores. Data moves between devices by JAX's collectives and lax.ppermute only.
A program may use at most 128 MiB of HBM per device.

v0:
```python
import jax
import jax.numpy as jnp
from jax import lax
from jax.sharding import PartitionSpec as P

MASKED_SCORE = -1e30


def shards(cache_hidden, group_hidden, proj_weight, row_place, cache_len, group_place):
    head_dim = proj_weight.shape[3]
    width = proj_weight.shape[0]
    score_scale = head_dim ** (-0.5)
    cycle_size = lax.axis_size("seq")
    cache_rows = cache_hidden.shape[0]
    group_rows = group_hidden.shape[0]
    session = cache_rows * cycle_size
    local_weight = proj_weight.reshape(width, 3 * head_dim)
    kv_weight = local_weight[:, head_dim:]
    all_places, all_group, all_group_places = (
        lax.all_gather(row_place, "seq", axis=0, tiled=True),
        lax.all_gather(group_hidden, "seq", axis=0, tiled=True),
        lax.all_gather(group_place, "seq", axis=0, tiled=True),
    )
    moved_kv = jnp.dot(
        lax.all_gather(cache_hidden, "seq", axis=0, tiled=True),
        kv_weight,
        preferred_element_type=jnp.float32,
    ).astype(jnp.bfloat16)
    restored = jnp.zeros((session, 2 * head_dim), jnp.bfloat16).at[all_places].set(moved_kv)
    fresh_qkv = jnp.dot(all_group, local_weight, preferred_element_type=jnp.float32).astype(
        jnp.bfloat16
    )
    positions = jnp.arange(session, dtype=jnp.int32)
    live_keys = positions % cache_rows < cache_len[positions // cache_rows]
    seen_keys = all_group_places[None, :] <= all_group_places[:, None]
    tokens = fresh_qkv.shape[0]
    visible = jnp.concatenate(
        [jnp.broadcast_to(live_keys[None, :], (tokens, session)), seen_keys], axis=1
    )
    queries = fresh_qkv[:, :head_dim]
    key_rows = jnp.concatenate(
        [restored[:, :head_dim], fresh_qkv[:, head_dim : 2 * head_dim]], axis=0
    )
    value_rows = jnp.concatenate([restored[:, head_dim:], fresh_qkv[:, 2 * head_dim :]], axis=0)
    scores = jnp.dot(queries, key_rows.T, preferred_element_type=jnp.float32) * score_scale
    scores = jnp.where(visible, scores, MASKED_SCORE)
    row_top = jnp.max(scores, axis=1, keepdims=True)
    weights = jnp.exp(scores - row_top)
    row_total = jnp.sum(weights, axis=1, keepdims=True)
    rounded = weights.astype(jnp.bfloat16)
    summed = jnp.dot(rounded, value_rows, preferred_element_type=jnp.float32)
    head_out = (summed / row_total).astype(jnp.bfloat16)
    landed = lax.all_to_all(head_out[:, None, :], "seq", split_axis=0, concat_axis=1, tiled=True)
    return landed.reshape(group_rows, landed.shape[1] * head_dim)


def solution(mesh):
    in_specs = (
        P(("grp", "seq"), None),
        P(("grp", "seq"), None),
        P(None, "seq", None, None),
        P(("grp", "seq")),
        P("grp"),
        P(("grp", "seq")),
    )
    out_specs = P(("grp", "seq"), None)
    return jax.shard_map(shards, mesh=mesh, in_specs=in_specs, out_specs=out_specs, check_vma=False)
```

profile of v0, /device:TPU:1, one launch (start us, length us, event | category | flops | bytes accessed | tf_op | source)
XLA Modules:
  0.0 196.2 jit_solution(8036642946576812318)
XLA Ops:
  6.5 0.0 all-gather.3.cloned.1.call-start
  6.5 0.7 all-gather.3.cloned.1.call-update
  7.3 0.0 all-gather.5.cloned.1.call-start
  7.3 0.7 all-gather.5.cloned.1.call-update
  8.0 1.3 dynamic-slice
  10.6 0.0 copy-start
  10.6 0.0 copy-start.1
  10.6 0.0 copy-start.2
  10.6 6.3 %copy.10 = bf16[5120,1,3,128]{0,3,2,1:T(8,128)(2,1)} copy(bf16[5120,1,3,128]{3,0,2,1:T(8,128)(2,1)} %param.8) | data formatting | bytes 7864320 | tf_op args[2]
  18.1 0.0 copy-done
  18.1 0.7 fusion.38
  18.8 0.7 fusion.37
  19.5 4.4 %compare_select_fusion.1 = s32[2048,1]{0,1:T(1,128)S(1)} fusion(s32[]{:T(128)} %bitcast.25, s32[]{:T(128)} %bitcast.26, s32[]{:T(128)} %bitcast.27, s32[]{:T(128)} %bitcast.28, s32[]{:T(128)} %bitcast.29, s32[]{:T(128)} %bitcast.31, s32[]{:T(128)} %bitcast.30), kind=kLoop, calls=%fused_computation.52 | loop fusion | flops 47104 | bytes 8220 | tf_op jit(solution)/shard_map/gather | solution.py:34
  24.0 15.5 %fusion.29 = pred[2048]{0:T(1024)(128)(4,1)S(1)} fusion(pred[2048]{0:T(1024)(128)(4,1)S(1)} %compare_reduce_fusion, pred[2048]{0:T(1024)(128)(4,1)S(1)} %compare_reduce_fusion.1, pred[2048]{0:T(1024)(128)(4,1)S(1)} %compare_reduce_fusion.2, pred[2048]{0:T(1024)(128)(4,1)S(1)} %compare_reduce_fusion.3, pred[2048]{0:T(1024)(128)(4,1)S(1)} %compare_reduce_fusion.4, ...), kind=kLoop, calls=%fused_computation.64 | loop fusion | flops 65536 | bytes 61540 | tf_op jit(solution)/shard_map/lt | solution.py:34
  39.5 0.3 dynamic-update-slice.1
  39.8 0.2 dynamic-update-slice
  40.0 15.4 %all-reduce.2 = (s32[256]{0:T(256)S(1)}, s32[2048]{0:T(1024)S(1)}) all-reduce(s32[256]{0:T(256)S(1)} %dynamic-update-slice, s32[2048]{0:T(1024)S(1)} %dynamic-update-slice.1), channel_id=1, replica_groups=mesh['grp'=8,'seq'=32] {'seq'}, use_global_device_ids=true, to_apply=%add | all-reduce | flops 2304 | bytes 18432
  55.5 0.1 broadcast_compare_fusion
  55.6 8.3 %all-gather.3.cloned.1.call-done = bf16[256,5120]{1,0:T(8,128)(2,1)} async-done(((bf16[8,5120]{1,0:T(8,128)(2,1)}), bf16[256,5120]{1,0:T(8,128)(2,1)}) %all-gather.3.cloned.1.call-update) | async-done | bytes 2621456 | tf_op jit(solution)/shard_map/all_gather | solution.py:21
  63.9 4.4 %convolution_convert_fusion = bf16[256,384]{1,0:T(8,128)(2,1)S(1)} fusion(bf16[256,5120]{1,0:T(8,128)(2,1)} %all-gather.3.cloned.1.call-done, bf16[5120,384]{0,1:T(8,128)(2,1)} %bitcast.48), kind=kOutput, calls=%fused_computation.11 | convolution fusion | flops 1006731264 | bytes 6750208 | tf_op jit(solution)/shard_map/dot_general | solution.py:30
  68.4 84.6 %all-gather.5.cloned.1.call-done = bf16[2048,5120]{1,0:T(8,128)(2,1)} async-done(((bf16[64,5120]{1,0:T(8,128)(2,1)}), bf16[2048,5120]{1,0:T(8,128)(2,1)}) %all-gather.5.cloned.1.call-update) | async-done | bytes 20971536 | tf_op jit(solution)/shard_map/all_gather | solution.py:25
  153.0 10.6 %fusion.3 = bf16[2048,256]{1,0:T(8,128)(2,1)S(1)} fusion(bf16[2048,5120]{1,0:T(8,128)(2,1)} %all-gather.5.cloned.1.call-done, bf16[5120,384]{0,1:T(8,128)(2,1)} %bitcast.49), kind=kOutput, calls=%fused_computation.5 | convolution fusion | flops 5369233408 | bytes 24641536 | tf_op jit(solution)/shard_map/dot_general | solution.py:24
  163.6 9.6 %scatter_custom_fusion = bf16[2048,256]{1,0:T(8,128)(2,1)S(1)} fusion(s32[2048]{0:T(1024)S(1)} %compare_select_fusion.7, bf16[2048,256]{1,0:T(8,128)(2,1)S(1)} %fusion.3, bf16[]{:T(256)} %constant.40.clone.1), kind=kCustom, calls=%fused_computation.21 | custom fusion | bytes 1048578 | tf_op jit(solution)/shard_map/scatter | solution.py:29
  173.2 0.1 fusion.35
  173.3 0.6 fusion.39
  173.9 0.5 fusion.6
  174.4 0.6 fusion.17
  175.0 0.5 broadcast.317
  175.5 0.7 reduce.50
  176.2 12.5 %all_to_all.15 = bf16[32,2,512]{2,1,0:T(2,128)(2,1)S(1)} all-to-all(bf16[32,2,512]{2,1,0:T(2,128)(2,1)S(1)} %reshape.231), channel_id=1, replica_groups=mesh['grp'=8,'seq'=32] {'seq'}, dimensions={0} | all-to-all | bytes 131072 | tf_op jit(solution)/shard_map/all_to_all | solution.py:53
  188.6 0.1 reshape.232
  188.7 0.6 copy.14
  (33 shorter events, 1.2 us)
Async XLA Ops:
  6.5 57.4 %all-gather.3.cloned.1.call-start = ((), (), s32[]{:S(2)}) async-start(), calls=%async_computation.1 | async-start | bytes 2703360 | tf_op jit(solution)/shard_map/all_gather | solution.py:21
  7.3 145.8 %all-gather.5.cloned.1.call-start = ((), (), s32[]{:S(2)}) async-start(), calls=%async_computation.2 | async-start | bytes 21626880 | tf_op jit(solution)/shard_map/all_gather | solution.py:25
  10.6 7.5 %copy-start = (s32[32]{0:T(128)S(1)}, s32[32]{0:T(128)}, u32[]{:S(2)}) copy-start(s32[32]{0:T(128)} %param.10) | copy-start | bytes 388
  10.6 28.9 %copy-start.1 = (s32[64]{0:T(128)S(1)}, s32[64]{0:T(128)}, u32[]{:S(2)}) copy-start(s32[64]{0:T(128)} %param.9) | copy-start | bytes 772
  10.6 29.2 %copy-start.2 = (s32[8]{0:T(128)S(1)}, s32[8]{0:T(128)}, u32[]{:S(2)}) copy-start(s32[8]{0:T(128)} %param.11) | copy-start | bytes 100
Sparse Core Ops, SparseCore 0:
  9.9 53.9 all-gather.2
  66.5 86.4 all-gather.4
where the time goes:
time: 197 us; the launch traced here: 196 us
  waiting for transfers between devices  94.3 us (48%)
  blocking collectives  27.9 us (14%)
  other arithmetic  22.3 us (11%)
  local copies, waits for them, and re-layouts  20.5 us (10%)
  matrix products  16.2 us (8%)
  between operations  14.9 us (8%)
    all_gather x1, waiting for transfers between devices, shards(): lax.all_gather(cache_hidden, 'seq', axis=0, tiled=True)  84.6 us
    lt x1, other arithmetic, shards(): live_keys = positions % cache_rows < cache_len[positions // cache_rows]  15.5 us
    unnamed x1, blocking collectives  15.4 us
    all_to_all x1, blocking collectives, shards(): lax.all_to_all(head_out[:, None, :], 'seq', split_axis=0, concat_axis=1,...  12.5 us
    dot_general x1, matrix products, shards(): jnp.dot(lax.all_gather(cache_hidden, 'seq', axis=0, tiled=True), kv_weigh...  10.6 us
    scatter x1, local copies, waits for them, and re-layouts, shards(): jnp.zeros((session, 2 * head_dim), jnp.bfloat16).at[all_places]  9.57 us
    unnamed x14, local copies, waits for them, and re-layouts  8.86 us
    all_gather x1, waiting for transfers between devices, shards(): lax.all_gather(group_hidden, 'seq', axis=0, tiled=True)  8.34 us
  transfers between devices with their start and end apart: 2, of which 2 were waited for; matrix products, arithmetic and copies ran while one was open for 18% of the time, Pallas kernels for 0%

commit v1 on v0

v1 whole, which is shorter than its diff:
```python
import functools

import jax
import jax.numpy as jnp
import numpy as np
from jax import lax
from jax.experimental import pallas as pl
from jax.experimental.pallas import tpu as pltpu
from jax.sharding import PartitionSpec as P

MASKED_SCORE = -1e30
NY, NX = 4, 4
LIVE = 48
HD = 128
TURN = 8
BF16 = jnp.bfloat16
F32 = jnp.float32


def index_of(y, x, c):
    return (y % NY * NX + x % NX) * 2 + c


def ring_pairs(step, first):
    pairs = []
    for y in range(NY):
        for x in range(NX):
            for c in range(2):
                along_x = (c == 0) == first
                dy, dx = (0, step) if along_x else (step, 0)
                pairs.append((index_of(y, x, c), index_of(y + dy, x + dx, c)))
    return pairs


A_UP, A_DOWN = ring_pairs(1, True), ring_pairs(-1, True)
B_UP, B_DOWN = ring_pairs(1, False), ring_pairs(-1, False)
SWAP = [(i, i ^ 1) for i in range(2 * NY * NX)]
OFFSETS = (0, -1, 1, -2)


def token_owner_table():
    table = np.zeros((2 * NY * NX, 2 * NY * NX), np.int32)
    for y in range(NY):
        for x in range(NX):
            for c in range(2):
                row = []
                for core in (c, 1 - c):
                    for b in OFFSETS:
                        for a in OFFSETS:
                            dy, dx = (b, a) if core == 0 else (a, b)
                            row.append(index_of(y + dy, x + dx, core))
                table[index_of(y, x, c)] = row
    return table


def send(value, pairs):
    return lax.ppermute(value, "seq", pairs)


def pack_kernel(place_ref, len_ref, rows_ref, out_ref):
    n = rows_ref.shape[0]
    block = n
    i0 = lax.broadcasted_iota(jnp.int32, (n, n), 0)
    i1 = lax.broadcasted_iota(jnp.int32, (n, n), 1)
    place_col = jnp.sum(jnp.where(i0 == i1, place_ref[...], 0), axis=1, keepdims=True)
    owner = place_col // block
    inner = place_col - owner * block
    owners = len_ref.shape[1]
    o1 = lax.broadcasted_iota(jnp.int32, (n, owners), 1)
    length = jnp.sum(jnp.where(o1 == owner, len_ref[...], 0), axis=1, keepdims=True)
    live_col = (inner < length).astype(jnp.int32)
    live_row = jnp.sum(jnp.where(i0 == i1, live_col, 0), axis=0, keepdims=True)
    rank_row = jnp.sum(jnp.where(i0 < i1, live_col, 0), axis=0, keepdims=True)
    k0 = lax.broadcasted_iota(jnp.int32, (LIVE, n), 0)
    pick = jnp.where((k0 == rank_row) & (live_row > 0), 1.0, 0.0).astype(BF16)
    out_ref[...] = jnp.dot(pick, rows_ref[...], preferred_element_type=F32).astype(BF16)


def pack(row_place, cache_len, cache_hidden):
    n, d = cache_hidden.shape
    return pl.pallas_call(
        pack_kernel,
        out_shape=jax.ShapeDtypeStruct((LIVE, d), BF16),
        cost_estimate=pl.CostEstimate(flops=2 * n * LIVE * d, bytes_accessed=4 * n * d, transcendentals=0),
        name="pack_live",
    )(row_place.reshape(1, n), cache_len.reshape(1, -1), cache_hidden)


def turn_kernel(a, b, c, d, pa, pb, pc, pd, own_ref, other_ref, q_ref, kv_ref, acc):
    k = pl.program_id(0)

    @pl.when(k == 0)
    def _():
        acc[...] = jnp.zeros_like(acc)

    x = jnp.concatenate([a[...], b[...], c[...], d[...]], axis=0)
    w = jnp.concatenate(
        [own_ref[0], other_ref[0], own_ref[1], own_ref[2], other_ref[1], other_ref[2]], axis=1
    )
    acc[...] += jnp.dot(x, w, preferred_element_type=F32)

    @pl.when(k == pl.num_programs(0) - 1)
    def _():
        q_ref[:, : 2 * HD] = acc[:, : 2 * HD].astype(BF16)
        q_ref[:, 2 * HD :] = jnp.concatenate([pa[...], pb[...], pc[...], pd[...]], axis=0)
        kv_ref[...] = acc[:, 2 * HD :].astype(BF16)


def turn_project(blocks, own, other, kb=1024):
    m = blocks[0].shape[0]
    d = own.shape[1]
    xs = pl.BlockSpec((m, kb), lambda k: (0, k))
    ps = pl.BlockSpec((m, HD), lambda k: (0, d // HD))
    ws = pl.BlockSpec((3, kb, HD), lambda k: (0, k, 0))
    return pl.pallas_call(
        turn_kernel,
        grid=(d // kb,),
        in_specs=[xs] * 4 + [ps] * 4 + [ws] * 2,
        out_specs=[
            pl.BlockSpec((4 * m, 3 * HD), lambda k: (0, 0)),
            pl.BlockSpec((4 * m, 4 * HD), lambda k: (0, 0)),
        ],
        out_shape=[
            jax.ShapeDtypeStruct((4 * m, 3 * HD), BF16),
            jax.ShapeDtypeStruct((4 * m, 4 * HD), BF16),
        ],
        scratch_shapes=[pltpu.VMEM((4 * m, 6 * HD), F32)],
        compiler_params=pltpu.CompilerParams(vmem_limit_bytes=24 * 2**20),
        cost_estimate=pl.CostEstimate(
            flops=2 * 4 * m * d * 6 * HD, bytes_accessed=2 * d * (4 * m + 6 * HD), transcendentals=0
        ),
        name="project_turn",
    )(*blocks, *blocks, own, other)


def cache_kernel(a, b, c, d, own_ref, other_ref, kv_ref, acc):
    k = pl.program_id(0)

    @pl.when(k == 0)
    def _():
        acc[...] = jnp.zeros_like(acc)

    x = jnp.concatenate([a[...], b[...], c[...], d[...]], axis=0)
    w = jnp.concatenate([own_ref[0], own_ref[1], other_ref[0], other_ref[1]], axis=1)
    acc[...] += jnp.dot(x, w, preferred_element_type=F32)

    @pl.when(k == pl.num_programs(0) - 1)
    def _():
        kv_ref[...] = acc[...].astype(BF16)


def cache_project(shards, own, other, kb=1024):
    m, d = shards[0].shape
    xs = pl.BlockSpec((m, kb), lambda k: (0, k))
    ws = [
        pl.BlockSpec((pl.Element(2), pl.Element(kb), pl.Element(HD)), lambda k: (1, k * kb, 0))
        for _ in range(2)
    ]
    return pl.pallas_call(
        cache_kernel,
        grid=(d // kb,),
        in_specs=[xs] * 4 + ws,
        out_specs=pl.BlockSpec((4 * m, 4 * HD), lambda k: (0, 0)),
        out_shape=jax.ShapeDtypeStruct((4 * m, 4 * HD), BF16),
        scratch_shapes=[pltpu.VMEM((4 * m, 4 * HD), F32)],
        compiler_params=pltpu.CompilerParams(vmem_limit_bytes=24 * 2**20),
        cost_estimate=pl.CostEstimate(
            flops=2 * 4 * m * d * 4 * HD, bytes_accessed=2 * d * (4 * m + 4 * HD), transcendentals=0
        ),
        name="project_cache",
    )(*shards, own, other)


def attend_kernel(core_ref, dest_ref, q_ref, qs_ref, kvf_ref, k0, k1, k2, k3, out_ref):
    core = core_ref[0]
    q_place = jnp.concatenate([q_ref[:, 2 * HD :], qs_ref[:, 2 * HD :]], axis=0).astype(F32)
    k_place = q_ref[:, 2 * HD :].astype(F32).T[0:1, :]
    seen = k_place <= q_place[:, 0:1]
    outs, tops, totals = [], [], []
    for h in range(2):
        q = jnp.concatenate(
            [q_ref[:, h * HD : (h + 1) * HD], qs_ref[:, (1 - h) * HD : (2 - h) * HD]], axis=0
        )
        ks = slice(2 * h * HD, (2 * h + 1) * HD)
        vs = slice((2 * h + 1) * HD, (2 * h + 2) * HD)
        scale = HD ** (-0.5)
        nt = (((1,), (1,)), ((), ()))
        s = [
            lax.dot_general(q, r[:, ks], nt, preferred_element_type=F32) * scale
            for r in (k0, k1, k2, k3)
        ]
        f = lax.dot_general(q, kvf_ref[:, ks], nt, preferred_element_type=F32) * scale
        s.append(jnp.where(seen, f, MASKED_SCORE))
        top = functools.reduce(
            jnp.maximum, [jnp.max(t, axis=1, keepdims=True) for t in s]
        )
        total = jnp.zeros_like(top)
        summed = jnp.zeros((q.shape[0], HD), F32)
        for t, r in zip(s, (k0, k1, k2, k3, kvf_ref)):
            e = jnp.exp(t - top)
            total += jnp.sum(e, axis=1, keepdims=True)
            summed += jnp.dot(e.astype(BF16), r[:, vs], preferred_element_type=F32)
        outs.append(summed)
        tops.append(top)
        totals.append(total)
    first = core == 0
    lane = lax.broadcasted_iota(jnp.int32, (outs[0].shape[0], HD), 1)
    stats = []
    for h in range(2):
        stats.append(jnp.where(lane % 64 < 32, tops[h], totals[h]))
    low = jnp.where(first, outs[0], outs[1])
    high = jnp.where(first, outs[1], outs[0])
    stat = jnp.where(
        lane < 64, jnp.where(first, stats[0], stats[1]), jnp.where(first, stats[1], stats[0])
    )
    whole = jnp.concatenate([low, high, stat], axis=1)
    for g in range(out_ref.shape[0]):
        out_ref[dest_ref[g]] = whole[g * TURN : (g + 1) * TURN]


def attend(core, dest, q, q_swapped, kv_turn, kv_cache):
    n = dest.shape[0]
    smem = pl.BlockSpec(memory_space=pltpu.SMEM)
    vmem = pl.BlockSpec(memory_space=pltpu.VMEM)
    keys = 128 + 4 * 192
    return pl.pallas_call(
        attend_kernel,
        in_specs=[smem, smem] + [vmem] * 7,
        out_specs=vmem,
        out_shape=jax.ShapeDtypeStruct((n, TURN, 3 * HD), F32),
        compiler_params=pltpu.CompilerParams(vmem_limit_bytes=24 * 2**20),
        cost_estimate=pl.CostEstimate(
            flops=2 * 2 * 2 * 256 * keys * HD, bytes_accessed=2 * 2**20, transcendentals=2 * 256 * keys
        ),
        name="attend",
    )(core, dest, q, q_swapped, kv_turn, *kv_cache)


def combine_kernel(in_ref, out_ref):
    for j in range(in_ref.shape[0] // 2):
        for h in range(2):
            cols = slice(h * HD, (h + 1) * HD)
            at = 2 * HD + 64 * h
            o0, o1 = in_ref[2 * j, :, cols], in_ref[2 * j + 1, :, cols]
            m0, m1 = in_ref[2 * j, :, at : at + 1], in_ref[2 * j + 1, :, at : at + 1]
            l0, l1 = in_ref[2 * j, :, at + 32 : at + 33], in_ref[2 * j + 1, :, at + 32 : at + 33]
            top = jnp.maximum(m0, m1)
            e0, e1 = jnp.exp(m0 - top), jnp.exp(m1 - top)
            out = (o0 * e0 + o1 * e1) / (l0 * e0 + l1 * e1)
            out_ref[:, (2 * j + h) * HD : (2 * j + h + 1) * HD] = out.astype(BF16)


def combine(parts):
    n, t, _ = parts.shape
    return pl.pallas_call(
        combine_kernel,
        out_shape=jax.ShapeDtypeStruct((t, n * HD), BF16),
        cost_estimate=pl.CostEstimate(flops=n * t * HD * 8, bytes_accessed=n * t * HD * 14, transcendentals=n * t),
        name="combine",
    )(parts)


def shards(cache_hidden, group_hidden, proj_weight, row_place, cache_len, group_place):
    me = lax.axis_index("seq")
    dest = lax.dynamic_index_in_dim(jnp.asarray(token_owner_table()), me, 0, keepdims=False)
    core = (me % 2).astype(jnp.int32).reshape(1)

    places = jnp.broadcast_to(group_place.astype(BF16)[:, None], (group_place.shape[0], HD))
    g = jnp.concatenate([group_hidden, places], axis=1)
    own = jnp.transpose(proj_weight[:, 0], (1, 0, 2))
    other = send(own, SWAP)

    g_up, g_down = send(g, A_UP), send(g, A_DOWN)
    block = jnp.concatenate([g, g_up, g_down, send(g_up, A_UP)], axis=0)
    b_up, b_down = send(block, B_UP), send(block, B_DOWN)
    q, kv_turn = turn_project([block, b_up, b_down, send(b_up, B_UP)], own, other)
    q_swapped = send(q, SWAP)

    s = pack(row_place, cache_len, cache_hidden)
    half = LIVE // 2
    up, down = send(s, A_UP), send(s, A_DOWN)
    far = jnp.concatenate([send(up[:half], A_UP), send(down[half:], A_DOWN)], axis=0)
    near = [s, up, down, far]
    ups = [send(v, B_UP) for v in near]
    downs = [send(v, B_DOWN) for v in near]
    fars = [send(v, B_UP) for v in ups[:2]] + [send(v, B_DOWN) for v in downs[2:]]
    kv = [cache_project(v, own, other) for v in (near, ups, downs, fars)]

    parts = attend(core, dest, q, q_swapped, kv_turn, kv)
    landed = lax.all_to_all(parts, "seq", split_axis=0, concat_axis=0, tiled=True)
    return combine(landed)


def solution(mesh):
    in_specs = (
        P(("grp", "seq"), None),
        P(("grp", "seq"), None),
        P(None, "seq", None, None),
        P(("grp", "seq")),
        P("grp"),
        P(("grp", "seq")),
    )
    out_specs = P(("grp", "seq"), None)
    return jax.shard_map(shards, mesh=mesh, in_specs=in_specs, out_specs=out_specs, check_vma=False)
```

time: 197 us -> 118 us (0.60)
  waiting for transfers between devices: 94.3 us -> 35.1 us
  Pallas kernels: 0 us -> 31.1 us
  starting transfers between devices: 0.04 us -> 29.2 us
  other arithmetic: 22.3 us -> 2.47 us
  matrix products: 16.2 us -> 0 us
  local copies, waits for them, and re-layouts: 20.5 us -> 5.57 us
  between operations: 14.9 us -> 0.21 us
  blocking collectives: 27.9 us -> 13.7 us
    all_gather x2 -> x0, waiting for transfers between devices: 92.9 us -> none  [the longest x1 84.6 us: shards(): lax.all_gather(cache_hidden, 'seq', axis=0, tiled=True)]
    ppermute x0 -> x24, waiting for transfers between devices: none -> 35.1 us  [send(): return lax.ppermute(value, 'seq', pairs)]
    pallas_call x0 -> x8, Pallas kernels: none -> 31.1 us  [the longest x4 19.2 us: cache_project(): pl.pallas_call(cache_kernel, grid=(d // kb,), in_specs=[xs] * 4 + ws, out...]
    ppermute x0 -> x24, starting transfers between devices: none -> 29.2 us  [send(): return lax.ppermute(value, 'seq', pairs)]
    dot_general x4 -> x0, matrix products: 16.2 us -> none  [the longest x1 10.6 us: shards(): jnp.dot(lax.all_gather(cache_hidden, 'seq', axis=0, tiled=True), kv_weigh...]
    lt x1 -> x0, other arithmetic: 15.5 us -> none  [shards(): live_keys = positions % cache_rows < cache_len[positions // cache_rows]]
    unnamed x1 -> x0, blocking collectives: 15.4 us -> none
    scatter x1 -> x0, local copies, waits for them, and re-layouts: 9.57 us -> none  [shards(): jnp.zeros((session, 2 * head_dim), jnp.bfloat16).at[all_places]]
  transfers between devices with their start and end apart: 2 -> 24, of which waited for: 2 -> 9; matrix products, arithmetic and copies ran while one was open for 18% -> 3% of each run, Pallas kernels for 0% -> 23%
where the time goes in v1:
time: 118 us; the launch traced here: 117 us
  waiting for transfers between devices  35.1 us (30%)
  Pallas kernels  31.1 us (26%)
  starting transfers between devices  29.2 us (25%)
  blocking collectives  13.7 us (12%)
  local copies, waits for them, and re-layouts  5.57 us (5%)
  other arithmetic  2.47 us (2%)
    ppermute x24, waiting for transfers between devices, send(): return lax.ppermute(value, 'seq', pairs)  35.1 us
    ppermute x24, starting transfers between devices, send(): return lax.ppermute(value, 'seq', pairs)  29.2 us
    pallas_call x4, Pallas kernels, cache_project(): pl.pallas_call(cache_kernel, grid=(d // kb,), in_specs=[xs] * 4 + ws, out...  19.2 us
    all_to_all x1, blocking collectives, shards(): lax.all_to_all(parts, 'seq', split_axis=0, concat_axis=0, tiled=True)  13.7 us
    pallas_call x1, Pallas kernels, turn_project(): pl.pallas_call(turn_kernel, grid=(d // kb,), in_specs=[xs] * 4 + [ps] * 4...  5.47 us
    unnamed x19, local copies, waits for them, and re-layouts  4.75 us
    pallas_call x1, Pallas kernels, pack(): pl.pallas_call(pack_kernel, out_shape=jax.ShapeDtypeStruct((LIVE, d), BF1...  2.44 us
  transfers between devices with their start and end apart: 24, of which 9 were waited for; matrix products, arithmetic and copies ran while one was open for 3% of the time, Pallas kernels for 23%

profile of v1, /device:TPU:1, one launch (start us, length us, event | category | flops | bytes accessed | tf_op | source)
XLA Modules:
  0.0 117.4 jit_solution(12628004502633097815)
XLA Ops:
  0.0 3.2 %collective-permute-start.6 = (bf16[3,5120,128]{2,1,0:T(8,128)(2,1)}, bf16[3,5120,128]{2,1,0:T(8,128)(2,1)}, u32[]{:S(2)}, u32[]{:S(2)}) collective-permute-start(bf16[3,5120,128]{2,1,0:T(8,128)(2,1)} %bitcast.8), channel_id=1, source_target_pairs={{0,1},{1,0},{2,3},{3,2},{4,5},{5,4},{6,7},{7,6},{8,9},{9,8},{10,11... | collective-permute-start | bytes 11796488 | tf_op jit(solution)/shard_map/ppermute | solution.py:57
  3.2 2.4 %pack_live.1.a = bf16[48,5120]{1,0:T(8,128)(2,1)} custom-call(s32[1,64]{1,0:T(1,128)} %bitcast.14, s32[1,32]{1,0:T(1,128)} %bitcast.15, bf16[64,5120]{1,0:T(8,128)(2,1)} %rows_ref.1), custom_call_target="tpu_custom_call" | custom-call | flops 31457280 | bytes 1310720 | tf_op jit(solution)/shard_map/pack_live/pallas_call | solution.py:81
  6.4 0.9 pad_maximum_fusion.1
  7.3 0.9 collective-permute-start
  8.2 1.9 %collective-permute-start.1 = (bf16[8,5248]{1,0:T(8,128)(2,1)S(1)}, bf16[8,5248]{1,0:T(8,128)(2,1)S(1)}, u32[]{:S(2)}, u32[]{:S(2)}) collective-permute-start(bf16[8,5248]{1,0:T(8,128)(2,1)S(1)} %pad_maximum_fusion.1), channel_id=1, source_target_pairs={{0,6},{1,25},{2,0},{3,27},{4,2},{5,29},{6,4},{7,31},{8,14},{9,1},{... | collective-permute-start | bytes 251912 | tf_op jit(solution)/shard_map/ppermute | solution.py:57
  10.1 5.9 %collective-permute-done = bf16[8,5248]{1,0:T(8,128)(2,1)S(1)} collective-permute-done((bf16[8,5248]{1,0:T(8,128)(2,1)S(1)}, bf16[8,5248]{1,0:T(8,128)(2,1)S(1)}, u32[]{:S(2)}, u32[]{:S(2)}) %collective-permute-start) | collective-permute-done | bytes 84000 | tf_op jit(solution)/shard_map/ppermute | solution.py:57
  16.0 2.7 %collective-permute-start.9 = (bf16[48,5120]{1,0:T(8,128)(2,1)}, bf16[48,5120]{1,0:T(8,128)(2,1)S(1)}, u32[]{:S(2)}, u32[]{:S(2)}) collective-permute-start(bf16[48,5120]{1,0:T(8,128)(2,1)} %pack_live.1.a), channel_id=1, source_target_pairs={{0,6},{1,25},{2,0},{3,27},{4,2},{5,29},{6,4},{7,31},{8,14},{9,1},{... | collective-permute-start | bytes 1474568 | tf_op jit(solution)/shard_map/ppermute | solution.py:57
  18.7 2.8 %collective-permute-start.16 = (bf16[48,5120]{1,0:T(8,128)(2,1)}, bf16[48,5120]{1,0:T(8,128)(2,1)S(1)}, u32[]{:S(2)}, u32[]{:S(2)}) collective-permute-start(bf16[48,5120]{1,0:T(8,128)(2,1)} %pack_live.1.a), channel_id=1, source_target_pairs={{0,24},{1,7},{2,26},{3,1},{4,28},{5,3},{6,30},{7,5},{8,0},{9,15},{... | collective-permute-start | bytes 1474568 | tf_op jit(solution)/shard_map/ppermute | solution.py:57
  21.4 0.9 pad_maximum_fusion.a.pa
  22.4 2.6 %collective-permute-done.9.c = bf16[48,5120]{1,0:T(8,128)(2,1)S(1)} collective-permute-done((bf16[48,5120]{1,0:T(8,128)(2,1)}, bf16[48,5120]{1,0:T(8,128)(2,1)S(1)}, u32[]{:S(2)}, u32[]{:S(2)}) %collective-permute-start.9) | collective-permute-done | bytes 491552 | tf_op jit(solution)/shard_map/ppermute | solution.py:57
  25.2 5.4 %collective-permute-done.10 = bf16[24,5120]{1,0:T(8,128)(2,1)S(1)} collective-permute-done((bf16[24,5120]{1,0:T(8,128)(2,1)S(1)}, bf16[24,5120]{1,0:T(8,128)(2,1)S(1)}, u32[]{:S(2)}, u32[]{:S(2)}) %collective-permute-start.10) | collective-permute-done | bytes 245792 | tf_op jit(solution)/shard_map/ppermute | solution.py:57
  32.2 1.8 %collective-permute-done.3.b.pb = bf16[32,5248]{1,0:T(8,128)(2,1)S(1)} collective-permute-done((bf16[32,5248]{1,0:T(8,128)(2,1)S(1)}, bf16[32,5248]{1,0:T(8,128)(2,1)S(1)}, u32[]{:S(2)}, u32[]{:S(2)}) %collective-permute-start.3) | collective-permute-done | bytes 335904 | tf_op jit(solution)/shard_map/ppermute | solution.py:57
  34.0 1.9 %collective-permute-done.11 = bf16[24,5120]{1,0:T(8,128)(2,1)S(1)} collective-permute-done((bf16[24,5120]{1,0:T(8,128)(2,1)S(1)}, bf16[24,5120]{1,0:T(8,128)(2,1)S(1)}, u32[]{:S(2)}, u32[]{:S(2)}) %collective-permute-start.11) | collective-permute-done | bytes 245792 | tf_op jit(solution)/shard_map/ppermute | solution.py:57
  36.0 2.0 %collective-permute-done.4.c.pc = bf16[32,5248]{1,0:T(8,128)(2,1)S(1)} collective-permute-done((bf16[32,5248]{1,0:T(8,128)(2,1)S(1)}, bf16[32,5248]{1,0:T(8,128)(2,1)S(1)}, u32[]{:S(2)}, u32[]{:S(2)}) %collective-permute-start.4) | collective-permute-done | bytes 335904 | tf_op jit(solution)/shard_map/ppermute | solution.py:57
  37.9 1.0 collective-permute-start.18
  38.9 11.1 %collective-permute-done.5.d.pd = bf16[32,5248]{1,0:T(8,128)(2,1)S(1)} collective-permute-done((bf16[32,5248]{1,0:T(8,128)(2,1)S(1)}, bf16[32,5248]{1,0:T(8,128)(2,1)S(1)}, u32[]{:S(2)}, u32[]{:S(2)}) %collective-permute-start.5) | collective-permute-done | bytes 335904 | tf_op jit(solution)/shard_map/ppermute | solution.py:57
  50.0 2.7 %collective-permute-start.19 = (bf16[48,5120]{1,0:T(8,128)(2,1)S(1)}, bf16[48,5120]{1,0:T(8,128)(2,1)}, u32[]{:S(2)}, u32[]{:S(2)}) collective-permute-start(bf16[48,5120]{1,0:T(8,128)(2,1)S(1)} %constant_dynamic-update-slice_fusion.d), channel_id=1, source_target_pairs={{0,24},{1,7},{2,26},{3,1},{4,28},{5,3},{6,30},{7,5},{8,0},{9,15},{... | collective-permute-start | bytes 1474568 | tf_op jit(solution)/shard_map/ppermute | solution.py:57
  52.7 0.8 copy-done.5
  53.8 1.1 collective-permute-start.20
  54.9 3.9 %collective-permute-done.15.d = bf16[48,5120]{1,0:T(8,128)(2,1)S(1)} collective-permute-done((bf16[48,5120]{1,0:T(8,128)(2,1)S(1)}, bf16[48,5120]{1,0:T(8,128)(2,1)S(1)}, u32[]{:S(2)}, u32[]{:S(2)}) %collective-permute-start.15) | collective-permute-done | bytes 491552 | tf_op jit(solution)/shard_map/ppermute | solution.py:57
  59.7 2.7 %collective-permute-start.22 = (bf16[48,5120]{1,0:T(8,128)(2,1)}, bf16[48,5120]{1,0:T(8,128)(2,1)}, u32[]{:S(2)}, u32[]{:S(2)}) collective-permute-start(bf16[48,5120]{1,0:T(8,128)(2,1)} %collective-permute-done.18.c), channel_id=1, source_target_pairs={{0,24},{1,7},{2,26},{3,1},{4,28},{5,3},{6,30},{7,5},{8,0},{9,15},{... | collective-permute-start | bytes 1474568 | tf_op jit(solution)/shard_map/ppermute | solution.py:57
  63.1 2.1 %copy-done = bf16[5120,1,3,128]{3,0,2,1:T(8,128)(2,1)S(1)} copy-done((bf16[5120,1,3,128]{3,0,2,1:T(8,128)(2,1)S(1)}, bf16[5120,1,3,128]{3,0,2,1:T(8,128)(2,1)}, u32[]{:S(2)}) %copy-start) | copy-done | bytes 3932184
  65.3 1.0 copy-done.2
  66.3 4.7 %project_cache.4.k0 = bf16[192,512]{1,0:T(8,128)(2,1)S(1)} custom-call(bf16[48,5120]{1,0:T(8,128)(2,1)S(1)} %copy-done.2, bf16[48,5120]{1,0:T(8,128)(2,1)S(1)} %collective-permute-done.8.b, bf16[48,5120]{1,0:T(8,128)(2,1)S(1)} %collective-permute-done.9.c, bf16[48,5120]{1,0:T(8,128)(2,1)S(1)} %constant_dynamic-update-slice_fusion.d, ...), custom_call_target="tpu_custom_call" | custom-call | flops 1006632960 | bytes 7208960 | tf_op jit(solution)/shard_map/project_cache/pallas_call | solution.py:159
  71.1 5.5 %project_turn.1 = (bf16[128,384]{1,0:T(8,128)(2,1)S(1)}, bf16[128,512]{1,0:T(8,128)(2,1)S(1)}) custom-call(bf16[32,5248]{1,0:T(8,128)(2,1)S(1)} %pad_maximum_fusion.a.pa, bf16[32,5248]{1,0:T(8,128)(2,1)S(1)} %collective-permute-done.3.b.pb, bf16[32,5248]{1,0:T(8,128)(2,1)S(1)} %collective-permute-done.4.c.pc, ...), custom_call_target="tpu_custom_call" | custom-call | flops 1006632960 | bytes 9175040 | tf_op jit(solution)/shard_map/project_turn/pallas_call | solution.py:115
  76.6 4.7 %project_cache.5.k1 = bf16[192,512]{1,0:T(8,128)(2,1)S(1)} custom-call(bf16[48,5120]{1,0:T(8,128)(2,1)S(1)} %collective-permute-done.12.a, bf16[48,5120]{1,0:T(8,128)(2,1)} %collective-permute-done.13.b, bf16[48,5120]{1,0:T(8,128)(2,1)S(1)} %copy-done.6, bf16[48,5120]{1,0:T(8,128)(2,1)S(1)} %copy-done.8, bf16[3,5120,128]{2,1,0:T(8,128)(2,1)S(1)} %bitcast.11, ...), custom_call_target="tpu_custom_call" | custom-call | flops 1006632960 | bytes 7208960 | tf_op jit(solution)/shard_map/project_cache/pallas_call | solution.py:159
  81.3 8.5 %collective-permute-start.7 = (bf16[128,384]{1,0:T(8,128)(2,1)S(1)}, bf16[128,384]{1,0:T(8,128)(2,1)S(1)}, u32[]{:S(2)}, u32[]{:S(2)}) collective-permute-start(bf16[128,384]{1,0:T(8,128)(2,1)S(1)} %get-tuple-element.7.q_ref), channel_id=1, source_target_pairs={{0,1},{1,0},{2,3},{3,2},{4,5},{5,4},{6,7},{7,6},{8,9},{9,8},{10,11... | collective-permute-start | bytes 294920 | tf_op jit(solution)/shard_map/ppermute | solution.py:57
  89.8 4.8 %project_cache.6.k2 = bf16[192,512]{1,0:T(8,128)(2,1)S(1)} custom-call(bf16[48,5120]{1,0:T(8,128)(2,1)S(1)} %copy-done.4, bf16[48,5120]{1,0:T(8,128)(2,1)} %collective-permute-done.17.b, bf16[48,5120]{1,0:T(8,128)(2,1)} %collective-permute-done.18.c, bf16[48,5120]{1,0:T(8,128)(2,1)} %collective-permute-done.19.d, bf16[3,5120,128]{2,1,0:T(8,128)(2,1)S(1)} %bitcast.12, ...), custom_call_target="tpu_custom_call" | custom-call | flops 1006632960 | bytes 7208960 | tf_op jit(solution)/shard_map/project_cache/pallas_call | solution.py:159
  94.7 5.0 %project_cache.7.k3 = bf16[192,512]{1,0:T(8,128)(2,1)S(1)} custom-call(bf16[48,5120]{1,0:T(8,128)(2,1)} %collective-permute-done.20.a, bf16[48,5120]{1,0:T(8,128)(2,1)} %collective-permute-done.21.b, bf16[48,5120]{1,0:T(8,128)(2,1)} %collective-permute-done.22.c, bf16[48,5120]{1,0:T(8,128)(2,1)} %collective-permute-done.23.d, ...), custom_call_target="tpu_custom_call" | custom-call | flops 1006632960 | bytes 7208960 | tf_op jit(solution)/shard_map/project_cache/pallas_call | solution.py:159
  99.7 1.9 %attend.1 = f32[32,8,384]{2,1,0:T(8,128)S(1)} custom-call(s32[1]{0:T(128)} %bitcast.core_ref, s32[32]{0:T(128)S(1)} %dynamic-slice_bitcast_fusion.dest_ref, bf16[128,384]{1,0:T(8,128)(2,1)S(1)} %get-tuple-element.7.q_ref, bf16[128,384]{1,0:T(8,128)(2,1)S(1)} %collective-permute-done.7.qs_ref, bf16[128,512]{1,0:T(8,128)(2,1)S(1)} %get-tuple-element.8.kvf_ref, ...), custom_call_target="tpu_custom_call" | custom-call | flops 234881024 | bytes 2097152 | tf_op jit(solution)/shard_map/attend/pallas_call | solution.py:226
  101.6 13.7 %all_to_all.5.in_ref = f32[32,8,384]{2,1,0:T(8,128)} all-to-all(f32[32,8,384]{2,1,0:T(8,128)S(1)} %attend.1), channel_id=1, replica_groups=mesh['grp'=8,'seq'=32] {'seq'}, dimensions={0} | all-to-all | bytes 786432 | tf_op jit(solution)/shard_map/all_to_all | solution.py:290
  115.2 2.1 %combine.1 = bf16[8,4096]{1,0:T(8,128)(2,1)} custom-call(f32[32,8,384]{2,1,0:T(8,128)} %all_to_all.5.in_ref), custom_call_target="tpu_custom_call" | custom-call | flops 262144 | bytes 458752 | tf_op jit(solution)/shard_map/combine/pallas_call | solution.py:255
  (52 shorter events, 4.5 us)
Async XLA Ops:
  0.0 62.4 %collective-permute-start.6 = (bf16[3,5120,128]{2,1,0:T(8,128)(2,1)}, bf16[3,5120,128]{2,1,0:T(8,128)(2,1)}, u32[]{:S(2)}, u32[]{:S(2)}) collective-permute-start(bf16[3,5120,128]{2,1,0:T(8,128)(2,1)} %bitcast.8), channel_id=1, source_target_pairs={{0,1},{1,0},{2,3},{3,2},{4,5},{5,4},{6,7},{7,6},{8,9},{9,8},{10,11... | collective-permute-start | bytes 11796488 | tf_op jit(solution)/shard_map/ppermute | solution.py:57
  5.7 13.0 %collective-permute-start.8 = (bf16[48,5120]{1,0:T(8,128)(2,1)}, bf16[48,5120]{1,0:T(8,128)(2,1)S(1)}, u32[]{:S(2)}, u32[]{:S(2)}) collective-permute-start(bf16[48,5120]{1,0:T(8,128)(2,1)} %pack_live.1.a), channel_id=1, source_target_pairs={{0,2},{1,9},{2,4},{3,11},{4,6},{5,13},{6,0},{7,15},{8,10},{9,17},{... | collective-permute-start | bytes 1474568 | tf_op jit(solution)/shard_map/ppermute | solution.py:57
  7.3 8.7 %collective-permute-start = (bf16[8,5248]{1,0:T(8,128)(2,1)S(1)}, bf16[8,5248]{1,0:T(8,128)(2,1)S(1)}, u32[]{:S(2)}, u32[]{:S(2)}) collective-permute-start(bf16[8,5248]{1,0:T(8,128)(2,1)S(1)} %pad_maximum_fusion.1), channel_id=1, source_target_pairs={{0,2},{1,9},{2,4},{3,11},{4,6},{5,13},{6,0},{7,15},{8,10},{9,17},{... | collective-permute-start | bytes 251912 | tf_op jit(solution)/shard_map/ppermute | solution.py:57
  8.2 10.5 %collective-permute-start.1 = (bf16[8,5248]{1,0:T(8,128)(2,1)S(1)}, bf16[8,5248]{1,0:T(8,128)(2,1)S(1)}, u32[]{:S(2)}, u32[]{:S(2)}) collective-permute-start(bf16[8,5248]{1,0:T(8,128)(2,1)S(1)} %pad_maximum_fusion.1), channel_id=1, source_target_pairs={{0,6},{1,25},{2,0},{3,27},{4,2},{5,29},{6,4},{7,31},{8,14},{9,1},{... | collective-permute-start | bytes 251912 | tf_op jit(solution)/shard_map/ppermute | solution.py:57
  16.0 5.5 %collective-permute-start.2 = (bf16[8,5248]{1,0:T(8,128)(2,1)S(1)}, bf16[8,5248]{1,0:T(8,128)(2,1)S(1)}, u32[]{:S(2)}, u32[]{:S(2)}) collective-permute-start(bf16[8,5248]{1,0:T(8,128)(2,1)S(1)} %collective-permute-done), channel_id=1, source_target_pairs={{0,2},{1,9},{2,4},{3,11},{4,6},{5,13},{6,0},{7,15},{8,10},{9,17},{... | collective-permute-start | bytes 251912 | tf_op jit(solution)/shard_map/ppermute | solution.py:57
  16.0 9.0 %collective-permute-start.9 = (bf16[48,5120]{1,0:T(8,128)(2,1)}, bf16[48,5120]{1,0:T(8,128)(2,1)S(1)}, u32[]{:S(2)}, u32[]{:S(2)}) collective-permute-start(bf16[48,5120]{1,0:T(8,128)(2,1)} %pack_live.1.a), channel_id=1, source_target_pairs={{0,6},{1,25},{2,0},{3,27},{4,2},{5,29},{6,4},{7,31},{8,14},{9,1},{... | collective-permute-start | bytes 1474568 | tf_op jit(solution)/shard_map/ppermute | solution.py:57
  18.7 12.0 %collective-permute-start.12 = (bf16[48,5120]{1,0:T(8,128)(2,1)}, bf16[48,5120]{1,0:T(8,128)(2,1)S(1)}, u32[]{:S(2)}, u32[]{:S(2)}) collective-permute-start(bf16[48,5120]{1,0:T(8,128)(2,1)} %pack_live.1.a), channel_id=1, source_target_pairs={{0,8},{1,3},{2,10},{3,5},{4,12},{5,7},{6,14},{7,1},{8,16},{9,11},{... | collective-permute-start | bytes 1474568 | tf_op jit(solution)/shard_map/ppermute | solution.py:57
  18.7 12.9 %collective-permute-start.16 = (bf16[48,5120]{1,0:T(8,128)(2,1)}, bf16[48,5120]{1,0:T(8,128)(2,1)S(1)}, u32[]{:S(2)}, u32[]{:S(2)}) collective-permute-start(bf16[48,5120]{1,0:T(8,128)(2,1)} %pack_live.1.a), channel_id=1, source_target_pairs={{0,24},{1,7},{2,26},{3,1},{4,28},{5,3},{6,30},{7,5},{8,0},{9,15},{... | collective-permute-start | bytes 1474568 | tf_op jit(solution)/shard_map/ppermute | solution.py:57
  21.4 9.1 %collective-permute-start.10 = (bf16[24,5120]{1,0:T(8,128)(2,1)S(1)}, bf16[24,5120]{1,0:T(8,128)(2,1)S(1)}, u32[]{:S(2)}, u32[]{:S(2)}) collective-permute-start(bf16[24,5120]{1,0:T(8,128)(2,1)S(1)} %slice.8), channel_id=1, source_target_pairs={{0,2},{1,9},{2,4},{3,11},{4,6},{5,13},{6,0},{7,15},{8,10},{9,17},{... | collective-permute-start | bytes 737288 | tf_op jit(solution)/shard_map/ppermute | solution.py:57
  25.0 9.0 %collective-permute-start.3 = (bf16[32,5248]{1,0:T(8,128)(2,1)S(1)}, bf16[32,5248]{1,0:T(8,128)(2,1)S(1)}, u32[]{:S(2)}, u32[]{:S(2)}) collective-permute-start(bf16[32,5248]{1,0:T(8,128)(2,1)S(1)} %pad_maximum_fusion.a.pa), channel_id=1, source_target_pairs={{0,8},{1,3},{2,10},{3,5},{4,12},{5,7},{6,14},{7,1},{8,16},{9,11},{... | collective-permute-start | bytes 1007624 | tf_op jit(solution)/shard_map/ppermute | solution.py:57
  30.6 5.3 %collective-permute-start.11 = (bf16[24,5120]{1,0:T(8,128)(2,1)S(1)}, bf16[24,5120]{1,0:T(8,128)(2,1)S(1)}, u32[]{:S(2)}, u32[]{:S(2)}) collective-permute-start(bf16[24,5120]{1,0:T(8,128)(2,1)S(1)} %slice.9), channel_id=1, source_target_pairs={{0,6},{1,25},{2,0},{3,27},{4,2},{5,29},{6,4},{7,31},{8,14},{9,1},{... | collective-permute-start | bytes 737288 | tf_op jit(solution)/shard_map/ppermute | solution.py:57
  30.6 7.3 %collective-permute-start.4 = (bf16[32,5248]{1,0:T(8,128)(2,1)S(1)}, bf16[32,5248]{1,0:T(8,128)(2,1)S(1)}, u32[]{:S(2)}, u32[]{:S(2)}) collective-permute-start(bf16[32,5248]{1,0:T(8,128)(2,1)S(1)} %pad_maximum_fusion.a.pa), channel_id=1, source_target_pairs={{0,24},{1,7},{2,26},{3,1},{4,28},{5,3},{6,30},{7,5},{8,0},{9,15},{... | collective-permute-start | bytes 1007624 | tf_op jit(solution)/shard_map/ppermute | solution.py:57
  31.6 28.1 %copy-start.3 = (bf16[48,5120]{1,0:T(8,128)(2,1)}, bf16[48,5120]{1,0:T(8,128)(2,1)S(1)}, u32[]{:S(2)}) copy-start(bf16[48,5120]{1,0:T(8,128)(2,1)S(1)} %collective-permute-done.16.a) | copy-start | bytes 1474564
  31.6 18.4 %collective-permute-start.13 = (bf16[48,5120]{1,0:T(8,128)(2,1)S(1)}, bf16[48,5120]{1,0:T(8,128)(2,1)}, u32[]{:S(2)}, u32[]{:S(2)}) collective-permute-start(bf16[48,5120]{1,0:T(8,128)(2,1)S(1)} %collective-permute-done.8.b), channel_id=1, source_target_pairs={{0,8},{1,3},{2,10},{3,5},{4,12},{5,7},{6,14},{7,1},{8,16},{9,11},{... | collective-permute-start | bytes 1474568 | tf_op jit(solution)/shard_map/ppermute | solution.py:57
  34.0 18.7 %collective-permute-start.14 = (bf16[48,5120]{1,0:T(8,128)(2,1)S(1)}, bf16[48,5120]{1,0:T(8,128)(2,1)S(1)}, u32[]{:S(2)}, u32[]{:S(2)}) collective-permute-start(bf16[48,5120]{1,0:T(8,128)(2,1)S(1)} %collective-permute-done.9.c), channel_id=1, source_target_pairs={{0,8},{1,3},{2,10},{3,5},{4,12},{5,7},{6,14},{7,1},{8,16},{9,11},{... | collective-permute-start | bytes 1474568 | tf_op jit(solution)/shard_map/ppermute | solution.py:57
  35.9 14.1 %collective-permute-start.5 = (bf16[32,5248]{1,0:T(8,128)(2,1)S(1)}, bf16[32,5248]{1,0:T(8,128)(2,1)S(1)}, u32[]{:S(2)}, u32[]{:S(2)}) collective-permute-start(bf16[32,5248]{1,0:T(8,128)(2,1)S(1)} %collective-permute-done.3.b.pb), channel_id=1, source_target_pairs={{0,8},{1,3},{2,10},{3,5},{4,12},{5,7},{6,14},{7,1},{8,16},{9,11},{... | collective-permute-start | bytes 1007624 | tf_op jit(solution)/shard_map/ppermute | solution.py:57
  37.9 15.9 %collective-permute-start.18 = (bf16[48,5120]{1,0:T(8,128)(2,1)S(1)}, bf16[48,5120]{1,0:T(8,128)(2,1)}, u32[]{:S(2)}, u32[]{:S(2)}) collective-permute-start(bf16[48,5120]{1,0:T(8,128)(2,1)S(1)} %collective-permute-done.9.c), channel_id=1, source_target_pairs={{0,24},{1,7},{2,26},{3,1},{4,28},{5,3},{6,30},{7,5},{8,0},{9,15},{... | collective-permute-start | bytes 1474568 | tf_op jit(solution)/shard_map/ppermute | solution.py:57
  50.0 8.9 %collective-permute-start.15 = (bf16[48,5120]{1,0:T(8,128)(2,1)S(1)}, bf16[48,5120]{1,0:T(8,128)(2,1)S(1)}, u32[]{:S(2)}, u32[]{:S(2)}) collective-permute-start(bf16[48,5120]{1,0:T(8,128)(2,1)S(1)} %constant_dynamic-update-slice_fusion.d), channel_id=1, source_target_pairs={{0,8},{1,3},{2,10},{3,5},{4,12},{5,7},{6,14},{7,1},{8,16},{9,11},{... | collective-permute-start | bytes 1474568 | tf_op jit(solution)/shard_map/ppermute | solution.py:57
  50.0 9.7 %collective-permute-start.19 = (bf16[48,5120]{1,0:T(8,128)(2,1)S(1)}, bf16[48,5120]{1,0:T(8,128)(2,1)}, u32[]{:S(2)}, u32[]{:S(2)}) collective-permute-start(bf16[48,5120]{1,0:T(8,128)(2,1)S(1)} %constant_dynamic-update-slice_fusion.d), channel_id=1, source_target_pairs={{0,24},{1,7},{2,26},{3,1},{4,28},{5,3},{6,30},{7,5},{8,0},{9,15},{... | collective-permute-start | bytes 1474568 | tf_op jit(solution)/shard_map/ppermute | solution.py:57
  52.7 0.8 copy-start.5
  53.5 27.8 %collective-permute-start.17 = (bf16[48,5120]{1,0:T(8,128)(2,1)S(1)}, bf16[48,5120]{1,0:T(8,128)(2,1)}, u32[]{:S(2)}, u32[]{:S(2)}) collective-permute-start(bf16[48,5120]{1,0:T(8,128)(2,1)S(1)} %collective-permute-done.8.b), channel_id=1, source_target_pairs={{0,24},{1,7},{2,26},{3,1},{4,28},{5,3},{6,30},{7,5},{8,0},{9,15},{... | collective-permute-start | bytes 1474568 | tf_op jit(solution)/shard_map/ppermute | solution.py:57
  53.8 40.8 %collective-permute-start.20 = (bf16[48,5120]{1,0:T(8,128)(2,1)S(1)}, bf16[48,5120]{1,0:T(8,128)(2,1)}, u32[]{:S(2)}, u32[]{:S(2)}) collective-permute-start(bf16[48,5120]{1,0:T(8,128)(2,1)S(1)} %collective-permute-done.12.a), channel_id=1, source_target_pairs={{0,8},{1,3},{2,10},{3,5},{4,12},{5,7},{6,14},{7,1},{8,16},{9,11},{... | collective-permute-start | bytes 1474568 | tf_op jit(solution)/shard_map/ppermute | solution.py:57
  59.7 35.0 %collective-permute-start.21 = (bf16[48,5120]{1,0:T(8,128)(2,1)}, bf16[48,5120]{1,0:T(8,128)(2,1)}, u32[]{:S(2)}, u32[]{:S(2)}) collective-permute-start(bf16[48,5120]{1,0:T(8,128)(2,1)} %collective-permute-done.13.b), channel_id=1, source_target_pairs={{0,8},{1,3},{2,10},{3,5},{4,12},{5,7},{6,14},{7,1},{8,16},{9,11},{... | collective-permute-start | bytes 1474568 | tf_op jit(solution)/shard_map/ppermute | solution.py:57
  59.7 35.0 %collective-permute-start.22 = (bf16[48,5120]{1,0:T(8,128)(2,1)}, bf16[48,5120]{1,0:T(8,128)(2,1)}, u32[]{:S(2)}, u32[]{:S(2)}) collective-permute-start(bf16[48,5120]{1,0:T(8,128)(2,1)} %collective-permute-done.18.c), channel_id=1, source_target_pairs={{0,24},{1,7},{2,26},{3,1},{4,28},{5,3},{6,30},{7,5},{8,0},{9,15},{... | collective-permute-start | bytes 1474568 | tf_op jit(solution)/shard_map/ppermute | solution.py:57
  62.4 32.3 %collective-permute-start.23 = (bf16[48,5120]{1,0:T(8,128)(2,1)}, bf16[48,5120]{1,0:T(8,128)(2,1)}, u32[]{:S(2)}, u32[]{:S(2)}) collective-permute-start(bf16[48,5120]{1,0:T(8,128)(2,1)} %collective-permute-done.19.d), channel_id=1, source_target_pairs={{0,24},{1,7},{2,26},{3,1},{4,28},{5,3},{6,30},{7,5},{8,0},{9,15},{... | collective-permute-start | bytes 1474568 | tf_op jit(solution)/shard_map/ppermute | solution.py:57
  63.1 2.1 %copy-start = (bf16[5120,1,3,128]{3,0,2,1:T(8,128)(2,1)S(1)}, bf16[5120,1,3,128]{3,0,2,1:T(8,128)(2,1)}, u32[]{:S(2)}) copy-start(bf16[5120,1,3,128]{3,0,2,1:T(8,128)(2,1)} %param.9) | copy-start | bytes 11796484
  65.3 1.0 copy-start.2
  66.3 4.8 %copy-start.1 = (bf16[5120,1,3,128]{3,0,2,1:T(8,128)(2,1)S(1)}, bf16[5120,1,3,128]{3,0,2,1:T(8,128)(2,1)}, u32[]{:S(2)}) copy-start(bf16[5120,1,3,128]{3,0,2,1:T(8,128)(2,1)} %param.9) | copy-start | bytes 11796484
  71.0 5.5 %copy-start.6 = (bf16[48,5120]{1,0:T(8,128)(2,1)S(1)}, bf16[48,5120]{1,0:T(8,128)(2,1)}, u32[]{:S(2)}) copy-start(bf16[48,5120]{1,0:T(8,128)(2,1)} %copy-done.5) | copy-start | bytes 1474564
  71.1 5.5 %copy-start.8 = (bf16[48,5120]{1,0:T(8,128)(2,1)S(1)}, bf16[48,5120]{1,0:T(8,128)(2,1)}, u32[]{:S(2)}) copy-start(bf16[48,5120]{1,0:T(8,128)(2,1)} %copy-done.7) | copy-start | bytes 1474564
  76.6 13.2 %copy-start.4 = (bf16[48,5120]{1,0:T(8,128)(2,1)S(1)}, bf16[48,5120]{1,0:T(8,128)(2,1)}, u32[]{:S(2)}) copy-start(bf16[48,5120]{1,0:T(8,128)(2,1)} %copy-done.3) | copy-start | bytes 1474564
  81.3 18.4 %collective-permute-start.7 = (bf16[128,384]{1,0:T(8,128)(2,1)S(1)}, bf16[128,384]{1,0:T(8,128)(2,1)S(1)}, u32[]{:S(2)}, u32[]{:S(2)}) collective-permute-start(bf16[128,384]{1,0:T(8,128)(2,1)S(1)} %get-tuple-element.7.q_ref), channel_id=1, source_target_pairs={{0,1},{1,0},{2,3},{3,2},{4,5},{5,4},{6,7},{7,6},{8,9},{9,8},{10,11... | collective-permute-start | bytes 294920 | tf_op jit(solution)/shard_map/ppermute | solution.py:57
  (1 other events, 0.8 us)

commit v2 on v0

v2 whole, which is shorter than its diff:
```python
import functools

import jax
import jax.numpy as jnp
from jax import lax
from jax.experimental import pallas as pl
from jax.experimental.pallas import tpu as pltpu
from jax.sharding import PartitionSpec as P

MASKED_SCORE = -1e30
NY, NX = 4, 4
LIVE = 48
HD = 128
TURN = 8
HALF = LIVE // 2
QUAD = TURN // 2
BF16 = jnp.bfloat16
F32 = jnp.float32


def index_of(y, x, c):
    return (y % NY * NX + x % NX) * 2 + c


def ring_pairs(step, first):
    pairs = []
    for y in range(NY):
        for x in range(NX):
            for c in range(2):
                along_x = (c == 0) == first
                dy, dx = (0, step) if along_x else (step, 0)
                pairs.append((index_of(y, x, c), index_of(y + dy, x + dx, c)))
    return pairs


A_UP, A_DOWN = ring_pairs(1, True), ring_pairs(-1, True)
B_UP, B_DOWN = ring_pairs(1, False), ring_pairs(-1, False)
SWAP = [(i, i ^ 1) for i in range(2 * NY * NX)]
OFFSETS = (0, -1, 1, -2)


def token_owner(me, group):
    core = lax.rem(me, 2)
    y, x = lax.div(me, 2 * NX), lax.rem(lax.div(me, 2), NX)
    along_x = core == 0
    if group >= NX * NY:
        core, along_x = 1 - core, core == 1
    b, a = OFFSETS[group % (NX * NY) // 4], OFFSETS[group % 4]
    dy, dx = jnp.where(along_x, b, a), jnp.where(along_x, a, b)
    return (lax.rem(y + dy + NY, NY) * NX + lax.rem(x + dx + NX, NX)) * 2 + core


def send(value, pairs):
    return lax.ppermute(value, "seq", pairs)


VMEM = pl.BlockSpec(memory_space=pltpu.VMEM)


def limit(mib):
    return pltpu.CompilerParams(vmem_limit_bytes=mib * 2**20)


def pack_kernel(*refs):
    sources, (one_ref, two_ref), scratch, sems = refs[:5], refs[5:7], refs[7:12], refs[12]
    copies = [pltpu.make_async_copy(a, b, sems.at[i]) for i, (a, b) in enumerate(zip(sources, scratch))]
    for copy in copies:
        copy.start()
    for copy in copies:
        copy.wait()
    place_ref, len_ref, turn_place_ref, rows_ref, turn_ref = scratch
    n, d = rows_ref.shape
    i0 = lax.broadcasted_iota(jnp.int32, (n, n), 0)
    i1 = lax.broadcasted_iota(jnp.int32, (n, n), 1)
    place_col = jnp.sum(jnp.where(i0 == i1, place_ref[...], 0), axis=1, keepdims=True)
    owner = place_col // n
    inner = place_col - owner * n
    o1 = lax.broadcasted_iota(jnp.int32, (n, len_ref.shape[1]), 1)
    length = jnp.sum(jnp.where(o1 == owner, len_ref[...], 0), axis=1, keepdims=True)
    live_col = (inner < length).astype(jnp.int32)
    live_row = jnp.sum(jnp.where(i0 == i1, live_col, 0), axis=0, keepdims=True)
    rank_row = jnp.sum(jnp.where(i0 < i1, live_col, 0), axis=0, keepdims=True)
    rank_row = jnp.where(live_row > 0, rank_row, -1)
    k0 = lax.broadcasted_iota(jnp.int32, (LIVE, n), 0)
    pick = jnp.where(k0 == rank_row, 1.0, 0.0).astype(BF16)
    live = jnp.dot(pick, rows_ref[...], preferred_element_type=F32)
    turn = turn_ref[...].astype(F32)
    m = HALF + QUAD
    t0 = lax.broadcasted_iota(jnp.int32, (m, TURN), 0)
    t1 = lax.broadcasted_iota(jnp.int32, (m, TURN), 1)
    for i, ref in enumerate((one_ref, two_ref)):
        rows, quad = live[i * HALF : (i + 1) * HALF], turn[i * QUAD : (i + 1) * QUAD]
        ref[:, :d] = jnp.concatenate([rows, quad], axis=0).astype(BF16)
        mine = t0 - HALF + i * QUAD == t1
        turn_col = jnp.sum(jnp.where(mine, turn_place_ref[...], 0), axis=1, keepdims=True)
        ref[:, d:] = jnp.broadcast_to(turn_col.astype(F32), (m, HD)).astype(BF16)


def pack(row_place, cache_len, group_place, cache_hidden, group_hidden):
    n, d = cache_hidden.shape
    m = HALF + QUAD
    args = (row_place.reshape(1, n), cache_len.reshape(1, -1), group_place.reshape(1, -1), cache_hidden, group_hidden)
    return pl.pallas_call(
        pack_kernel,
        in_specs=[pl.BlockSpec(memory_space=pl.ANY)] * 5,
        out_specs=[VMEM] * 2,
        out_shape=[jax.ShapeDtypeStruct((m, d + HD), BF16)] * 2,
        scratch_shapes=[pltpu.VMEM(v.shape, v.dtype) for v in args] + [pltpu.SemaphoreType.DMA((5,))],
        compiler_params=limit(56),
        cost_estimate=pl.CostEstimate(flops=2 * n * LIVE * d, bytes_accessed=4 * n * d, transcendentals=0),
        name="pack_live",
    )(*args)


def join_kernel(a, b, c, e, out_ref):
    x = [r[...].astype(F32) for r in (a, b, c, e)]
    out_ref[: 4 * HALF] = jnp.concatenate([v[:HALF] for v in x], axis=0).astype(BF16)
    out_ref[4 * HALF :] = jnp.concatenate([v[HALF:] for v in x], axis=0).astype(BF16)


def join(parts):
    m, w = parts[0].shape
    return pl.pallas_call(
        join_kernel,
        in_specs=[VMEM] * 4,
        out_specs=VMEM,
        out_shape=jax.ShapeDtypeStruct((4 * m, w), BF16),
        compiler_params=limit(8),
        cost_estimate=pl.CostEstimate(flops=0, bytes_accessed=16 * m * w, transcendentals=0),
        name="join_shards",
    )(*parts)


def project_rows(refs, own_ref, other_ref):
    d = own_ref.shape[1]
    x = jnp.concatenate([r[: 4 * HALF, :d] for r in refs], axis=0)
    w = jnp.concatenate([own_ref[1], own_ref[2], other_ref[1], other_ref[2]], axis=1)
    return jnp.dot(x, w, preferred_element_type=F32).astype(BF16)


def turn_kernel(*refs):
    *blocks, own_ref, other_ref, q_ref, kv_ref = refs
    d = own_ref.shape[1]
    turns = jnp.concatenate([r[4 * HALF :] for r in blocks], axis=0)
    x, places = turns[:, :d], turns[:, d:]
    w = jnp.concatenate([r[i] for r in (own_ref, other_ref) for i in range(3)], axis=1)
    qkv = jnp.dot(x, w, preferred_element_type=F32).astype(BF16)
    n = x.shape[0]
    to = lax.broadcasted_iota(jnp.int32, (n, n), 0)
    source = to - to % 32 + to % 8 // QUAD * 16 + to % 32 // 8 * QUAD + to % QUAD
    order = jnp.where(source == lax.broadcasted_iota(jnp.int32, (n, n), 1), 1.0, 0.0).astype(BF16)
    both = jnp.concatenate([qkv, places], axis=1)
    both = jnp.dot(order, both, preferred_element_type=F32).astype(BF16)
    q_ref[:, :HD] = both[:, :HD]
    q_ref[:, HD : 2 * HD] = both[:, 3 * HD : 4 * HD]
    q_ref[:, 2 * HD :] = both[:, 6 * HD :]
    kv_ref[:, : 2 * HD] = both[:, HD : 3 * HD]
    kv_ref[:, 2 * HD :] = both[:, 4 * HD : 6 * HD]


def turn_project(blocks, own, other):
    m, d = 4 * QUAD * len(blocks), own.shape[1]
    return pl.pallas_call(
        turn_kernel,
        in_specs=[VMEM] * (len(blocks) + 2),
        out_specs=[VMEM] * 2,
        out_shape=[
            jax.ShapeDtypeStruct((m, 3 * HD), BF16),
            jax.ShapeDtypeStruct((m, 4 * HD), BF16),
        ],
        compiler_params=limit(16),
        cost_estimate=pl.CostEstimate(flops=2 * m * d * 6 * HD * 3, bytes_accessed=2**20, transcendentals=0),
        name="project_turn",
    )(*blocks, own, other)


def cache_kernel(*refs):
    *rows, own_ref, other_ref, kv_ref = refs
    kv_ref[...] = project_rows(rows, own_ref, other_ref)


def cache_project(rows, own, other):
    m, d = 4 * HALF * len(rows), own.shape[1]
    return pl.pallas_call(
        cache_kernel,
        in_specs=[VMEM] * (len(rows) + 2),
        out_specs=VMEM,
        out_shape=jax.ShapeDtypeStruct((m, 4 * HD), BF16),
        compiler_params=limit(16),
        cost_estimate=pl.CostEstimate(flops=2 * m * d * 4 * HD * 3, bytes_accessed=2**20, transcendentals=0),
        name="project_cache",
    )(*rows, own, other)


def terms(x):
    hi = x.astype(BF16).astype(F32)
    mid = (x - hi).astype(BF16).astype(F32)
    return [hi, mid, x - hi - mid]


def attend_kernel(qa_ref, qb_ref, qsa_ref, qsb_ref, kva_ref, kvb_ref, k0, k1, k2, out_ref):
    me = lax.axis_index("seq")
    first = lax.rem(me, 2) == 0
    mine = jnp.concatenate([qa_ref[...], qb_ref[...]], axis=0)
    theirs = jnp.concatenate([qsa_ref[...], qsb_ref[...]], axis=0)
    fresh = jnp.concatenate([kva_ref[...], kvb_ref[...]], axis=0)
    q_place = jnp.concatenate([mine[:, 2 * HD :], theirs[:, 2 * HD :]], axis=0).astype(F32)
    k_place = mine[:, 2 * HD :].astype(F32).T[0:1, :]
    seen = k_place <= q_place[:, 0:1]
    scale = HD ** (-0.5)
    nt = (((1,), (1,)), ((), ()))
    outs, stats = [], []
    lane = lax.broadcasted_iota(jnp.int32, (q_place.shape[0], HD), 1) % 64
    for h in range(2):
        q = jnp.concatenate(
            [mine[:, h * HD : (h + 1) * HD], theirs[:, (1 - h) * HD : (2 - h) * HD]], axis=0
        )
        ks = slice(2 * h * HD, (2 * h + 1) * HD)
        vs = slice((2 * h + 1) * HD, (2 * h + 2) * HD)
        s = [
            lax.dot_general(q, r[:, ks], nt, preferred_element_type=F32) * scale
            for r in (k0, k1, k2)
        ]
        f = lax.dot_general(q, fresh[:, ks], nt, preferred_element_type=F32) * scale
        s.append(jnp.where(seen, f, MASKED_SCORE))
        top = functools.reduce(jnp.maximum, [jnp.max(t, axis=1, keepdims=True) for t in s])
        total = jnp.zeros_like(top)
        summed = jnp.zeros((q.shape[0], HD), F32)
        for t, r in zip(s, (k0, k1, k2, fresh)):
            e = jnp.exp(t - top)
            total += jnp.sum(e, axis=1, keepdims=True)
            summed += jnp.dot(e.astype(BF16), r[:, vs], preferred_element_type=F32)
        outs.append(summed)
        stat = jnp.zeros((q.shape[0], HD), F32)
        for i, v in enumerate(terms(top) + terms(total)):
            stat = jnp.where(lane // 8 == i, v, stat)
        stats.append(stat)
    low = jnp.where(first, outs[0], outs[1])
    high = jnp.where(first, outs[1], outs[0])
    left = lax.broadcasted_iota(jnp.int32, low.shape, 1) < 64
    stat = jnp.where(left == first, stats[0], stats[1])
    whole = jnp.concatenate([low, high, stat], axis=1)
    for g in range(out_ref.shape[0]):
        out_ref[token_owner(me, g)] = whole[g * TURN : (g + 1) * TURN].astype(BF16)


def attend(*arrays):
    n = 2 * NY * NX
    keys = sum(v.shape[0] for v in arrays[4:])
    return pl.pallas_call(
        attend_kernel,
        in_specs=[VMEM] * len(arrays),
        out_specs=VMEM,
        out_shape=jax.ShapeDtypeStruct((n, TURN, 3 * HD), BF16),
        compiler_params=limit(12),
        cost_estimate=pl.CostEstimate(
            flops=2 * 2 * 2 * 256 * keys * HD, bytes_accessed=2 * 2**20, transcendentals=2 * 256 * keys
        ),
        name="attend",
    )(*arrays)


def combine_kernel(in_ref, out_ref):
    for j in range(in_ref.shape[0] // 2):
        x = [in_ref[2 * j + i].astype(F32) for i in range(2)]
        for h in range(2):
            at = 2 * HD + 64 * h

            def total(v, i):
                s = at + 24 * i
                return v[:, s : s + 1] + v[:, s + 8 : s + 9] + v[:, s + 16 : s + 17]

            o0, o1 = [v[:, h * HD : (h + 1) * HD] for v in x]
            m0, m1 = [total(v, 0) for v in x]
            l0, l1 = [total(v, 1) for v in x]
            top = jnp.maximum(m0, m1)
            e0, e1 = jnp.exp(m0 - top), jnp.exp(m1 - top)
            out = (o0 * e0 + o1 * e1) / (l0 * e0 + l1 * e1)
            out_ref[:, (2 * j + h) * HD : (2 * j + h + 1) * HD] = out.astype(BF16)


def combine(parts):
    n, t, _ = parts.shape
    return pl.pallas_call(
        combine_kernel,
        out_shape=jax.ShapeDtypeStruct((t, n * HD), BF16),
        compiler_params=limit(4),
        cost_estimate=pl.CostEstimate(flops=n * t * HD * 8, bytes_accessed=n * t * HD * 14, transcendentals=n * t),
        name="combine",
    )(parts)


def shards(cache_hidden, group_hidden, proj_weight, row_place, cache_len, group_place):
    own = jnp.transpose(proj_weight[:, 0], (1, 0, 2))

    one, two = pack(row_place, cache_len, group_place, cache_hidden, group_hidden)
    own, one, two = lax.optimization_barrier((own, one, two))
    other = send(own, SWAP)
    one_up, one_down = send(one, A_UP), send(one, A_DOWN)
    two_up, two_down = send(two, A_UP), send(two, A_DOWN)
    first = join([one, one_up, one_down, send(one_up, A_UP)])
    second = join([two, two_up, two_down, send(two_down, A_DOWN)])
    first_up, second_down = send(first, B_UP), send(second, B_DOWN)
    second_up, first_down = send(second, B_UP), send(first, B_DOWN)
    kv_near = cache_project((first, second), own, other)
    first_up, second_down, kv_near = lax.optimization_barrier((first_up, second_down, kv_near))
    far = send(first_up, B_UP), send(second_down, B_DOWN)

    mid = (first_up, second_up, first_down, second_down)
    kv_mid = cache_project(mid, own, other)
    q_most, kv_most = turn_project((first, second, *mid), own, other)
    *far, kv_mid, q_most = lax.optimization_barrier((*far, kv_mid, q_most))
    q_last, kv_last = turn_project(far, own, other)
    kv_far = cache_project(far, own, other)
    queries = q_most, q_last, send(q_most, SWAP), send(q_last, SWAP)
    parts = attend(*queries, kv_most, kv_last, kv_near, kv_mid, kv_far)
    landed = lax.all_to_all(parts, "seq", split_axis=0, concat_axis=0, tiled=True)
    return combine(landed)


def solution(mesh):
    in_specs = (
        P(("grp", "seq"), None),
        P(("grp", "seq"), None),
        P(None, "seq", None, None),
        P(("grp", "seq")),
        P("grp"),
        P(("grp", "seq")),
    )
    out_specs = P(("grp", "seq"), None)
    return jax.shard_map(shards, mesh=mesh, in_specs=in_specs, out_specs=out_specs, check_vma=False)
```

time: 197 us -> 88.9 us (0.45)
  waiting for transfers between devices: 94.3 us -> 38.1 us
  other arithmetic: 22.3 us -> 0 us
  starting transfers between devices: 0.04 us -> 21.2 us
  local copies, waits for them, and re-layouts: 20.5 us -> 0.98 us
  matrix products: 16.2 us -> 0 us
  between operations: 14.9 us -> 0.1 us
  Pallas kernels: 0 us -> 13.1 us
  blocking collectives: 27.9 us -> 15.2 us
    all_gather x2 -> x0, waiting for transfers between devices: 92.9 us -> none  [the longest x1 84.6 us: shards(): lax.all_gather(cache_hidden, 'seq', axis=0, tiled=True)]
    ppermute x0 -> x15, waiting for transfers between devices: none -> 38.1 us  [send(): return lax.ppermute(value, 'seq', pairs)]
    ppermute x0 -> x15, starting transfers between devices: none -> 21.2 us  [send(): return lax.ppermute(value, 'seq', pairs)]
    dot_general x4 -> x0, matrix products: 16.2 us -> none  [the longest x1 10.6 us: shards(): jnp.dot(lax.all_gather(cache_hidden, 'seq', axis=0, tiled=True), kv_weigh...]
    lt x1 -> x0, other arithmetic: 15.5 us -> none  [shards(): live_keys = positions % cache_rows < cache_len[positions // cache_rows]]
    unnamed x1 -> x0, blocking collectives: 15.4 us -> none
    pallas_call x0 -> x10, Pallas kernels: none -> 13.1 us  [the longest x3 4.63 us: cache_project(): pl.pallas_call(cache_kernel, in_specs=[VMEM] * (len(rows) + 2), out_specs...]
    scatter x1 -> x0, local copies, waits for them, and re-layouts: 9.57 us -> none  [shards(): jnp.zeros((session, 2 * head_dim), jnp.bfloat16).at[all_places]]
  transfers between devices with their start and end apart: 2 -> 15, of which waited for: 2 -> 7; matrix products, arithmetic and copies ran while one was open for 18% -> 0% of each run, Pallas kernels for 0% -> 7%
where the time goes in v2:
time: 88.9 us; the launch traced here: 88.7 us
  waiting for transfers between devices  38.1 us (43%)
  starting transfers between devices  21.2 us (24%)
  blocking collectives  15.2 us (17%)
  Pallas kernels  13.1 us (15%)
  local copies, waits for them, and re-layouts  0.98 us (1%)
    ppermute x15, waiting for transfers between devices, send(): return lax.ppermute(value, 'seq', pairs)  38.1 us
    ppermute x15, starting transfers between devices, send(): return lax.ppermute(value, 'seq', pairs)  21.2 us
    all_to_all x1, blocking collectives, shards(): lax.all_to_all(parts, 'seq', split_axis=0, concat_axis=0, tiled=True)  15.2 us
    pallas_call x3, Pallas kernels, cache_project(): pl.pallas_call(cache_kernel, in_specs=[VMEM] * (len(rows) + 2), out_specs...  4.63 us
    pallas_call x2, Pallas kernels, turn_project(): pl.pallas_call(turn_kernel, in_specs=[VMEM] * (len(blocks) + 2), out_spec...  3.22 us
    pallas_call x1, Pallas kernels, pack(): pl.pallas_call(pack_kernel, in_specs=[pl.BlockSpec(memory_space=pl.ANY)]...  2.53 us
  transfers between devices with their start and end apart: 15, of which 7 were waited for; matrix products, arithmetic and copies ran while one was open for 0% of the time, Pallas kernels for 7%

profile of v2, /device:TPU:1, one launch (start us, length us, event | category | flops | bytes accessed | tf_op | source)
XLA Modules:
  0.0 88.7 jit_solution(8905785642235392321)
XLA Ops:
  0.0 2.5 %pack_live.1 = (bf16[28,5248]{1,0:T(8,128)(2,1)}, bf16[28,5248]{1,0:T(8,128)(2,1)}) custom-call(s32[1,64]{1,0:T(1,128)} %bitcast.12, s32[1,32]{1,0:T(1,128)} %bitcast.13, s32[1,8]{1,0:T(1,128)} %bitcast.14, bf16[64,5120]{1,0:T(8,128)(2,1)} %refs_3_.1, bf16[8,5120]{1,0:T(8,128)(2,1)} %refs_4_.1), custom_call_target="tpu_custom_call" | custom-call | flops 31457280 | bytes 1310720 | tf_op jit(solution)/shard_map/pack_live/pallas_call | solution.py:103
  2.5 3.3 %collective-permute-start.8 = (bf16[3,5120,128]{2,1,0:T(8,128)(2,1)}, bf16[3,5120,128]{2,1,0:T(8,128)(2,1)S(1)}, u32[]{:S(2)}, u32[]{:S(2)}) collective-permute-start(bf16[3,5120,128]{2,1,0:T(8,128)(2,1)} %bitcast.6), channel_id=1, source_target_pairs={{0,1},{1,0},{2,3},{3,2},{4,5},{5,4},{6,7},{7,6},{8,9},{9,8},{10,11... | collective-permute-start | bytes 11796488 | tf_op jit(solution)/shard_map/ppermute | solution.py:54
  5.9 1.0 %collective-permute-start.5 = (bf16[28,5248]{1,0:T(8,128)(2,1)}, bf16[28,5248]{1,0:T(8,128)(2,1)S(1)}, u32[]{:S(2)}, u32[]{:S(2)}) collective-permute-start(bf16[28,5248]{1,0:T(8,128)(2,1)} %get-tuple-element.24.a), channel_id=1, source_target_pairs={{0,6},{1,25},{2,0},{3,27},{4,2},{5,29},{6,4},{7,31},{8,14},{9,1},{... | collective-permute-start | bytes 881672 | tf_op jit(solution)/shard_map/ppermute | solution.py:54
  6.9 0.5 collective-permute-start
  7.4 5.0 %collective-permute-done.5.c = bf16[28,5248]{1,0:T(8,128)(2,1)S(1)} collective-permute-done((bf16[28,5248]{1,0:T(8,128)(2,1)}, bf16[28,5248]{1,0:T(8,128)(2,1)S(1)}, u32[]{:S(2)}, u32[]{:S(2)}) %collective-permute-start.5) | collective-permute-done | bytes 293920 | tf_op jit(solution)/shard_map/ppermute | solution.py:54
  12.4 2.2 %collective-permute-start.6 = (bf16[28,5248]{1,0:T(8,128)(2,1)S(1)}, bf16[28,5248]{1,0:T(8,128)(2,1)S(1)}, u32[]{:S(2)}, u32[]{:S(2)}) collective-permute-start(bf16[28,5248]{1,0:T(8,128)(2,1)S(1)} %collective-permute-done.5.c), channel_id=1, source_target_pairs={{0,6},{1,25},{2,0},{3,27},{4,2},{5,29},{6,4},{7,31},{8,14},{9,1},{... | collective-permute-start | bytes 881672 | tf_op jit(solution)/shard_map/ppermute | solution.py:54
  14.6 1.4 %collective-permute-start.2 = (bf16[28,5248]{1,0:T(8,128)(2,1)S(1)}, bf16[28,5248]{1,0:T(8,128)(2,1)S(1)}, u32[]{:S(2)}, u32[]{:S(2)}) collective-permute-start(bf16[28,5248]{1,0:T(8,128)(2,1)S(1)} %collective-permute-done.b), channel_id=1, source_target_pairs={{0,2},{1,9},{2,4},{3,11},{4,6},{5,13},{6,0},{7,15},{8,10},{9,17},{... | collective-permute-start | bytes 881672 | tf_op jit(solution)/shard_map/ppermute | solution.py:54
  16.1 2.1 %collective-permute-done.4.b = bf16[28,5248]{1,0:T(8,128)(2,1)S(1)} collective-permute-done((bf16[28,5248]{1,0:T(8,128)(2,1)}, bf16[28,5248]{1,0:T(8,128)(2,1)S(1)}, u32[]{:S(2)}, u32[]{:S(2)}) %collective-permute-start.4) | collective-permute-done | bytes 293920 | tf_op jit(solution)/shard_map/ppermute | solution.py:54
  18.2 0.5 collective-permute-done.6.e
  18.7 1.0 %copy-done.2 = bf16[28,5248]{1,0:T(8,128)(2,1)S(1)} copy-done((bf16[28,5248]{1,0:T(8,128)(2,1)S(1)}, bf16[28,5248]{1,0:T(8,128)(2,1)}, u32[]{:S(2)}) %copy-start.2) | copy-done | bytes 293912
  19.7 0.1 join_shards.3.refs_1_
  19.8 2.6 %collective-permute-start.7 = (bf16[112,5248]{1,0:T(8,128)(2,1)S(1)}, bf16[112,5248]{1,0:T(8,128)(2,1)S(1)}, u32[]{:S(2)}, u32[]{:S(2)}) collective-permute-start(bf16[112,5248]{1,0:T(8,128)(2,1)S(1)} %join_shards.3.refs_1_), channel_id=1, source_target_pairs={{0,24},{1,7},{2,26},{3,1},{4,28},{5,3},{6,30},{7,5},{8,0},{9,15},{... | collective-permute-start | bytes 3526664 | tf_op jit(solution)/shard_map/ppermute | solution.py:54
  22.4 0.0 collective-permute-done.1.c
  22.4 0.1 join_shards.2.refs_0_
  22.5 1.0 %collective-permute-start.3 = (bf16[112,5248]{1,0:T(8,128)(2,1)S(1)}, bf16[112,5248]{1,0:T(8,128)(2,1)S(1)}, u32[]{:S(2)}, u32[]{:S(2)}) collective-permute-start(bf16[112,5248]{1,0:T(8,128)(2,1)S(1)} %join_shards.2.refs_0_), channel_id=1, source_target_pairs={{0,8},{1,3},{2,10},{3,5},{4,12},{5,7},{6,14},{7,1},{8,16},{9,11},{... | collective-permute-start | bytes 3526664 | tf_op jit(solution)/shard_map/ppermute | solution.py:54
  23.5 1.2 %collective-permute-start.11 = (bf16[112,5248]{1,0:T(8,128)(2,1)S(1)}, bf16[112,5248]{1,0:T(8,128)(2,1)S(1)}, u32[]{:S(2)}, u32[]{:S(2)}) collective-permute-start(bf16[112,5248]{1,0:T(8,128)(2,1)S(1)} %join_shards.3.refs_1_), channel_id=1, source_target_pairs={{0,8},{1,3},{2,10},{3,5},{4,12},{5,7},{6,14},{7,1},{8,16},{9,11},{... | collective-permute-start | bytes 3526664 | tf_op jit(solution)/shard_map/ppermute | solution.py:54
  24.7 1.5 %collective-permute-start.12 = (bf16[112,5248]{1,0:T(8,128)(2,1)S(1)}, bf16[112,5248]{1,0:T(8,128)(2,1)S(1)}, u32[]{:S(2)}, u32[]{:S(2)}) collective-permute-start(bf16[112,5248]{1,0:T(8,128)(2,1)S(1)} %join_shards.2.refs_0_), channel_id=1, source_target_pairs={{0,24},{1,7},{2,26},{3,1},{4,28},{5,3},{6,30},{7,5},{8,0},{9,15},{... | collective-permute-start | bytes 3526664 | tf_op jit(solution)/shard_map/ppermute | solution.py:54
  26.2 1.2 %project_cache.3.k0 = bf16[192,512]{1,0:T(8,128)(2,1)S(1)} custom-call(bf16[112,5248]{1,0:T(8,128)(2,1)S(1)} %join_shards.2.refs_0_, bf16[112,5248]{1,0:T(8,128)(2,1)S(1)} %join_shards.3.refs_1_, bf16[3,5120,128]{2,1,0:T(8,128)(2,1)S(1)} %bitcast.7, bf16[3,5120,128]{2,1,0:T(8,128)(2,1)S(1)} %collective-permute-done.8.refs_3_.refs_5_.refs_7_), custom_call_target="tpu_custom_call" | custom-call | flops 3019898880 | bytes 1048576 | tf_op jit(solution)/shard_map/project_cache/pallas_call | solution.py:184
  27.4 8.9 %collective-permute-done.7.refs_3_.refs_5_ = bf16[112,5248]{1,0:T(8,128)(2,1)S(1)} collective-permute-done((bf16[112,5248]{1,0:T(8,128)(2,1)S(1)}, bf16[112,5248]{1,0:T(8,128)(2,1)S(1)}, u32[]{:S(2)}, u32[]{:S(2)}) %collective-permute-start.7) | collective-permute-done | bytes 1175584 | tf_op jit(solution)/shard_map/ppermute | solution.py:54
  36.3 2.8 %collective-permute-done.3.refs_0_.refs_2_ = bf16[112,5248]{1,0:T(8,128)(2,1)S(1)} collective-permute-done((bf16[112,5248]{1,0:T(8,128)(2,1)S(1)}, bf16[112,5248]{1,0:T(8,128)(2,1)S(1)}, u32[]{:S(2)}, u32[]{:S(2)}) %collective-permute-start.3) | collective-permute-done | bytes 1175584 | tf_op jit(solution)/shard_map/ppermute | solution.py:54
  39.1 2.7 %collective-permute-start.10 = (bf16[112,5248]{1,0:T(8,128)(2,1)S(1)}, bf16[112,5248]{1,0:T(8,128)(2,1)S(1)}, u32[]{:S(2)}, u32[]{:S(2)}) collective-permute-start(bf16[112,5248]{1,0:T(8,128)(2,1)S(1)} %collective-permute-done.7.refs_3_.refs_5_), channel_id=1, source_target_pairs={{0,24},{1,7},{2,26},{3,1},{4,28},{5,3},{6,30},{7,5},{8,0},{9,15},{... | collective-permute-start | bytes 3526664 | tf_op jit(solution)/shard_map/ppermute | solution.py:54
  41.8 9.9 %collective-permute-done.11.refs_1_.refs_3_ = bf16[112,5248]{1,0:T(8,128)(2,1)S(1)} collective-permute-done((bf16[112,5248]{1,0:T(8,128)(2,1)S(1)}, bf16[112,5248]{1,0:T(8,128)(2,1)S(1)}, u32[]{:S(2)}, u32[]{:S(2)}) %collective-permute-start.11) | collective-permute-done | bytes 1175584 | tf_op jit(solution)/shard_map/ppermute | solution.py:54
  51.7 1.6 %project_turn.2 = (bf16[96,384]{1,0:T(8,128)(2,1)S(1)}, bf16[96,512]{1,0:T(8,128)(2,1)S(1)}) custom-call(bf16[112,5248]{1,0:T(8,128)(2,1)S(1)} %join_shards.2.refs_0_, bf16[112,5248]{1,0:T(8,128)(2,1)S(1)} %join_shards.3.refs_1_, bf16[112,5248]{1,0:T(8,128)(2,1)S(1)} %collective-permute-done.3.refs_0_.refs_2_, ...), custom_call_target="tpu_custom_call" | custom-call | flops 2264924160 | bytes 1048576 | tf_op jit(solution)/shard_map/project_turn/pallas_call | solution.py:163
  53.4 2.2 %project_cache.4.k1 = bf16[384,512]{1,0:T(8,128)(2,1)S(1)} custom-call(bf16[112,5248]{1,0:T(8,128)(2,1)S(1)} %collective-permute-done.3.refs_0_.refs_2_, bf16[112,5248]{1,0:T(8,128)(2,1)S(1)} %collective-permute-done.11.refs_1_.refs_3_, bf16[112,5248]{1,0:T(8,128)(2,1)S(1)} %collective-permute-done.12.refs_2_.refs_4_, ...), custom_call_target="tpu_custom_call" | custom-call | flops 6039797760 | bytes 1048576 | tf_op jit(solution)/shard_map/project_cache/pallas_call | solution.py:184
  55.6 8.7 %collective-permute-done.9.refs_0_ = bf16[112,5248]{1,0:T(8,128)(2,1)S(1)} collective-permute-done((bf16[112,5248]{1,0:T(8,128)(2,1)S(1)}, bf16[112,5248]{1,0:T(8,128)(2,1)S(1)}, u32[]{:S(2)}, u32[]{:S(2)}) %collective-permute-start.9) | collective-permute-done | bytes 1175584 | tf_op jit(solution)/shard_map/ppermute | solution.py:54
  64.3 1.6 %project_turn.3 = (bf16[32,384]{1,0:T(8,128)(2,1)S(1)}, bf16[32,512]{1,0:T(8,128)(2,1)S(1)}) custom-call(bf16[112,5248]{1,0:T(8,128)(2,1)S(1)} %collective-permute-done.9.refs_0_, bf16[112,5248]{1,0:T(8,128)(2,1)S(1)} %collective-permute-done.10.refs_1_, bf16[3,5120,128]{2,1,0:T(8,128)(2,1)S(1)} %bitcast.10, ...), custom_call_target="tpu_custom_call" | custom-call | flops 754974720 | bytes 1048576 | tf_op jit(solution)/shard_map/project_turn/pallas_call | solution.py:163
  65.9 3.7 %collective-permute-start.14 = (bf16[32,384]{1,0:T(8,128)(2,1)S(1)}, bf16[32,384]{1,0:T(8,128)(2,1)S(1)}, u32[]{:S(2)}, u32[]{:S(2)}) collective-permute-start(bf16[32,384]{1,0:T(8,128)(2,1)S(1)} %get-tuple-element.32.qb_ref), channel_id=1, source_target_pairs={{0,1},{1,0},{2,3},{3,2},{4,5},{5,4},{6,7},{7,6},{8,9},{9,8},{10,11... | collective-permute-start | bytes 73736 | tf_op jit(solution)/shard_map/ppermute | solution.py:54
  69.6 0.1 collective-permute-start.13
  69.7 1.2 %project_cache.5.k2 = bf16[192,512]{1,0:T(8,128)(2,1)S(1)} custom-call(bf16[112,5248]{1,0:T(8,128)(2,1)S(1)} %collective-permute-done.9.refs_0_, bf16[112,5248]{1,0:T(8,128)(2,1)S(1)} %collective-permute-done.10.refs_1_, bf16[3,5120,128]{2,1,0:T(8,128)(2,1)S(1)} %bitcast.11, bf16[3,5120,128]{2,1,0:T(8,128)(2,1)S(1)} %collective-permute-done.8.refs_3_.refs_5_.refs_7_), custom_call_target="tpu_custom_call" | custom-call | flops 3019898880 | bytes 1048576 | tf_op jit(solution)/shard_map/project_cache/pallas_call | solution.py:184
  70.9 1.4 %attend.1 = bf16[32,8,384]{2,1,0:T(8,128)(2,1)S(1)} custom-call(bf16[96,384]{1,0:T(8,128)(2,1)S(1)} %get-tuple-element.29.qa_ref, bf16[32,384]{1,0:T(8,128)(2,1)S(1)} %get-tuple-element.32.qb_ref, bf16[96,384]{1,0:T(8,128)(2,1)S(1)} %collective-permute-done.13.qsa_ref, bf16[32,384]{1,0:T(8,128)(2,1)S(1)} %collective-permute-done.14.qsb_ref, ...), custom_call_target="tpu_custom_call" | custom-call | flops 234881024 | bytes 2097152 | tf_op jit(solution)/shard_map/attend/pallas_call | solution.py:250
  72.3 15.2 %all_to_all.5.in_ref = bf16[32,8,384]{2,1,0:T(8,128)(2,1)S(1)} all-to-all(bf16[32,8,384]{2,1,0:T(8,128)(2,1)S(1)} %attend.1), channel_id=1, replica_groups=mesh['grp'=8,'seq'=32] {'seq'}, dimensions={0} | all-to-all | bytes 393216 | tf_op jit(solution)/shard_map/all_to_all | solution.py:317
  87.6 1.1 %combine.1 = bf16[8,4096]{1,0:T(8,128)(2,1)} custom-call(bf16[32,8,384]{2,1,0:T(8,128)(2,1)S(1)} %all_to_all.5.in_ref), custom_call_target="tpu_custom_call" | custom-call | flops 262144 | bytes 458752 | tf_op jit(solution)/shard_map/combine/pallas_call | solution.py:284
  (15 shorter events, 0.1 us)
Async XLA Ops:
  2.5 19.9 %copy-start.1 = (bf16[28,5248]{1,0:T(8,128)(2,1)S(1)}, bf16[28,5248]{1,0:T(8,128)(2,1)}, u32[]{:S(2)}) copy-start(bf16[28,5248]{1,0:T(8,128)(2,1)} %get-tuple-element.23.a) | copy-start | bytes 881668
  2.5 23.7 %collective-permute-start.8 = (bf16[3,5120,128]{2,1,0:T(8,128)(2,1)}, bf16[3,5120,128]{2,1,0:T(8,128)(2,1)S(1)}, u32[]{:S(2)}, u32[]{:S(2)}) collective-permute-start(bf16[3,5120,128]{2,1,0:T(8,128)(2,1)} %bitcast.6), channel_id=1, source_target_pairs={{0,1},{1,0},{2,3},{3,2},{4,5},{5,4},{6,7},{7,6},{8,9},{9,8},{10,11... | collective-permute-start | bytes 11796488 | tf_op jit(solution)/shard_map/ppermute | solution.py:54
  5.9 6.5 %collective-permute-start.5 = (bf16[28,5248]{1,0:T(8,128)(2,1)}, bf16[28,5248]{1,0:T(8,128)(2,1)S(1)}, u32[]{:S(2)}, u32[]{:S(2)}) collective-permute-start(bf16[28,5248]{1,0:T(8,128)(2,1)} %get-tuple-element.24.a), channel_id=1, source_target_pairs={{0,6},{1,25},{2,0},{3,27},{4,2},{5,29},{6,4},{7,31},{8,14},{9,1},{... | collective-permute-start | bytes 881672 | tf_op jit(solution)/shard_map/ppermute | solution.py:54
  6.9 7.8 %collective-permute-start = (bf16[28,5248]{1,0:T(8,128)(2,1)}, bf16[28,5248]{1,0:T(8,128)(2,1)S(1)}, u32[]{:S(2)}, u32[]{:S(2)}) collective-permute-start(bf16[28,5248]{1,0:T(8,128)(2,1)} %get-tuple-element.23.a), channel_id=1, source_target_pairs={{0,2},{1,9},{2,4},{3,11},{4,6},{5,13},{6,0},{7,15},{8,10},{9,17},{... | collective-permute-start | bytes 881672 | tf_op jit(solution)/shard_map/ppermute | solution.py:54
  7.3 10.9 %collective-permute-start.4 = (bf16[28,5248]{1,0:T(8,128)(2,1)}, bf16[28,5248]{1,0:T(8,128)(2,1)S(1)}, u32[]{:S(2)}, u32[]{:S(2)}) collective-permute-start(bf16[28,5248]{1,0:T(8,128)(2,1)} %get-tuple-element.24.a), channel_id=1, source_target_pairs={{0,2},{1,9},{2,4},{3,11},{4,6},{5,13},{6,0},{7,15},{8,10},{9,17},{... | collective-permute-start | bytes 881672 | tf_op jit(solution)/shard_map/ppermute | solution.py:54
  12.4 6.3 %collective-permute-start.6 = (bf16[28,5248]{1,0:T(8,128)(2,1)S(1)}, bf16[28,5248]{1,0:T(8,128)(2,1)S(1)}, u32[]{:S(2)}, u32[]{:S(2)}) collective-permute-start(bf16[28,5248]{1,0:T(8,128)(2,1)S(1)} %collective-permute-done.5.c), channel_id=1, source_target_pairs={{0,6},{1,25},{2,0},{3,27},{4,2},{5,29},{6,4},{7,31},{8,14},{9,1},{... | collective-permute-start | bytes 881672 | tf_op jit(solution)/shard_map/ppermute | solution.py:54
  14.6 7.8 %collective-permute-start.1 = (bf16[28,5248]{1,0:T(8,128)(2,1)}, bf16[28,5248]{1,0:T(8,128)(2,1)S(1)}, u32[]{:S(2)}, u32[]{:S(2)}) collective-permute-start(bf16[28,5248]{1,0:T(8,128)(2,1)} %get-tuple-element.23.a), channel_id=1, source_target_pairs={{0,6},{1,25},{2,0},{3,27},{4,2},{5,29},{6,4},{7,31},{8,14},{9,1},{... | collective-permute-start | bytes 881672 | tf_op jit(solution)/shard_map/ppermute | solution.py:54
  14.6 7.8 %collective-permute-start.2 = (bf16[28,5248]{1,0:T(8,128)(2,1)S(1)}, bf16[28,5248]{1,0:T(8,128)(2,1)S(1)}, u32[]{:S(2)}, u32[]{:S(2)}) collective-permute-start(bf16[28,5248]{1,0:T(8,128)(2,1)S(1)} %collective-permute-done.b), channel_id=1, source_target_pairs={{0,2},{1,9},{2,4},{3,11},{4,6},{5,13},{6,0},{7,15},{8,10},{9,17},{... | collective-permute-start | bytes 881672 | tf_op jit(solution)/shard_map/ppermute | solution.py:54
  18.7 1.0 %copy-start.2 = (bf16[28,5248]{1,0:T(8,128)(2,1)S(1)}, bf16[28,5248]{1,0:T(8,128)(2,1)}, u32[]{:S(2)}) copy-start(bf16[28,5248]{1,0:T(8,128)(2,1)} %get-tuple-element.24.a) | copy-start | bytes 881668
  19.7 6.5 %copy-start = (bf16[5120,1,3,128]{3,0,2,1:T(8,128)(2,1)S(1)}, bf16[5120,1,3,128]{3,0,2,1:T(8,128)(2,1)}, u32[]{:S(2)}) copy-start(bf16[5120,1,3,128]{3,0,2,1:T(8,128)(2,1)} %param.8) | copy-start | bytes 11796484
  19.8 16.5 %collective-permute-start.7 = (bf16[112,5248]{1,0:T(8,128)(2,1)S(1)}, bf16[112,5248]{1,0:T(8,128)(2,1)S(1)}, u32[]{:S(2)}, u32[]{:S(2)}) collective-permute-start(bf16[112,5248]{1,0:T(8,128)(2,1)S(1)} %join_shards.3.refs_1_), channel_id=1, source_target_pairs={{0,24},{1,7},{2,26},{3,1},{4,28},{5,3},{6,30},{7,5},{8,0},{9,15},{... | collective-permute-start | bytes 3526664 | tf_op jit(solution)/shard_map/ppermute | solution.py:54
  22.5 16.6 %collective-permute-start.3 = (bf16[112,5248]{1,0:T(8,128)(2,1)S(1)}, bf16[112,5248]{1,0:T(8,128)(2,1)S(1)}, u32[]{:S(2)}, u32[]{:S(2)}) collective-permute-start(bf16[112,5248]{1,0:T(8,128)(2,1)S(1)} %join_shards.2.refs_0_), channel_id=1, source_target_pairs={{0,8},{1,3},{2,10},{3,5},{4,12},{5,7},{6,14},{7,1},{8,16},{9,11},{... | collective-permute-start | bytes 3526664 | tf_op jit(solution)/shard_map/ppermute | solution.py:54
  23.5 28.2 %collective-permute-start.11 = (bf16[112,5248]{1,0:T(8,128)(2,1)S(1)}, bf16[112,5248]{1,0:T(8,128)(2,1)S(1)}, u32[]{:S(2)}, u32[]{:S(2)}) collective-permute-start(bf16[112,5248]{1,0:T(8,128)(2,1)S(1)} %join_shards.3.refs_1_), channel_id=1, source_target_pairs={{0,8},{1,3},{2,10},{3,5},{4,12},{5,7},{6,14},{7,1},{8,16},{9,11},{... | collective-permute-start | bytes 3526664 | tf_op jit(solution)/shard_map/ppermute | solution.py:54
  24.7 27.0 %collective-permute-start.12 = (bf16[112,5248]{1,0:T(8,128)(2,1)S(1)}, bf16[112,5248]{1,0:T(8,128)(2,1)S(1)}, u32[]{:S(2)}, u32[]{:S(2)}) collective-permute-start(bf16[112,5248]{1,0:T(8,128)(2,1)S(1)} %join_shards.2.refs_0_), channel_id=1, source_target_pairs={{0,24},{1,7},{2,26},{3,1},{4,28},{5,3},{6,30},{7,5},{8,0},{9,15},{... | collective-permute-start | bytes 3526664 | tf_op jit(solution)/shard_map/ppermute | solution.py:54
  39.1 25.2 %collective-permute-start.9 = (bf16[112,5248]{1,0:T(8,128)(2,1)S(1)}, bf16[112,5248]{1,0:T(8,128)(2,1)S(1)}, u32[]{:S(2)}, u32[]{:S(2)}) collective-permute-start(bf16[112,5248]{1,0:T(8,128)(2,1)S(1)} %collective-permute-done.3.refs_0_.refs_2_), channel_id=1, source_target_pairs={{0,8},{1,3},{2,10},{3,5},{4,12},{5,7},{6,14},{7,1},{8,16},{9,11},{... | collective-permute-start | bytes 3526664 | tf_op jit(solution)/shard_map/ppermute | solution.py:54
  39.1 25.2 %collective-permute-start.10 = (bf16[112,5248]{1,0:T(8,128)(2,1)S(1)}, bf16[112,5248]{1,0:T(8,128)(2,1)S(1)}, u32[]{:S(2)}, u32[]{:S(2)}) collective-permute-start(bf16[112,5248]{1,0:T(8,128)(2,1)S(1)} %collective-permute-done.7.refs_3_.refs_5_), channel_id=1, source_target_pairs={{0,24},{1,7},{2,26},{3,1},{4,28},{5,3},{6,30},{7,5},{8,0},{9,15},{... | collective-permute-start | bytes 3526664 | tf_op jit(solution)/shard_map/ppermute | solution.py:54
  65.9 5.0 %collective-permute-start.14 = (bf16[32,384]{1,0:T(8,128)(2,1)S(1)}, bf16[32,384]{1,0:T(8,128)(2,1)S(1)}, u32[]{:S(2)}, u32[]{:S(2)}) collective-permute-start(bf16[32,384]{1,0:T(8,128)(2,1)S(1)} %get-tuple-element.32.qb_ref), channel_id=1, source_target_pairs={{0,1},{1,0},{2,3},{3,2},{4,5},{5,4},{6,7},{7,6},{8,9},{9,8},{10,11... | collective-permute-start | bytes 73736 | tf_op jit(solution)/shard_map/ppermute | solution.py:54
  69.6 1.3 %collective-permute-start.13 = (bf16[96,384]{1,0:T(8,128)(2,1)S(1)}, bf16[96,384]{1,0:T(8,128)(2,1)S(1)}, u32[]{:S(2)}, u32[]{:S(2)}) collective-permute-start(bf16[96,384]{1,0:T(8,128)(2,1)S(1)} %get-tuple-element.29.qa_ref), channel_id=1, source_target_pairs={{0,1},{1,0},{2,3},{3,2},{4,5},{5,4},{6,7},{7,6},{8,9},{9,8},{10,11... | collective-permute-start | bytes 221192 | tf_op jit(solution)/shard_map/ppermute | solution.py:54

commit v3 on v2

v3 whole, which is shorter than its diff:
```python
import functools

import jax
import jax.numpy as jnp
from jax import lax
from jax.experimental import pallas as pl
from jax.experimental.pallas import tpu as pltpu
from jax.sharding import PartitionSpec as P

MASKED_SCORE = -1e30
NY, NX = 4, 4
LIVE = 48
HD = 128
TURN = 8
PART = 20
REST = LIVE - PART
BF16 = jnp.bfloat16
F32 = jnp.float32


def index_of(y, x, c):
    return (y % NY * NX + x % NX) * 2 + c


def ring_pairs(step, first):
    pairs = []
    for y in range(NY):
        for x in range(NX):
            for c in range(2):
                along_x = (c == 0) == first
                dy, dx = (0, step) if along_x else (step, 0)
                pairs.append((index_of(y, x, c), index_of(y + dy, x + dx, c)))
    return pairs


A_UP, A_DOWN = ring_pairs(1, True), ring_pairs(-1, True)
B_UP, B_DOWN = ring_pairs(1, False), ring_pairs(-1, False)
SWAP = [(i, i ^ 1) for i in range(2 * NY * NX)]
OFFSETS = (0, -1, 1, -2)


def token_owner(me, group):
    core = lax.rem(me, 2)
    y, x = lax.div(me, 2 * NX), lax.rem(lax.div(me, 2), NX)
    along_x = core == 0
    if group >= NX * NY:
        core, along_x = 1 - core, core == 1
    b, a = OFFSETS[group % (NX * NY) // 4], OFFSETS[group % 4]
    dy, dx = jnp.where(along_x, b, a), jnp.where(along_x, a, b)
    return (lax.rem(y + dy + NY, NY) * NX + lax.rem(x + dx + NX, NX)) * 2 + core


def send(value, pairs):
    return lax.ppermute(value, "seq", pairs)


VMEM = pl.BlockSpec(memory_space=pltpu.VMEM)


def limit(mib):
    return pltpu.CompilerParams(vmem_limit_bytes=mib * 2**20)


def pack_kernel(*refs):
    sources, (one_ref, two_ref, both_ref), scratch, sems = refs[:5], refs[5:8], refs[8:13], refs[13]
    copies = [pltpu.make_async_copy(a, b, sems.at[i]) for i, (a, b) in enumerate(zip(sources, scratch))]
    for copy in copies:
        copy.start()
    for copy in copies:
        copy.wait()
    place_ref, len_ref, turn_place_ref, rows_ref, turn_ref = scratch
    n, d = rows_ref.shape
    i0 = lax.broadcasted_iota(jnp.int32, (n, n), 0)
    i1 = lax.broadcasted_iota(jnp.int32, (n, n), 1)
    place_col = jnp.sum(jnp.where(i0 == i1, place_ref[...], 0), axis=1, keepdims=True)
    owner = place_col // n
    inner = place_col - owner * n
    o1 = lax.broadcasted_iota(jnp.int32, (n, len_ref.shape[1]), 1)
    length = jnp.sum(jnp.where(o1 == owner, len_ref[...], 0), axis=1, keepdims=True)
    live_col = (inner < length).astype(jnp.int32)
    live_row = jnp.sum(jnp.where(i0 == i1, live_col, 0), axis=0, keepdims=True)
    rank_row = jnp.sum(jnp.where(i0 < i1, live_col, 0), axis=0, keepdims=True)
    rank_row = jnp.where(live_row > 0, rank_row, -1)
    k0 = lax.broadcasted_iota(jnp.int32, (LIVE, n), 0)
    pick = jnp.where(k0 == rank_row, 1.0, 0.0).astype(BF16)
    live = jnp.dot(pick, rows_ref[...], preferred_element_type=F32)
    two_ref[...] = live[PART:].astype(BF16)
    rows = jnp.concatenate([turn_ref[...].astype(F32), live], axis=0).astype(BF16)
    m = TURN + PART
    one_ref[:, :d] = rows[:m]
    both_ref[:, :d] = rows
    t0 = lax.broadcasted_iota(jnp.int32, (TURN + LIVE, TURN), 0)
    t1 = lax.broadcasted_iota(jnp.int32, (TURN + LIVE, TURN), 1)
    turn_col = jnp.sum(jnp.where(t0 == t1, turn_place_ref[...], 0), axis=1, keepdims=True)
    places = jnp.broadcast_to(turn_col.astype(F32), (TURN + LIVE, HD)).astype(BF16)
    one_ref[:, d:] = places[:m]
    both_ref[:, d:] = places


def pack(row_place, cache_len, group_place, cache_hidden, group_hidden):
    n, d = cache_hidden.shape
    m = TURN + PART
    args = (row_place.reshape(1, n), cache_len.reshape(1, -1), group_place.reshape(1, -1), cache_hidden, group_hidden)
    return pl.pallas_call(
        pack_kernel,
        in_specs=[pl.BlockSpec(memory_space=pl.ANY)] * 5,
        out_specs=[VMEM] * 3,
        out_shape=[jax.ShapeDtypeStruct(s, BF16) for s in ((m, d + HD), (REST, d), (m + REST, d + HD))],
        scratch_shapes=[pltpu.VMEM(v.shape, v.dtype) for v in args] + [pltpu.SemaphoreType.DMA((5,))],
        compiler_params=limit(56),
        cost_estimate=pl.CostEstimate(flops=2 * n * LIVE * d, bytes_accessed=4 * n * d, transcendentals=0),
        name="pack_live",
    )(*args)


def stage_kernel(in_ref, out_ref):
    out_ref[...] = in_ref[...]


def stage(x):
    return pl.pallas_call(
        stage_kernel,
        in_specs=[VMEM],
        out_specs=VMEM,
        out_shape=jax.ShapeDtypeStruct(x.shape, x.dtype),
        compiler_params=limit(8),
        cost_estimate=pl.CostEstimate(flops=0, bytes_accessed=4 * x.size, transcendentals=0),
        name="stage_rows",
    )(x)


def join_kernel(turns, own, up, down, far, out_ref):
    m, w = up.shape
    half = slice(0, m) if turns else slice(own.shape[0] - m, own.shape[0])
    x = [own[...].astype(F32)[half, :w], up[...].astype(F32), down[...].astype(F32)[half, :w], far[...].astype(F32)]
    n = len(x) * turns
    if turns:
        out_ref[:n] = jnp.concatenate([v[:turns] for v in x], axis=0).astype(BF16)
    out_ref[n:] = jnp.concatenate([v[turns:] for v in x], axis=0).astype(BF16)


def join(turns, *parts):
    m, w = parts[1].shape
    n = len(parts) * m
    return pl.pallas_call(
        functools.partial(join_kernel, turns),
        in_specs=[VMEM] * len(parts),
        out_specs=VMEM,
        out_shape=jax.ShapeDtypeStruct((n, w), BF16),
        compiler_params=limit(8),
        cost_estimate=pl.CostEstimate(flops=0, bytes_accessed=4 * n * w, transcendentals=0),
        name="join_shards",
    )(*parts)


def split_kernel(in_ref, turn_ref, rows_ref):
    n = turn_ref.shape[0]
    turn_ref[...] = in_ref[:n]
    rows_ref[...] = in_ref[n:, : rows_ref.shape[1]]


def split(block):
    m, w = block.shape
    n = 4 * TURN
    return pl.pallas_call(
        split_kernel,
        in_specs=[VMEM],
        out_specs=[VMEM] * 2,
        out_shape=[jax.ShapeDtypeStruct((n, w), BF16), jax.ShapeDtypeStruct((m - n, w - HD), BF16)],
        compiler_params=limit(8),
        cost_estimate=pl.CostEstimate(flops=0, bytes_accessed=4 * m * w, transcendentals=0),
        name="split_block",
    )(block)


def project_rows(refs, own_ref, other_ref):
    d = own_ref.shape[1]
    x = [r[4 * TURN :, :d] if r.shape[1] > d else r[...] for r in refs]
    w = jnp.concatenate([own_ref[1], own_ref[2], other_ref[1], other_ref[2]], axis=1)
    return jnp.dot(jnp.concatenate(x, axis=0), w, preferred_element_type=F32).astype(BF16)


def turn_kernel(*refs):
    *blocks, own_ref, other_ref, q_ref, kv_ref = refs
    d = own_ref.shape[1]
    turns = jnp.concatenate([r[: 4 * TURN] for r in blocks], axis=0)
    x = turns[:, :d]
    wq = jnp.concatenate([own_ref[0], other_ref[0]], axis=1)
    q_ref[:, : 2 * HD] = jnp.dot(x, wq, preferred_element_type=F32).astype(BF16)
    q_ref[:, 2 * HD :] = turns[:, d:]
    w = jnp.concatenate([own_ref[1], own_ref[2], other_ref[1], other_ref[2]], axis=1)
    kv_ref[...] = jnp.dot(x, w, preferred_element_type=F32).astype(BF16)


def turn_project(blocks, own, other):
    m, d = 16 * TURN, own.shape[1]
    return pl.pallas_call(
        turn_kernel,
        in_specs=[VMEM] * (len(blocks) + 2),
        out_specs=[VMEM] * 2,
        out_shape=[jax.ShapeDtypeStruct((m, 3 * HD), BF16), jax.ShapeDtypeStruct((m, 4 * HD), BF16)],
        compiler_params=limit(16),
        cost_estimate=pl.CostEstimate(flops=2 * m * d * 6 * HD * 6, bytes_accessed=2**20, transcendentals=0),
        name="project_turn",
    )(*blocks, own, other)


def cache_kernel(*refs):
    *rows, own_ref, other_ref, kv_ref = refs
    kv_ref[...] = project_rows(rows, own_ref, other_ref)


def cache_project(rows, own, other):
    m, d = 2 * LIVE * len(rows), own.shape[1]
    return pl.pallas_call(
        cache_kernel,
        in_specs=[VMEM] * (len(rows) + 2),
        out_specs=VMEM,
        out_shape=jax.ShapeDtypeStruct((m, 4 * HD), BF16),
        compiler_params=limit(16),
        cost_estimate=pl.CostEstimate(flops=2 * m * d * 4 * HD, bytes_accessed=2**20, transcendentals=0),
        name="project_cache",
    )(*rows, own, other)


def terms(x):
    hi = x.astype(BF16).astype(F32)
    mid = (x - hi).astype(BF16).astype(F32)
    return [hi, mid, x - hi - mid]


def scores_of(mine, theirs, h, keys):
    q = jnp.concatenate([mine[:, h * HD : (h + 1) * HD], theirs[:, (1 - h) * HD : (2 - h) * HD]], axis=0)
    nt = (((1,), (1,)), ((), ()))
    return lax.dot_general(q, keys, nt, preferred_element_type=F32) * HD ** (-0.5)


def key_value(block, h):
    return block[:, 2 * h * HD : (2 * h + 1) * HD], block[:, (2 * h + 1) * HD : (2 * h + 2) * HD]


def begin_kernel(q_ref, qs_ref, kvf_ref, *refs):
    *cache, sum_ref, top_ref, total_ref = refs
    mine, theirs, fresh = q_ref[...], qs_ref[...], kvf_ref[...]
    q_place = jnp.concatenate([mine[:, 2 * HD :], theirs[:, 2 * HD :]], axis=0).astype(F32)
    k_place = mine[:, 2 * HD :].astype(F32).T[0:1, :]
    seen = k_place <= q_place[:, 0:1]
    for h in range(2):
        pairs = [key_value(r[...], h) for r in cache] + [key_value(fresh, h)]
        s = [scores_of(mine, theirs, h, k) for k, _ in pairs]
        s[-1] = jnp.where(seen, s[-1], MASKED_SCORE)
        top = functools.reduce(jnp.maximum, [jnp.max(t, axis=1, keepdims=True) for t in s])
        total = jnp.zeros_like(top)
        summed = jnp.zeros((top.shape[0], HD), F32)
        for t, (_, v) in zip(s, pairs):
            e = jnp.exp(t - top)
            total += jnp.sum(e, axis=1, keepdims=True)
            summed += jnp.dot(e.astype(BF16), v, preferred_element_type=F32)
        sum_ref[h] = summed
        top_ref[h] = jnp.broadcast_to(top, summed.shape)
        total_ref[h] = jnp.broadcast_to(total, summed.shape)


def begin_attention(*arrays):
    tokens, keys = 2 * arrays[0].shape[0], sum(v.shape[0] for v in arrays[2:])
    return pl.pallas_call(
        begin_kernel,
        in_specs=[VMEM] * len(arrays),
        out_specs=[VMEM] * 3,
        out_shape=[jax.ShapeDtypeStruct((2, tokens, HD), F32)] * 3,
        compiler_params=limit(12),
        cost_estimate=pl.CostEstimate(
            flops=8 * tokens * keys * HD, bytes_accessed=2 * 2**20, transcendentals=2 * tokens * keys
        ),
        name="attend_begin",
    )(*arrays)


def end_kernel(q_ref, qs_ref, sum_ref, top_ref, total_ref, *refs):
    *rows, own_ref, other_ref, out_ref = refs
    me = lax.axis_index("seq")
    first = lax.rem(me, 2) == 0
    kv = project_rows(rows, own_ref, other_ref)
    mine, theirs = q_ref[...], qs_ref[...]
    tokens = sum_ref.shape[1]
    lane = lax.broadcasted_iota(jnp.int32, (tokens, HD), 1)
    outs, stats = [], []
    for h in range(2):
        keys, values = key_value(kv, h)
        s = scores_of(mine, theirs, h, keys)
        old = top_ref[h]
        top = jnp.maximum(old, jnp.max(s, axis=1, keepdims=True))
        e = jnp.exp(s - top[:, 0:1])
        scale = jnp.exp(old - top)
        total = total_ref[h] * scale + jnp.sum(e, axis=1, keepdims=True)
        outs.append(sum_ref[h] * scale + jnp.dot(e.astype(BF16), values, preferred_element_type=F32))
        stat = jnp.zeros((tokens, HD), F32)
        for i, v in enumerate(terms(top) + terms(total)):
            stat = jnp.where(lane % 64 // 8 == i, v, stat)
        stats.append(stat)
    low = jnp.where(first, outs[0], outs[1])
    high = jnp.where(first, outs[1], outs[0])
    stat = jnp.where((lane < 64) == first, stats[0], stats[1])
    whole = jnp.concatenate([low, high, stat], axis=1)
    for g in range(out_ref.shape[0]):
        out_ref[token_owner(me, g)] = whole[g * TURN : (g + 1) * TURN].astype(BF16)


def end_attention(*arrays):
    tokens, d, keys = 2 * arrays[0].shape[0], arrays[-1].shape[1], 4 * LIVE
    return pl.pallas_call(
        end_kernel,
        in_specs=[VMEM] * len(arrays),
        out_specs=VMEM,
        out_shape=jax.ShapeDtypeStruct((2 * NY * NX, TURN, 3 * HD), BF16),
        compiler_params=limit(16),
        cost_estimate=pl.CostEstimate(
            flops=8 * keys * HD * (d + tokens), bytes_accessed=2 * 2**20, transcendentals=2 * tokens * keys
        ),
        name="attend_end",
    )(*arrays)


def combine_kernel(in_ref, out_ref):
    for j in range(in_ref.shape[0] // 2):
        x = [in_ref[2 * j + i].astype(F32) for i in range(2)]
        for h in range(2):
            at = 2 * HD + 64 * h

            def total(v, i):
                s = at + 24 * i
                return v[:, s : s + 1] + v[:, s + 8 : s + 9] + v[:, s + 16 : s + 17]

            o0, o1 = [v[:, h * HD : (h + 1) * HD] for v in x]
            m0, m1 = [total(v, 0) for v in x]
            l0, l1 = [total(v, 1) for v in x]
            top = jnp.maximum(m0, m1)
            e0, e1 = jnp.exp(m0 - top), jnp.exp(m1 - top)
            out = (o0 * e0 + o1 * e1) / (l0 * e0 + l1 * e1)
            out_ref[:, (2 * j + h) * HD : (2 * j + h + 1) * HD] = out.astype(BF16)


def combine(parts):
    n, t, _ = parts.shape
    return pl.pallas_call(
        combine_kernel,
        out_shape=jax.ShapeDtypeStruct((t, n * HD), BF16),
        compiler_params=limit(4),
        cost_estimate=pl.CostEstimate(flops=n * t * HD * 8, bytes_accessed=n * t * HD * 14, transcendentals=n * t),
        name="combine",
    )(parts)


def shards(cache_hidden, group_hidden, proj_weight, row_place, cache_len, group_place):
    own = jnp.transpose(proj_weight[:, 0], (1, 0, 2))

    tie = lax.optimization_barrier
    one, two, both = pack(row_place, cache_len, group_place, cache_hidden, group_hidden)
    own, one, two, both = tie((own, one, two, both))
    one_up, two_up, down = send(one, A_UP), send(two, A_UP), send(both, A_DOWN)
    other = send(own, SWAP)
    one_up, staged = tie((one_up, stage(both)))
    first = join(TURN, staged, one_up, down, send(one_up, A_UP))
    second = join(0, staged, two_up, down, send(two_up, A_UP))
    first_down, second_up = send(first, B_DOWN), send(second, B_UP)
    second_down, first_up = send(second, B_DOWN), send(first, B_UP)
    first_down, second_up, other = tie((first_down, second_up, other))
    turn, rows = split(first_down)
    turn_far = send(turn, B_DOWN)
    far = send(rows, B_DOWN), send(second_up, B_UP)

    q, kv_turn = turn_project((first, first_up, first_down, turn_far), own, other)
    swapped = send(q, SWAP)
    kv = cache_project((first, second, first_up, second_up, first_down, second_down), own, other)
    begun = begin_attention(q, swapped, kv_turn, kv)
    *far, begun = tie((*far, begun))
    parts = end_attention(q, swapped, *begun, *far, own, other)
    landed = lax.all_to_all(parts, "seq", split_axis=0, concat_axis=0, tiled=True)
    return combine(landed)


def solution(mesh):
    in_specs = (
        P(("grp", "seq"), None),
        P(("grp", "seq"), None),
        P(None, "seq", None, None),
        P(("grp", "seq")),
        P("grp"),
        P(("grp", "seq")),
    )
    out_specs = P(("grp", "seq"), None)
    return jax.shard_map(shards, mesh=mesh, in_specs=in_specs, out_specs=out_specs, check_vma=False)
```

time: 88.9 us -> 83.4 us (0.938)
  starting transfers between devices: 21.2 us -> 15.2 us
  waiting for transfers between devices: 38.1 us -> 41 us
  blocking collectives: 15.2 us -> 13.7 us
  Pallas kernels: 13.1 us -> 12.2 us
    ppermute x15 -> x14, starting transfers between devices: 21.2 us -> 15.2 us  [send(): return lax.ppermute(value, 'seq', pairs)]
    ppermute x15 -> x14, waiting for transfers between devices: 38.1 us -> 41 us  [send(): return lax.ppermute(value, 'seq', pairs)]
    pallas_call x3 -> x6, Pallas kernels: 1.63 us -> 3.81 us  [the longest x1 2.14 us: end_attention(): pl.pallas_call(end_kernel, in_specs=[VMEM] * len(arrays), out_specs=VMEM,...]
    pallas_call x2 -> x1, Pallas kernels: 3.22 us -> 1.26 us  [turn_project(): pl.pallas_call(turn_kernel, in_specs=[VMEM] * (len(blocks) + 2), out_spec...]
    all_to_all x1, blocking collectives: 15.2 us -> 13.7 us  [shards(): lax.all_to_all(parts, 'seq', split_axis=0, concat_axis=0, tiled=True)]
    pallas_call x3 -> x1, Pallas kernels: 4.63 us -> 3.26 us  [cache_project(): pl.pallas_call(cache_kernel, in_specs=[VMEM] * (len(rows) + 2), out_specs...]
  transfers between devices with their start and end apart: 15 -> 14, of which waited for: 7 -> 7; matrix products, arithmetic and copies ran while one was open for 0% -> 0% of each run, Pallas kernels for 7% -> 7%
where the time goes in v3:
time: 83.4 us; the launch traced here: 83.2 us
  waiting for transfers between devices  41 us (49%)
  starting transfers between devices  15.2 us (18%)
  blocking collectives  13.7 us (16%)
  Pallas kernels  12.2 us (15%)
  local copies, waits for them, and re-layouts  1.1 us (1%)
    ppermute x14, waiting for transfers between devices, send(): return lax.ppermute(value, 'seq', pairs)  41 us
    ppermute x14, starting transfers between devices, send(): return lax.ppermute(value, 'seq', pairs)  15.2 us
    all_to_all x1, blocking collectives, shards(): lax.all_to_all(parts, 'seq', split_axis=0, concat_axis=0, tiled=True)  13.7 us
    pallas_call x1, Pallas kernels, cache_project(): pl.pallas_call(cache_kernel, in_specs=[VMEM] * (len(rows) + 2), out_specs...  3.26 us
    pallas_call x1, Pallas kernels, pack(): pl.pallas_call(pack_kernel, in_specs=[pl.BlockSpec(memory_space=pl.ANY)]...  2.71 us
    pallas_call x1, Pallas kernels, end_attention(): pl.pallas_call(end_kernel, in_specs=[VMEM] * len(arrays), out_specs=VMEM,...  2.14 us
  transfers between devices with their start and end apart: 14, of which 7 were waited for; matrix products, arithmetic and copies ran while one was open for 0% of the time, Pallas kernels for 7%

profile of v3, /device:TPU:1, one launch (start us, length us, event | category | flops | bytes accessed | tf_op | source)
XLA Modules:
  0.0 83.2 jit_solution(9054784178413277323)
XLA Ops:
  0.0 2.7 %pack_live.1 = (bf16[28,5248]{1,0:T(8,128)(2,1)}, bf16[28,5120]{1,0:T(8,128)(2,1)}, bf16[56,5248]{1,0:T(8,128)(2,1)}) custom-call(s32[1,64]{1,0:T(1,128)} %bitcast.10, s32[1,32]{1,0:T(1,128)} %bitcast.11, s32[1,8]{1,0:T(1,128)} %bitcast.12, bf16[64,5120]{1,0:T(8,128)(2,1)} %refs_3_.1, bf16[8,5120]{1,0:T(8,128)(2,1)} %refs_4_.1), custom_call_target="tpu_custom_call" | custom-call | flops 31457280 | bytes 1310720 | tf_op jit(solution)/shard_map/pack_live/pallas_call | solution.py:104
  2.7 3.3 %collective-permute-start.8 = (bf16[3,5120,128]{2,1,0:T(8,128)(2,1)}, bf16[3,5120,128]{2,1,0:T(8,128)(2,1)S(1)}, u32[]{:S(2)}, u32[]{:S(2)}) collective-permute-start(bf16[3,5120,128]{2,1,0:T(8,128)(2,1)} %bitcast.6), channel_id=1, source_target_pairs={{0,1},{1,0},{2,3},{3,2},{4,5},{5,4},{6,7},{7,6},{8,9},{9,8},{10,11... | collective-permute-start | bytes 11796488 | tf_op jit(solution)/shard_map/ppermute | solution.py:54
  6.0 0.0 collective-permute-start
  6.0 2.7 %collective-permute-start.1 = (bf16[56,5248]{1,0:T(8,128)(2,1)}, bf16[56,5248]{1,0:T(8,128)(2,1)S(1)}, u32[]{:S(2)}, u32[]{:S(2)}) collective-permute-start(bf16[56,5248]{1,0:T(8,128)(2,1)} %get-tuple-element.33.in_ref), channel_id=1, source_target_pairs={{0,6},{1,25},{2,0},{3,27},{4,2},{5,29},{6,4},{7,31},{8,14},{9,1},{... | collective-permute-start | bytes 1763336 | tf_op jit(solution)/shard_map/ppermute | solution.py:54
  8.7 1.1 %copy-done.1 = bf16[56,5248]{1,0:T(8,128)(2,1)S(1)} copy-done((bf16[56,5248]{1,0:T(8,128)(2,1)S(1)}, bf16[56,5248]{1,0:T(8,128)(2,1)}, u32[]{:S(2)}) %copy-start.1) | copy-done | bytes 587800
  9.9 3.9 %collective-permute-done.up = bf16[28,5248]{1,0:T(8,128)(2,1)S(1)} collective-permute-done((bf16[28,5248]{1,0:T(8,128)(2,1)}, bf16[28,5248]{1,0:T(8,128)(2,1)S(1)}, u32[]{:S(2)}, u32[]{:S(2)}) %collective-permute-start) | collective-permute-done | bytes 293920 | tf_op jit(solution)/shard_map/ppermute | solution.py:54
  13.8 3.5 %collective-permute-done.5.up = bf16[28,5120]{1,0:T(8,128)(2,1)S(1)} collective-permute-done((bf16[28,5120]{1,0:T(8,128)(2,1)}, bf16[28,5120]{1,0:T(8,128)(2,1)S(1)}, u32[]{:S(2)}, u32[]{:S(2)}) %collective-permute-start.5) | collective-permute-done | bytes 286752 | tf_op jit(solution)/shard_map/ppermute | solution.py:54
  17.3 0.0 collective-permute-start.6
  17.3 4.0 %collective-permute-done.2.far = bf16[28,5248]{1,0:T(8,128)(2,1)S(1)} collective-permute-done((bf16[28,5248]{1,0:T(8,128)(2,1)S(1)}, bf16[28,5248]{1,0:T(8,128)(2,1)S(1)}, u32[]{:S(2)}, u32[]{:S(2)}) %collective-permute-start.2) | collective-permute-done | bytes 293920 | tf_op jit(solution)/shard_map/ppermute | solution.py:54
  21.3 0.2 join_shards.2.refs_0_
  21.5 0.6 collective-permute-start.4
  22.1 2.7 %collective-permute-done.6.far = bf16[28,5120]{1,0:T(8,128)(2,1)S(1)} collective-permute-done((bf16[28,5120]{1,0:T(8,128)(2,1)S(1)}, bf16[28,5120]{1,0:T(8,128)(2,1)S(1)}, u32[]{:S(2)}, u32[]{:S(2)}) %collective-permute-start.6) | collective-permute-done | bytes 286752 | tf_op jit(solution)/shard_map/ppermute | solution.py:54
  24.8 0.3 join_shards.3.refs_1_
  25.1 0.1 collective-permute-start.7
  25.2 0.2 collective-permute-start.3
  25.3 2.6 %collective-permute-start.13 = (bf16[112,5120]{1,0:T(8,128)(2,1)S(1)}, bf16[112,5120]{1,0:T(8,128)(2,1)S(1)}, u32[]{:S(2)}, u32[]{:S(2)}) collective-permute-start(bf16[112,5120]{1,0:T(8,128)(2,1)S(1)} %join_shards.3.refs_1_), channel_id=1, source_target_pairs={{0,24},{1,7},{2,26},{3,1},{4,28},{5,3},{6,30},{7,5},{8,0},{9,15},{... | collective-permute-start | bytes 3440648 | tf_op jit(solution)/shard_map/ppermute | solution.py:54
  27.9 13.4 %collective-permute-done.7.refs_3_ = bf16[112,5120]{1,0:T(8,128)(2,1)S(1)} collective-permute-done((bf16[112,5120]{1,0:T(8,128)(2,1)S(1)}, bf16[112,5120]{1,0:T(8,128)(2,1)S(1)}, u32[]{:S(2)}, u32[]{:S(2)}) %collective-permute-start.7) | collective-permute-done | bytes 1146912 | tf_op jit(solution)/shard_map/ppermute | solution.py:54
  41.4 0.1 split_block.1
  41.5 0.1 collective-permute-start.9
  41.6 1.5 %collective-permute-start.12 = (bf16[112,5120]{1,0:T(8,128)(2,1)S(1)}, bf16[112,5120]{1,0:T(8,128)(2,1)S(1)}, u32[]{:S(2)}, u32[]{:S(2)}) collective-permute-start(bf16[112,5120]{1,0:T(8,128)(2,1)S(1)} %collective-permute-done.7.refs_3_), channel_id=1, source_target_pairs={{0,8},{1,3},{2,10},{3,5},{4,12},{5,7},{6,14},{7,1},{8,16},{9,11},{... | collective-permute-start | bytes 3440648 | tf_op jit(solution)/shard_map/ppermute | solution.py:54
  43.0 1.3 %collective-permute-start.11 = (bf16[80,5120]{1,0:T(8,128)(2,1)S(1)}, bf16[80,5120]{1,0:T(8,128)(2,1)S(1)}, u32[]{:S(2)}, u32[]{:S(2)}) collective-permute-start(bf16[80,5120]{1,0:T(8,128)(2,1)S(1)} %get-tuple-element.42), channel_id=1, source_target_pairs={{0,24},{1,7},{2,26},{3,1},{4,28},{5,3},{6,30},{7,5},{8,0},{9,15},{... | collective-permute-start | bytes 2457608 | tf_op jit(solution)/shard_map/ppermute | solution.py:54
  44.3 9.7 %collective-permute-done.3.refs_1_.refs_2_ = bf16[112,5248]{1,0:T(8,128)(2,1)S(1)} collective-permute-done((bf16[112,5248]{1,0:T(8,128)(2,1)S(1)}, bf16[112,5248]{1,0:T(8,128)(2,1)S(1)}, u32[]{:S(2)}, u32[]{:S(2)}) %collective-permute-start.3) | collective-permute-done | bytes 1175584 | tf_op jit(solution)/shard_map/ppermute | solution.py:54
  54.0 0.0 collective-permute-done.9.refs_3_
  54.0 1.3 %project_turn.1 = (bf16[128,384]{1,0:T(8,128)(2,1)S(1)}, bf16[128,512]{1,0:T(8,128)(2,1)S(1)}) custom-call(bf16[112,5248]{1,0:T(8,128)(2,1)S(1)} %join_shards.2.refs_0_, bf16[112,5248]{1,0:T(8,128)(2,1)S(1)} %collective-permute-done.3.refs_1_.refs_2_, bf16[112,5248]{1,0:T(8,128)(2,1)S(1)} %collective-permute-done.4.in_ref.refs_2_.refs_4_, ...), custom_call_target="tpu_custom_call" | custom-call | flops 6039797760 | bytes 1048576 | tf_op jit(solution)/shard_map/project_turn/pallas_call | solution.py:197
  55.2 2.9 %collective-permute-start.10 = (bf16[128,384]{1,0:T(8,128)(2,1)S(1)}, bf16[128,384]{1,0:T(8,128)(2,1)S(1)}, u32[]{:S(2)}, u32[]{:S(2)}) collective-permute-start(bf16[128,384]{1,0:T(8,128)(2,1)S(1)} %get-tuple-element.41.q_ref), channel_id=1, source_target_pairs={{0,1},{1,0},{2,3},{3,2},{4,5},{5,4},{6,7},{7,6},{8,9},{9,8},{10,11... | collective-permute-start | bytes 294920 | tf_op jit(solution)/shard_map/ppermute | solution.py:54
  58.2 3.3 %project_cache.1.refs_0_ = bf16[576,512]{1,0:T(8,128)(2,1)S(1)} custom-call(bf16[112,5248]{1,0:T(8,128)(2,1)S(1)} %join_shards.2.refs_0_, bf16[112,5120]{1,0:T(8,128)(2,1)S(1)} %join_shards.3.refs_1_, bf16[112,5248]{1,0:T(8,128)(2,1)S(1)} %collective-permute-done.3.refs_1_.refs_2_, bf16[112,5120]{1,0:T(8,128)(2,1)S(1)} %collective-permute-done.7.refs_3_, ...), custom_call_target="tpu_custom_call" | custom-call | flops 3019898880 | bytes 1048576 | tf_op jit(solution)/shard_map/project_cache/pallas_call | solution.py:215
  61.4 1.1 %attend_begin.1 = (f32[2,256,128]{2,1,0:T(8,128)S(1)}, f32[2,256,128]{2,1,0:T(8,128)S(1)}, f32[2,256,128]{2,1,0:T(8,128)S(1)}) custom-call(bf16[128,384]{1,0:T(8,128)(2,1)S(1)} %get-tuple-element.41.q_ref, bf16[128,384]{1,0:T(8,128)(2,1)S(1)} %collective-permute-done.10.qs_ref, bf16[128,512]{1,0:T(8,128)(2,1)S(1)} %get-tuple-element.44.kvf_ref, ...), custom_call_target="tpu_custom_call" | custom-call | flops 184549376 | bytes 2097152 | tf_op jit(solution)/shard_map/attend_begin/pallas_call | solution.py:266
  62.6 0.0 collective-permute-done.11.refs_0_
  62.6 3.7 %collective-permute-done.12.refs_1_ = bf16[112,5120]{1,0:T(8,128)(2,1)S(1)} collective-permute-done((bf16[112,5120]{1,0:T(8,128)(2,1)S(1)}, bf16[112,5120]{1,0:T(8,128)(2,1)S(1)}, u32[]{:S(2)}, u32[]{:S(2)}) %collective-permute-start.12) | collective-permute-done | bytes 1146912 | tf_op jit(solution)/shard_map/ppermute | solution.py:54
  66.3 2.1 %attend_end.1 = bf16[32,8,384]{2,1,0:T(8,128)(2,1)S(1)} custom-call(bf16[128,384]{1,0:T(8,128)(2,1)S(1)} %get-tuple-element.41.q_ref, bf16[128,384]{1,0:T(8,128)(2,1)S(1)} %collective-permute-done.10.qs_ref, f32[2,256,128]{2,1,0:T(8,128)S(1)} %get-tuple-element.48.sum_ref, f32[2,256,128]{2,1,0:T(8,128)S(1)} %get-tuple-element.49.top_ref, ...), custom_call_target="tpu_custom_call" | custom-call | flops 1056964608 | bytes 2097152 | tf_op jit(solution)/shard_map/attend_end/pallas_call | solution.py:311
  68.4 13.7 %all_to_all.5.in_ref = bf16[32,8,384]{2,1,0:T(8,128)(2,1)S(1)} all-to-all(bf16[32,8,384]{2,1,0:T(8,128)(2,1)S(1)} %attend_end.1), channel_id=1, replica_groups=mesh['grp'=8,'seq'=32] {'seq'}, dimensions={0} | all-to-all | bytes 393216 | tf_op jit(solution)/shard_map/all_to_all | solution.py:378
  82.1 1.1 %combine.1 = bf16[8,4096]{1,0:T(8,128)(2,1)} custom-call(bf16[32,8,384]{2,1,0:T(8,128)(2,1)S(1)} %all_to_all.5.in_ref), custom_call_target="tpu_custom_call" | custom-call | flops 262144 | bytes 458752 | tf_op jit(solution)/shard_map/combine/pallas_call | solution.py:345
  (11 shorter events, 0.1 us)
Async XLA Ops:
  2.7 38.7 %collective-permute-start.8 = (bf16[3,5120,128]{2,1,0:T(8,128)(2,1)}, bf16[3,5120,128]{2,1,0:T(8,128)(2,1)S(1)}, u32[]{:S(2)}, u32[]{:S(2)}) collective-permute-start(bf16[3,5120,128]{2,1,0:T(8,128)(2,1)} %bitcast.6), channel_id=1, source_target_pairs={{0,1},{1,0},{2,3},{3,2},{4,5},{5,4},{6,7},{7,6},{8,9},{9,8},{10,11... | collective-permute-start | bytes 11796488 | tf_op jit(solution)/shard_map/ppermute | solution.py:54
  6.0 7.7 %collective-permute-start = (bf16[28,5248]{1,0:T(8,128)(2,1)}, bf16[28,5248]{1,0:T(8,128)(2,1)S(1)}, u32[]{:S(2)}, u32[]{:S(2)}) collective-permute-start(bf16[28,5248]{1,0:T(8,128)(2,1)} %get-tuple-element.32), channel_id=1, source_target_pairs={{0,2},{1,9},{2,4},{3,11},{4,6},{5,13},{6,0},{7,15},{8,10},{9,17},{... | collective-permute-start | bytes 881672 | tf_op jit(solution)/shard_map/ppermute | solution.py:54
  6.0 15.2 %collective-permute-start.1 = (bf16[56,5248]{1,0:T(8,128)(2,1)}, bf16[56,5248]{1,0:T(8,128)(2,1)S(1)}, u32[]{:S(2)}, u32[]{:S(2)}) collective-permute-start(bf16[56,5248]{1,0:T(8,128)(2,1)} %get-tuple-element.33.in_ref), channel_id=1, source_target_pairs={{0,6},{1,25},{2,0},{3,27},{4,2},{5,29},{6,4},{7,31},{8,14},{9,1},{... | collective-permute-start | bytes 1763336 | tf_op jit(solution)/shard_map/ppermute | solution.py:54
  8.7 8.6 %collective-permute-start.5 = (bf16[28,5120]{1,0:T(8,128)(2,1)}, bf16[28,5120]{1,0:T(8,128)(2,1)S(1)}, u32[]{:S(2)}, u32[]{:S(2)}) collective-permute-start(bf16[28,5120]{1,0:T(8,128)(2,1)} %get-tuple-element.36), channel_id=1, source_target_pairs={{0,2},{1,9},{2,4},{3,11},{4,6},{5,13},{6,0},{7,15},{8,10},{9,17},{... | collective-permute-start | bytes 860168 | tf_op jit(solution)/shard_map/ppermute | solution.py:54
  8.7 1.1 %copy-start.1 = (bf16[56,5248]{1,0:T(8,128)(2,1)S(1)}, bf16[56,5248]{1,0:T(8,128)(2,1)}, u32[]{:S(2)}) copy-start(bf16[56,5248]{1,0:T(8,128)(2,1)} %get-tuple-element.33.in_ref) | copy-start | bytes 1763332
  13.8 7.5 %collective-permute-start.2 = (bf16[28,5248]{1,0:T(8,128)(2,1)S(1)}, bf16[28,5248]{1,0:T(8,128)(2,1)S(1)}, u32[]{:S(2)}, u32[]{:S(2)}) collective-permute-start(bf16[28,5248]{1,0:T(8,128)(2,1)S(1)} %collective-permute-done.up), channel_id=1, source_target_pairs={{0,2},{1,9},{2,4},{3,11},{4,6},{5,13},{6,0},{7,15},{8,10},{9,17},{... | collective-permute-start | bytes 881672 | tf_op jit(solution)/shard_map/ppermute | solution.py:54
  17.3 7.5 %collective-permute-start.6 = (bf16[28,5120]{1,0:T(8,128)(2,1)S(1)}, bf16[28,5120]{1,0:T(8,128)(2,1)S(1)}, u32[]{:S(2)}, u32[]{:S(2)}) collective-permute-start(bf16[28,5120]{1,0:T(8,128)(2,1)S(1)} %collective-permute-done.5.up), channel_id=1, source_target_pairs={{0,2},{1,9},{2,4},{3,11},{4,6},{5,13},{6,0},{7,15},{8,10},{9,17},{... | collective-permute-start | bytes 860168 | tf_op jit(solution)/shard_map/ppermute | solution.py:54
  21.5 19.9 %collective-permute-start.4 = (bf16[112,5248]{1,0:T(8,128)(2,1)S(1)}, bf16[112,5248]{1,0:T(8,128)(2,1)S(1)}, u32[]{:S(2)}, u32[]{:S(2)}) collective-permute-start(bf16[112,5248]{1,0:T(8,128)(2,1)S(1)} %join_shards.2.refs_0_), channel_id=1, source_target_pairs={{0,24},{1,7},{2,26},{3,1},{4,28},{5,3},{6,30},{7,5},{8,0},{9,15},{... | collective-permute-start | bytes 3526664 | tf_op jit(solution)/shard_map/ppermute | solution.py:54
  24.8 29.2 %copy-start = (bf16[5120,1,3,128]{3,0,2,1:T(8,128)(2,1)S(1)}, bf16[5120,1,3,128]{3,0,2,1:T(8,128)(2,1)}, u32[]{:S(2)}) copy-start(bf16[5120,1,3,128]{3,0,2,1:T(8,128)(2,1)} %param.8) | copy-start | bytes 11796484
  25.1 16.3 %collective-permute-start.7 = (bf16[112,5120]{1,0:T(8,128)(2,1)S(1)}, bf16[112,5120]{1,0:T(8,128)(2,1)S(1)}, u32[]{:S(2)}, u32[]{:S(2)}) collective-permute-start(bf16[112,5120]{1,0:T(8,128)(2,1)S(1)} %join_shards.3.refs_1_), channel_id=1, source_target_pairs={{0,8},{1,3},{2,10},{3,5},{4,12},{5,7},{6,14},{7,1},{8,16},{9,11},{... | collective-permute-start | bytes 3440648 | tf_op jit(solution)/shard_map/ppermute | solution.py:54
  25.2 28.8 %collective-permute-start.3 = (bf16[112,5248]{1,0:T(8,128)(2,1)S(1)}, bf16[112,5248]{1,0:T(8,128)(2,1)S(1)}, u32[]{:S(2)}, u32[]{:S(2)}) collective-permute-start(bf16[112,5248]{1,0:T(8,128)(2,1)S(1)} %join_shards.2.refs_0_), channel_id=1, source_target_pairs={{0,8},{1,3},{2,10},{3,5},{4,12},{5,7},{6,14},{7,1},{8,16},{9,11},{... | collective-permute-start | bytes 3526664 | tf_op jit(solution)/shard_map/ppermute | solution.py:54
  25.3 32.8 %collective-permute-start.13 = (bf16[112,5120]{1,0:T(8,128)(2,1)S(1)}, bf16[112,5120]{1,0:T(8,128)(2,1)S(1)}, u32[]{:S(2)}, u32[]{:S(2)}) collective-permute-start(bf16[112,5120]{1,0:T(8,128)(2,1)S(1)} %join_shards.3.refs_1_), channel_id=1, source_target_pairs={{0,24},{1,7},{2,26},{3,1},{4,28},{5,3},{6,30},{7,5},{8,0},{9,15},{... | collective-permute-start | bytes 3440648 | tf_op jit(solution)/shard_map/ppermute | solution.py:54
  41.5 12.5 %collective-permute-start.9 = (bf16[32,5248]{1,0:T(8,128)(2,1)S(1)}, bf16[32,5248]{1,0:T(8,128)(2,1)S(1)}, u32[]{:S(2)}, u32[]{:S(2)}) collective-permute-start(bf16[32,5248]{1,0:T(8,128)(2,1)S(1)} %get-tuple-element.39), channel_id=1, source_target_pairs={{0,24},{1,7},{2,26},{3,1},{4,28},{5,3},{6,30},{7,5},{8,0},{9,15},{... | collective-permute-start | bytes 1007624 | tf_op jit(solution)/shard_map/ppermute | solution.py:54
  41.6 24.7 %collective-permute-start.12 = (bf16[112,5120]{1,0:T(8,128)(2,1)S(1)}, bf16[112,5120]{1,0:T(8,128)(2,1)S(1)}, u32[]{:S(2)}, u32[]{:S(2)}) collective-permute-start(bf16[112,5120]{1,0:T(8,128)(2,1)S(1)} %collective-permute-done.7.refs_3_), channel_id=1, source_target_pairs={{0,8},{1,3},{2,10},{3,5},{4,12},{5,7},{6,14},{7,1},{8,16},{9,11},{... | collective-permute-start | bytes 3440648 | tf_op jit(solution)/shard_map/ppermute | solution.py:54
  43.0 19.6 %collective-permute-start.11 = (bf16[80,5120]{1,0:T(8,128)(2,1)S(1)}, bf16[80,5120]{1,0:T(8,128)(2,1)S(1)}, u32[]{:S(2)}, u32[]{:S(2)}) collective-permute-start(bf16[80,5120]{1,0:T(8,128)(2,1)S(1)} %get-tuple-element.42), channel_id=1, source_target_pairs={{0,24},{1,7},{2,26},{3,1},{4,28},{5,3},{6,30},{7,5},{8,0},{9,15},{... | collective-permute-start | bytes 2457608 | tf_op jit(solution)/shard_map/ppermute | solution.py:54
  55.2 6.2 %collective-permute-start.10 = (bf16[128,384]{1,0:T(8,128)(2,1)S(1)}, bf16[128,384]{1,0:T(8,128)(2,1)S(1)}, u32[]{:S(2)}, u32[]{:S(2)}) collective-permute-start(bf16[128,384]{1,0:T(8,128)(2,1)S(1)} %get-tuple-element.41.q_ref), channel_id=1, source_target_pairs={{0,1},{1,0},{2,3},{3,2},{4,5},{5,4},{6,7},{7,6},{8,9},{9,8},{10,11... | collective-permute-start | bytes 294920 | tf_op jit(solution)/shard_map/ppermute | solution.py:54

commit v4 on v3

--- a/solution.py
+++ b/solution.py
@@ -12,7 +12,7 @@
 LIVE = 48
 HD = 128
 TURN = 8
-PART = 20
+PART = 22
 REST = LIVE - PART
 BF16 = jnp.bfloat16
 F32 = jnp.float32
@@ -324,19 +324,16 @@
 def combine_kernel(in_ref, out_ref):
     for j in range(in_ref.shape[0] // 2):
         x = [in_ref[2 * j + i].astype(F32) for i in range(2)]
+        stat = [v[:, 2 * HD :] for v in x]
+        stat = [v + pltpu.roll(v, HD - 8, 1) + pltpu.roll(v, HD - 16, 1) for v in stat]
+        total = [pltpu.roll(v, HD - 24, 1) for v in stat]
+        top = jnp.maximum(*stat)
+        scale = [jnp.exp(v - top) for v in stat]
+        share = 1.0 / (total[0] * scale[0] + total[1] * scale[1])
+        scale = [v * share for v in scale]
         for h in range(2):
-            at = 2 * HD + 64 * h
-
-            def total(v, i):
-                s = at + 24 * i
-                return v[:, s : s + 1] + v[:, s + 8 : s + 9] + v[:, s + 16 : s + 17]
-
-            o0, o1 = [v[:, h * HD : (h + 1) * HD] for v in x]
-            m0, m1 = [total(v, 0) for v in x]
-            l0, l1 = [total(v, 1) for v in x]
-            top = jnp.maximum(m0, m1)
-            e0, e1 = jnp.exp(m0 - top), jnp.exp(m1 - top)
-            out = (o0 * e0 + o1 * e1) / (l0 * e0 + l1 * e1)
+            cols = slice(h * HD, (h + 1) * HD)
+            out = sum(v[:, cols] * e[:, 64 * h : 64 * h + 1] for v, e in zip(x, scale))
             out_ref[:, (2 * j + h) * HD : (2 * j + h + 1) * HD] = out.astype(BF16)
 
 

time: 83.4 us -> 82.3 us (0.987)
  waiting for transfers between devices: 41 us -> 40.1 us
    ppermute x14, waiting for transfers between devices: 41 us -> 40.1 us  [send(): return lax.ppermute(value, 'seq', pairs)]
  transfers between devices with their start and end apart: 14 -> 14, of which waited for: 7 -> 7; matrix products, arithmetic and copies ran while one was open for 0% -> 0% of each run, Pallas kernels for 7% -> 8%
where the time goes in v4:
time: 82.3 us; the launch traced here: 82.1 us
  waiting for transfers between devices  40.1 us (49%)
  starting transfers between devices  15.2 us (18%)
  blocking collectives  13.7 us (17%)
  Pallas kernels  12 us (15%)
  local copies, waits for them, and re-layouts  1.1 us (1%)
    ppermute x14, waiting for transfers between devices, send(): return lax.ppermute(value, 'seq', pairs)  40.1 us
    ppermute x14, starting transfers between devices, send(): return lax.ppermute(value, 'seq', pairs)  15.2 us
    all_to_all x1, blocking collectives, shards(): lax.all_to_all(parts, 'seq', split_axis=0, concat_axis=0, tiled=True)  13.7 us
    pallas_call x1, Pallas kernels, cache_project(): pl.pallas_call(cache_kernel, in_specs=[VMEM] * (len(rows) + 2), out_specs...  3.23 us
    pallas_call x1, Pallas kernels, pack(): pl.pallas_call(pack_kernel, in_specs=[pl.BlockSpec(memory_space=pl.ANY)]...  2.71 us
    pallas_call x1, Pallas kernels, end_attention(): pl.pallas_call(end_kernel, in_specs=[VMEM] * len(arrays), out_specs=VMEM,...  2.13 us
  transfers between devices with their start and end apart: 14, of which 7 were waited for; matrix products, arithmetic and copies ran while one was open for 0% of the time, Pallas kernels for 8%

profile of v4, /device:TPU:1, one launch (start us, length us, event | category | flops | bytes accessed | tf_op | source)
XLA Modules:
  0.0 82.1 jit_solution(15463907295901474657)
XLA Ops:
  0.0 2.7 %pack_live.1 = (bf16[30,5248]{1,0:T(8,128)(2,1)}, bf16[26,5120]{1,0:T(8,128)(2,1)}, bf16[56,5248]{1,0:T(8,128)(2,1)}) custom-call(s32[1,64]{1,0:T(1,128)} %bitcast.10, s32[1,32]{1,0:T(1,128)} %bitcast.11, s32[1,8]{1,0:T(1,128)} %bitcast.12, bf16[64,5120]{1,0:T(8,128)(2,1)} %refs_3_.1, bf16[8,5120]{1,0:T(8,128)(2,1)} %refs_4_.1), custom_call_target="tpu_custom_call" | custom-call | flops 31457280 | bytes 1310720 | tf_op jit(solution)/shard_map/pack_live/pallas_call | solution.py:104
  2.7 3.3 %collective-permute-start.8 = (bf16[3,5120,128]{2,1,0:T(8,128)(2,1)}, bf16[3,5120,128]{2,1,0:T(8,128)(2,1)S(1)}, u32[]{:S(2)}, u32[]{:S(2)}) collective-permute-start(bf16[3,5120,128]{2,1,0:T(8,128)(2,1)} %bitcast.6), channel_id=1, source_target_pairs={{0,1},{1,0},{2,3},{3,2},{4,5},{5,4},{6,7},{7,6},{8,9},{9,8},{10,11... | collective-permute-start | bytes 11796488 | tf_op jit(solution)/shard_map/ppermute | solution.py:54
  6.0 2.7 %collective-permute-start.1 = (bf16[56,5248]{1,0:T(8,128)(2,1)}, bf16[56,5248]{1,0:T(8,128)(2,1)S(1)}, u32[]{:S(2)}, u32[]{:S(2)}) collective-permute-start(bf16[56,5248]{1,0:T(8,128)(2,1)} %get-tuple-element.33.in_ref), channel_id=1, source_target_pairs={{0,6},{1,25},{2,0},{3,27},{4,2},{5,29},{6,4},{7,31},{8,14},{9,1},{... | collective-permute-start | bytes 1763336 | tf_op jit(solution)/shard_map/ppermute | solution.py:54
  8.7 0.0 collective-permute-start.5
  8.7 1.1 %copy-done.1 = bf16[56,5248]{1,0:T(8,128)(2,1)S(1)} copy-done((bf16[56,5248]{1,0:T(8,128)(2,1)S(1)}, bf16[56,5248]{1,0:T(8,128)(2,1)}, u32[]{:S(2)}) %copy-start.1) | copy-done | bytes 587800
  9.9 3.9 %collective-permute-done.up = bf16[30,5248]{1,0:T(8,128)(2,1)S(1)} collective-permute-done((bf16[30,5248]{1,0:T(8,128)(2,1)}, bf16[30,5248]{1,0:T(8,128)(2,1)S(1)}, u32[]{:S(2)}, u32[]{:S(2)}) %collective-permute-start) | collective-permute-done | bytes 314912 | tf_op jit(solution)/shard_map/ppermute | solution.py:54
  13.8 3.5 %collective-permute-done.5.up = bf16[26,5120]{1,0:T(8,128)(2,1)S(1)} collective-permute-done((bf16[26,5120]{1,0:T(8,128)(2,1)}, bf16[26,5120]{1,0:T(8,128)(2,1)S(1)}, u32[]{:S(2)}, u32[]{:S(2)}) %collective-permute-start.5) | collective-permute-done | bytes 266272 | tf_op jit(solution)/shard_map/ppermute | solution.py:54
  17.3 0.0 collective-permute-done.1.down
  17.3 4.0 %collective-permute-done.2.far = bf16[30,5248]{1,0:T(8,128)(2,1)S(1)} collective-permute-done((bf16[30,5248]{1,0:T(8,128)(2,1)S(1)}, bf16[30,5248]{1,0:T(8,128)(2,1)S(1)}, u32[]{:S(2)}, u32[]{:S(2)}) %collective-permute-start.2) | collective-permute-done | bytes 314912 | tf_op jit(solution)/shard_map/ppermute | solution.py:54
  21.3 0.2 join_shards.2.refs_0_
  21.5 0.6 collective-permute-start.4
  22.1 2.7 %collective-permute-done.6.far = bf16[26,5120]{1,0:T(8,128)(2,1)S(1)} collective-permute-done((bf16[26,5120]{1,0:T(8,128)(2,1)S(1)}, bf16[26,5120]{1,0:T(8,128)(2,1)S(1)}, u32[]{:S(2)}, u32[]{:S(2)}) %collective-permute-start.6) | collective-permute-done | bytes 266272 | tf_op jit(solution)/shard_map/ppermute | solution.py:54
  24.8 0.3 join_shards.3.refs_1_
  25.1 0.1 collective-permute-start.7
  25.2 0.2 collective-permute-start.3
  25.3 2.6 %collective-permute-start.13 = (bf16[104,5120]{1,0:T(8,128)(2,1)S(1)}, bf16[104,5120]{1,0:T(8,128)(2,1)S(1)}, u32[]{:S(2)}, u32[]{:S(2)}) collective-permute-start(bf16[104,5120]{1,0:T(8,128)(2,1)S(1)} %join_shards.3.refs_1_), channel_id=1, source_target_pairs={{0,24},{1,7},{2,26},{3,1},{4,28},{5,3},{6,30},{7,5},{8,0},{9,15},{... | collective-permute-start | bytes 3194888 | tf_op jit(solution)/shard_map/ppermute | solution.py:54
  27.9 12.6 %collective-permute-done.7.refs_3_ = bf16[104,5120]{1,0:T(8,128)(2,1)S(1)} collective-permute-done((bf16[104,5120]{1,0:T(8,128)(2,1)S(1)}, bf16[104,5120]{1,0:T(8,128)(2,1)S(1)}, u32[]{:S(2)}, u32[]{:S(2)}) %collective-permute-start.7) | collective-permute-done | bytes 1064992 | tf_op jit(solution)/shard_map/ppermute | solution.py:54
  40.5 0.0 collective-permute-done.8.refs_5_.refs_7_.refs_3_
  40.5 0.1 split_block.1
  40.6 0.1 collective-permute-start.9
  40.7 1.5 %collective-permute-start.12 = (bf16[104,5120]{1,0:T(8,128)(2,1)S(1)}, bf16[104,5120]{1,0:T(8,128)(2,1)S(1)}, u32[]{:S(2)}, u32[]{:S(2)}) collective-permute-start(bf16[104,5120]{1,0:T(8,128)(2,1)S(1)} %collective-permute-done.7.refs_3_), channel_id=1, source_target_pairs={{0,8},{1,3},{2,10},{3,5},{4,12},{5,7},{6,14},{7,1},{8,16},{9,11},{... | collective-permute-start | bytes 3194888 | tf_op jit(solution)/shard_map/ppermute | solution.py:54
  42.1 1.3 %collective-permute-start.11 = (bf16[88,5120]{1,0:T(8,128)(2,1)S(1)}, bf16[88,5120]{1,0:T(8,128)(2,1)S(1)}, u32[]{:S(2)}, u32[]{:S(2)}) collective-permute-start(bf16[88,5120]{1,0:T(8,128)(2,1)S(1)} %get-tuple-element.42), channel_id=1, source_target_pairs={{0,24},{1,7},{2,26},{3,1},{4,28},{5,3},{6,30},{7,5},{8,0},{9,15},{... | collective-permute-start | bytes 2703368 | tf_op jit(solution)/shard_map/ppermute | solution.py:54
  43.4 10.6 %collective-permute-done.3.refs_1_.refs_2_ = bf16[120,5248]{1,0:T(8,128)(2,1)S(1)} collective-permute-done((bf16[120,5248]{1,0:T(8,128)(2,1)S(1)}, bf16[120,5248]{1,0:T(8,128)(2,1)S(1)}, u32[]{:S(2)}, u32[]{:S(2)}) %collective-permute-start.3) | collective-permute-done | bytes 1259552 | tf_op jit(solution)/shard_map/ppermute | solution.py:54
  54.0 0.0 collective-permute-done.9.refs_3_
  54.0 1.3 %project_turn.1 = (bf16[128,384]{1,0:T(8,128)(2,1)S(1)}, bf16[128,512]{1,0:T(8,128)(2,1)S(1)}) custom-call(bf16[120,5248]{1,0:T(8,128)(2,1)S(1)} %join_shards.2.refs_0_, bf16[120,5248]{1,0:T(8,128)(2,1)S(1)} %collective-permute-done.3.refs_1_.refs_2_, bf16[120,5248]{1,0:T(8,128)(2,1)S(1)} %collective-permute-done.4.in_ref.refs_2_.refs_4_, ...), custom_call_target="tpu_custom_call" | custom-call | flops 6039797760 | bytes 1048576 | tf_op jit(solution)/shard_map/project_turn/pallas_call | solution.py:197
  55.3 2.9 %collective-permute-start.10 = (bf16[128,384]{1,0:T(8,128)(2,1)S(1)}, bf16[128,384]{1,0:T(8,128)(2,1)S(1)}, u32[]{:S(2)}, u32[]{:S(2)}) collective-permute-start(bf16[128,384]{1,0:T(8,128)(2,1)S(1)} %get-tuple-element.41.q_ref), channel_id=1, source_target_pairs={{0,1},{1,0},{2,3},{3,2},{4,5},{5,4},{6,7},{7,6},{8,9},{9,8},{10,11... | collective-permute-start | bytes 294920 | tf_op jit(solution)/shard_map/ppermute | solution.py:54
  58.2 3.2 %project_cache.1.refs_0_ = bf16[576,512]{1,0:T(8,128)(2,1)S(1)} custom-call(bf16[120,5248]{1,0:T(8,128)(2,1)S(1)} %join_shards.2.refs_0_, bf16[104,5120]{1,0:T(8,128)(2,1)S(1)} %join_shards.3.refs_1_, bf16[120,5248]{1,0:T(8,128)(2,1)S(1)} %collective-permute-done.3.refs_1_.refs_2_, bf16[104,5120]{1,0:T(8,128)(2,1)S(1)} %collective-permute-done.7.refs_3_, ...), custom_call_target="tpu_custom_call" | custom-call | flops 3019898880 | bytes 1048576 | tf_op jit(solution)/shard_map/project_cache/pallas_call | solution.py:215
  61.5 1.1 %attend_begin.1 = (f32[2,256,128]{2,1,0:T(8,128)S(1)}, f32[2,256,128]{2,1,0:T(8,128)S(1)}, f32[2,256,128]{2,1,0:T(8,128)S(1)}) custom-call(bf16[128,384]{1,0:T(8,128)(2,1)S(1)} %get-tuple-element.41.q_ref, bf16[128,384]{1,0:T(8,128)(2,1)S(1)} %collective-permute-done.10.qs_ref, bf16[128,512]{1,0:T(8,128)(2,1)S(1)} %get-tuple-element.44.kvf_ref, ...), custom_call_target="tpu_custom_call" | custom-call | flops 184549376 | bytes 2097152 | tf_op jit(solution)/shard_map/attend_begin/pallas_call | solution.py:266
  62.6 2.8 %collective-permute-done.12.refs_1_ = bf16[104,5120]{1,0:T(8,128)(2,1)S(1)} collective-permute-done((bf16[104,5120]{1,0:T(8,128)(2,1)S(1)}, bf16[104,5120]{1,0:T(8,128)(2,1)S(1)}, u32[]{:S(2)}, u32[]{:S(2)}) %collective-permute-start.12) | collective-permute-done | bytes 1064992 | tf_op jit(solution)/shard_map/ppermute | solution.py:54
  65.4 2.1 %attend_end.1 = bf16[32,8,384]{2,1,0:T(8,128)(2,1)S(1)} custom-call(bf16[128,384]{1,0:T(8,128)(2,1)S(1)} %get-tuple-element.41.q_ref, bf16[128,384]{1,0:T(8,128)(2,1)S(1)} %collective-permute-done.10.qs_ref, f32[2,256,128]{2,1,0:T(8,128)S(1)} %get-tuple-element.48.sum_ref, f32[2,256,128]{2,1,0:T(8,128)S(1)} %get-tuple-element.49.top_ref, ...), custom_call_target="tpu_custom_call" | custom-call | flops 1056964608 | bytes 2097152 | tf_op jit(solution)/shard_map/attend_end/pallas_call | solution.py:311
  67.5 13.7 %all_to_all.5.in_ref = bf16[32,8,384]{2,1,0:T(8,128)(2,1)S(1)} all-to-all(bf16[32,8,384]{2,1,0:T(8,128)(2,1)S(1)} %attend_end.1), channel_id=1, replica_groups=mesh['grp'=8,'seq'=32] {'seq'}, dimensions={0} | all-to-all | bytes 393216 | tf_op jit(solution)/shard_map/all_to_all | solution.py:375
  81.2 0.9 %combine.1 = bf16[8,4096]{1,0:T(8,128)(2,1)} custom-call(bf16[32,8,384]{2,1,0:T(8,128)(2,1)S(1)} %all_to_all.5.in_ref), custom_call_target="tpu_custom_call" | custom-call | flops 262144 | bytes 458752 | tf_op jit(solution)/shard_map/combine/pallas_call | solution.py:342
  (11 shorter events, 0.1 us)
Async XLA Ops:
  2.7 37.8 %collective-permute-start.8 = (bf16[3,5120,128]{2,1,0:T(8,128)(2,1)}, bf16[3,5120,128]{2,1,0:T(8,128)(2,1)S(1)}, u32[]{:S(2)}, u32[]{:S(2)}) collective-permute-start(bf16[3,5120,128]{2,1,0:T(8,128)(2,1)} %bitcast.6), channel_id=1, source_target_pairs={{0,1},{1,0},{2,3},{3,2},{4,5},{5,4},{6,7},{7,6},{8,9},{9,8},{10,11... | collective-permute-start | bytes 11796488 | tf_op jit(solution)/shard_map/ppermute | solution.py:54
  6.0 7.7 %collective-permute-start = (bf16[30,5248]{1,0:T(8,128)(2,1)}, bf16[30,5248]{1,0:T(8,128)(2,1)S(1)}, u32[]{:S(2)}, u32[]{:S(2)}) collective-permute-start(bf16[30,5248]{1,0:T(8,128)(2,1)} %get-tuple-element.32), channel_id=1, source_target_pairs={{0,2},{1,9},{2,4},{3,11},{4,6},{5,13},{6,0},{7,15},{8,10},{9,17},{... | collective-permute-start | bytes 944648 | tf_op jit(solution)/shard_map/ppermute | solution.py:54
  6.0 11.2 %collective-permute-start.1 = (bf16[56,5248]{1,0:T(8,128)(2,1)}, bf16[56,5248]{1,0:T(8,128)(2,1)S(1)}, u32[]{:S(2)}, u32[]{:S(2)}) collective-permute-start(bf16[56,5248]{1,0:T(8,128)(2,1)} %get-tuple-element.33.in_ref), channel_id=1, source_target_pairs={{0,6},{1,25},{2,0},{3,27},{4,2},{5,29},{6,4},{7,31},{8,14},{9,1},{... | collective-permute-start | bytes 1763336 | tf_op jit(solution)/shard_map/ppermute | solution.py:54
  8.7 8.6 %collective-permute-start.5 = (bf16[26,5120]{1,0:T(8,128)(2,1)}, bf16[26,5120]{1,0:T(8,128)(2,1)S(1)}, u32[]{:S(2)}, u32[]{:S(2)}) collective-permute-start(bf16[26,5120]{1,0:T(8,128)(2,1)} %get-tuple-element.36), channel_id=1, source_target_pairs={{0,2},{1,9},{2,4},{3,11},{4,6},{5,13},{6,0},{7,15},{8,10},{9,17},{... | collective-permute-start | bytes 798728 | tf_op jit(solution)/shard_map/ppermute | solution.py:54
  8.7 1.1 %copy-start.1 = (bf16[56,5248]{1,0:T(8,128)(2,1)S(1)}, bf16[56,5248]{1,0:T(8,128)(2,1)}, u32[]{:S(2)}) copy-start(bf16[56,5248]{1,0:T(8,128)(2,1)} %get-tuple-element.33.in_ref) | copy-start | bytes 1763332
  13.8 7.5 %collective-permute-start.2 = (bf16[30,5248]{1,0:T(8,128)(2,1)S(1)}, bf16[30,5248]{1,0:T(8,128)(2,1)S(1)}, u32[]{:S(2)}, u32[]{:S(2)}) collective-permute-start(bf16[30,5248]{1,0:T(8,128)(2,1)S(1)} %collective-permute-done.up), channel_id=1, source_target_pairs={{0,2},{1,9},{2,4},{3,11},{4,6},{5,13},{6,0},{7,15},{8,10},{9,17},{... | collective-permute-start | bytes 944648 | tf_op jit(solution)/shard_map/ppermute | solution.py:54
  17.3 7.5 %collective-permute-start.6 = (bf16[26,5120]{1,0:T(8,128)(2,1)S(1)}, bf16[26,5120]{1,0:T(8,128)(2,1)S(1)}, u32[]{:S(2)}, u32[]{:S(2)}) collective-permute-start(bf16[26,5120]{1,0:T(8,128)(2,1)S(1)} %collective-permute-done.5.up), channel_id=1, source_target_pairs={{0,2},{1,9},{2,4},{3,11},{4,6},{5,13},{6,0},{7,15},{8,10},{9,17},{... | collective-permute-start | bytes 798728 | tf_op jit(solution)/shard_map/ppermute | solution.py:54
  21.5 19.0 %collective-permute-start.4 = (bf16[120,5248]{1,0:T(8,128)(2,1)S(1)}, bf16[120,5248]{1,0:T(8,128)(2,1)S(1)}, u32[]{:S(2)}, u32[]{:S(2)}) collective-permute-start(bf16[120,5248]{1,0:T(8,128)(2,1)S(1)} %join_shards.2.refs_0_), channel_id=1, source_target_pairs={{0,24},{1,7},{2,26},{3,1},{4,28},{5,3},{6,30},{7,5},{8,0},{9,15},{... | collective-permute-start | bytes 3778568 | tf_op jit(solution)/shard_map/ppermute | solution.py:54
  24.8 29.2 %copy-start = (bf16[5120,1,3,128]{3,0,2,1:T(8,128)(2,1)S(1)}, bf16[5120,1,3,128]{3,0,2,1:T(8,128)(2,1)}, u32[]{:S(2)}) copy-start(bf16[5120,1,3,128]{3,0,2,1:T(8,128)(2,1)} %param.8) | copy-start | bytes 11796484
  25.1 15.4 %collective-permute-start.7 = (bf16[104,5120]{1,0:T(8,128)(2,1)S(1)}, bf16[104,5120]{1,0:T(8,128)(2,1)S(1)}, u32[]{:S(2)}, u32[]{:S(2)}) collective-permute-start(bf16[104,5120]{1,0:T(8,128)(2,1)S(1)} %join_shards.3.refs_1_), channel_id=1, source_target_pairs={{0,8},{1,3},{2,10},{3,5},{4,12},{5,7},{6,14},{7,1},{8,16},{9,11},{... | collective-permute-start | bytes 3194888 | tf_op jit(solution)/shard_map/ppermute | solution.py:54
  25.2 28.8 %collective-permute-start.3 = (bf16[120,5248]{1,0:T(8,128)(2,1)S(1)}, bf16[120,5248]{1,0:T(8,128)(2,1)S(1)}, u32[]{:S(2)}, u32[]{:S(2)}) collective-permute-start(bf16[120,5248]{1,0:T(8,128)(2,1)S(1)} %join_shards.2.refs_0_), channel_id=1, source_target_pairs={{0,8},{1,3},{2,10},{3,5},{4,12},{5,7},{6,14},{7,1},{8,16},{9,11},{... | collective-permute-start | bytes 3778568 | tf_op jit(solution)/shard_map/ppermute | solution.py:54
  25.3 32.9 %collective-permute-start.13 = (bf16[104,5120]{1,0:T(8,128)(2,1)S(1)}, bf16[104,5120]{1,0:T(8,128)(2,1)S(1)}, u32[]{:S(2)}, u32[]{:S(2)}) collective-permute-start(bf16[104,5120]{1,0:T(8,128)(2,1)S(1)} %join_shards.3.refs_1_), channel_id=1, source_target_pairs={{0,24},{1,7},{2,26},{3,1},{4,28},{5,3},{6,30},{7,5},{8,0},{9,15},{... | collective-permute-start | bytes 3194888 | tf_op jit(solution)/shard_map/ppermute | solution.py:54
  40.6 13.4 %collective-permute-start.9 = (bf16[32,5248]{1,0:T(8,128)(2,1)S(1)}, bf16[32,5248]{1,0:T(8,128)(2,1)S(1)}, u32[]{:S(2)}, u32[]{:S(2)}) collective-permute-start(bf16[32,5248]{1,0:T(8,128)(2,1)S(1)} %get-tuple-element.39), channel_id=1, source_target_pairs={{0,24},{1,7},{2,26},{3,1},{4,28},{5,3},{6,30},{7,5},{8,0},{9,15},{... | collective-permute-start | bytes 1007624 | tf_op jit(solution)/shard_map/ppermute | solution.py:54
  40.7 24.7 %collective-permute-start.12 = (bf16[104,5120]{1,0:T(8,128)(2,1)S(1)}, bf16[104,5120]{1,0:T(8,128)(2,1)S(1)}, u32[]{:S(2)}, u32[]{:S(2)}) collective-permute-start(bf16[104,5120]{1,0:T(8,128)(2,1)S(1)} %collective-permute-done.7.refs_3_), channel_id=1, source_target_pairs={{0,8},{1,3},{2,10},{3,5},{4,12},{5,7},{6,14},{7,1},{8,16},{9,11},{... | collective-permute-start | bytes 3194888 | tf_op jit(solution)/shard_map/ppermute | solution.py:54
  42.1 20.4 %collective-permute-start.11 = (bf16[88,5120]{1,0:T(8,128)(2,1)S(1)}, bf16[88,5120]{1,0:T(8,128)(2,1)S(1)}, u32[]{:S(2)}, u32[]{:S(2)}) collective-permute-start(bf16[88,5120]{1,0:T(8,128)(2,1)S(1)} %get-tuple-element.42), channel_id=1, source_target_pairs={{0,24},{1,7},{2,26},{3,1},{4,28},{5,3},{6,30},{7,5},{8,0},{9,15},{... | collective-permute-start | bytes 2703368 | tf_op jit(solution)/shard_map/ppermute | solution.py:54
  55.3 6.2 %collective-permute-start.10 = (bf16[128,384]{1,0:T(8,128)(2,1)S(1)}, bf16[128,384]{1,0:T(8,128)(2,1)S(1)}, u32[]{:S(2)}, u32[]{:S(2)}) collective-permute-start(bf16[128,384]{1,0:T(8,128)(2,1)S(1)} %get-tuple-element.41.q_ref), channel_id=1, source_target_pairs={{0,1},{1,0},{2,3},{3,2},{4,5},{5,4},{6,7},{7,6},{8,9},{9,8},{10,11... | collective-permute-start | bytes 294920 | tf_op jit(solution)/shard_map/ppermute | solution.py:54

commit v5 on v4

--- a/solution.py
+++ b/solution.py
@@ -61,14 +61,7 @@
     return pltpu.CompilerParams(vmem_limit_bytes=mib * 2**20)
 
 
-def pack_kernel(*refs):
-    sources, (one_ref, two_ref, both_ref), scratch, sems = refs[:5], refs[5:8], refs[8:13], refs[13]
-    copies = [pltpu.make_async_copy(a, b, sems.at[i]) for i, (a, b) in enumerate(zip(sources, scratch))]
-    for copy in copies:
-        copy.start()
-    for copy in copies:
-        copy.wait()
-    place_ref, len_ref, turn_place_ref, rows_ref, turn_ref = scratch
+def pack_kernel(place_ref, len_ref, turn_place_ref, rows_ref, turn_ref, one_ref, two_ref, both_ref):
     n, d = rows_ref.shape
     i0 = lax.broadcasted_iota(jnp.int32, (n, n), 0)
     i1 = lax.broadcasted_iota(jnp.int32, (n, n), 1)
@@ -103,10 +96,9 @@
     args = (row_place.reshape(1, n), cache_len.reshape(1, -1), group_place.reshape(1, -1), cache_hidden, group_hidden)
     return pl.pallas_call(
         pack_kernel,
-        in_specs=[pl.BlockSpec(memory_space=pl.ANY)] * 5,
+        in_specs=[VMEM] * 5,
         out_specs=[VMEM] * 3,
         out_shape=[jax.ShapeDtypeStruct(s, BF16) for s in ((m, d + HD), (REST, d), (m + REST, d + HD))],
-        scratch_shapes=[pltpu.VMEM(v.shape, v.dtype) for v in args] + [pltpu.SemaphoreType.DMA((5,))],
         compiler_params=limit(56),
         cost_estimate=pl.CostEstimate(flops=2 * n * LIVE * d, bytes_accessed=4 * n * d, transcendentals=0),
         name="pack_live",

time: 82.3 us -> 82.1 us (level)
  no operation moved by 1% of the time
where the time goes in v5:
time: 82.1 us; the launch traced here: 81.9 us
  waiting for transfers between devices  40.2 us (49%)
  starting transfers between devices  15 us (18%)
  blocking collectives  13.6 us (17%)
  Pallas kernels  12 us (15%)
  local copies, waits for them, and re-layouts  1.1 us (1%)
    ppermute x14, waiting for transfers between devices, send(): return lax.ppermute(value, 'seq', pairs)  40.2 us
    ppermute x14, starting transfers between devices, send(): return lax.ppermute(value, 'seq', pairs)  15 us
    all_to_all x1, blocking collectives, shards(): lax.all_to_all(parts, 'seq', split_axis=0, concat_axis=0, tiled=True)  13.6 us
    pallas_call x1, Pallas kernels, cache_project(): pl.pallas_call(cache_kernel, in_specs=[VMEM] * (len(rows) + 2), out_specs...  3.23 us
    pallas_call x1, Pallas kernels, pack(): pl.pallas_call(pack_kernel, in_specs=[VMEM] * 5, out_specs=[VMEM] * 3, ou...  2.66 us
    pallas_call x1, Pallas kernels, end_attention(): pl.pallas_call(end_kernel, in_specs=[VMEM] * len(arrays), out_specs=VMEM,...  2.14 us
  transfers between devices with their start and end apart: 14, of which 7 were waited for; matrix products, arithmetic and copies ran while one was open for 0% of the time, Pallas kernels for 8%

profile of v5, /device:TPU:1, one launch (start us, length us, event | category | flops | bytes accessed | tf_op | source)
XLA Modules:
  0.0 81.9 jit_solution(15796598837914419935)
XLA Ops:
  0.0 2.7 %pack_live.1 = (bf16[30,5248]{1,0:T(8,128)(2,1)}, bf16[26,5120]{1,0:T(8,128)(2,1)}, bf16[56,5248]{1,0:T(8,128)(2,1)}) custom-call(s32[1,64]{1,0:T(1,128)} %bitcast.10, s32[1,32]{1,0:T(1,128)} %bitcast.11, s32[1,8]{1,0:T(1,128)} %bitcast.12, bf16[64,5120]{1,0:T(8,128)(2,1)} %rows_ref.1, bf16[8,5120]{1,0:T(8,128)(2,1)} %turn_ref.1), custom_call_target="tpu_custom_call" | custom-call | flops 31457280 | bytes 1310720 | tf_op jit(solution)/shard_map/pack_live/pallas_call | solution.py:97
  2.7 3.2 %collective-permute-start.8 = (bf16[3,5120,128]{2,1,0:T(8,128)(2,1)}, bf16[3,5120,128]{2,1,0:T(8,128)(2,1)S(1)}, u32[]{:S(2)}, u32[]{:S(2)}) collective-permute-start(bf16[3,5120,128]{2,1,0:T(8,128)(2,1)} %bitcast.6), channel_id=1, source_target_pairs={{0,1},{1,0},{2,3},{3,2},{4,5},{5,4},{6,7},{7,6},{8,9},{9,8},{10,11... | collective-permute-start | bytes 11796488 | tf_op jit(solution)/shard_map/ppermute | solution.py:54
  5.9 0.0 collective-permute-start
  5.9 2.7 %collective-permute-start.1 = (bf16[56,5248]{1,0:T(8,128)(2,1)}, bf16[56,5248]{1,0:T(8,128)(2,1)S(1)}, u32[]{:S(2)}, u32[]{:S(2)}) collective-permute-start(bf16[56,5248]{1,0:T(8,128)(2,1)} %get-tuple-element.33.in_ref), channel_id=1, source_target_pairs={{0,6},{1,25},{2,0},{3,27},{4,2},{5,29},{6,4},{7,31},{8,14},{9,1},{... | collective-permute-start | bytes 1763336 | tf_op jit(solution)/shard_map/ppermute | solution.py:54
  8.6 1.1 %copy-done.1 = bf16[56,5248]{1,0:T(8,128)(2,1)S(1)} copy-done((bf16[56,5248]{1,0:T(8,128)(2,1)S(1)}, bf16[56,5248]{1,0:T(8,128)(2,1)}, u32[]{:S(2)}) %copy-start.1) | copy-done | bytes 587800
  9.7 3.9 %collective-permute-done.up = bf16[30,5248]{1,0:T(8,128)(2,1)S(1)} collective-permute-done((bf16[30,5248]{1,0:T(8,128)(2,1)}, bf16[30,5248]{1,0:T(8,128)(2,1)S(1)}, u32[]{:S(2)}, u32[]{:S(2)}) %collective-permute-start) | collective-permute-done | bytes 314912 | tf_op jit(solution)/shard_map/ppermute | solution.py:54
  13.6 3.5 %collective-permute-done.5.up = bf16[26,5120]{1,0:T(8,128)(2,1)S(1)} collective-permute-done((bf16[26,5120]{1,0:T(8,128)(2,1)}, bf16[26,5120]{1,0:T(8,128)(2,1)S(1)}, u32[]{:S(2)}, u32[]{:S(2)}) %collective-permute-start.5) | collective-permute-done | bytes 266272 | tf_op jit(solution)/shard_map/ppermute | solution.py:54
  17.1 0.0 collective-permute-start.6
  17.1 0.0 collective-permute-done.1.down
  17.1 4.0 %collective-permute-done.2.far = bf16[30,5248]{1,0:T(8,128)(2,1)S(1)} collective-permute-done((bf16[30,5248]{1,0:T(8,128)(2,1)S(1)}, bf16[30,5248]{1,0:T(8,128)(2,1)S(1)}, u32[]{:S(2)}, u32[]{:S(2)}) %collective-permute-start.2) | collective-permute-done | bytes 314912 | tf_op jit(solution)/shard_map/ppermute | solution.py:54
  21.1 0.2 join_shards.2.refs_0_
  21.4 0.6 collective-permute-start.4
  22.0 2.7 %collective-permute-done.6.far = bf16[26,5120]{1,0:T(8,128)(2,1)S(1)} collective-permute-done((bf16[26,5120]{1,0:T(8,128)(2,1)S(1)}, bf16[26,5120]{1,0:T(8,128)(2,1)S(1)}, u32[]{:S(2)}, u32[]{:S(2)}) %collective-permute-start.6) | collective-permute-done | bytes 266272 | tf_op jit(solution)/shard_map/ppermute | solution.py:54
  24.7 0.3 join_shards.3.refs_1_
  25.0 0.1 collective-permute-start.7
  25.0 0.1 collective-permute-start.3
  25.2 2.6 %collective-permute-start.13 = (bf16[104,5120]{1,0:T(8,128)(2,1)S(1)}, bf16[104,5120]{1,0:T(8,128)(2,1)S(1)}, u32[]{:S(2)}, u32[]{:S(2)}) collective-permute-start(bf16[104,5120]{1,0:T(8,128)(2,1)S(1)} %join_shards.3.refs_1_), channel_id=1, source_target_pairs={{0,24},{1,7},{2,26},{3,1},{4,28},{5,3},{6,30},{7,5},{8,0},{9,15},{... | collective-permute-start | bytes 3194888 | tf_op jit(solution)/shard_map/ppermute | solution.py:54
  27.8 12.6 %collective-permute-done.7.refs_3_ = bf16[104,5120]{1,0:T(8,128)(2,1)S(1)} collective-permute-done((bf16[104,5120]{1,0:T(8,128)(2,1)S(1)}, bf16[104,5120]{1,0:T(8,128)(2,1)S(1)}, u32[]{:S(2)}, u32[]{:S(2)}) %collective-permute-start.7) | collective-permute-done | bytes 1064992 | tf_op jit(solution)/shard_map/ppermute | solution.py:54
  40.4 0.0 collective-permute-done.4.in_ref.refs_2_.refs_4_
  40.4 0.1 split_block.1
  40.5 0.1 collective-permute-start.9
  40.5 1.5 %collective-permute-start.12 = (bf16[104,5120]{1,0:T(8,128)(2,1)S(1)}, bf16[104,5120]{1,0:T(8,128)(2,1)S(1)}, u32[]{:S(2)}, u32[]{:S(2)}) collective-permute-start(bf16[104,5120]{1,0:T(8,128)(2,1)S(1)} %collective-permute-done.7.refs_3_), channel_id=1, source_target_pairs={{0,8},{1,3},{2,10},{3,5},{4,12},{5,7},{6,14},{7,1},{8,16},{9,11},{... | collective-permute-start | bytes 3194888 | tf_op jit(solution)/shard_map/ppermute | solution.py:54
  42.0 1.3 %collective-permute-start.11 = (bf16[88,5120]{1,0:T(8,128)(2,1)S(1)}, bf16[88,5120]{1,0:T(8,128)(2,1)S(1)}, u32[]{:S(2)}, u32[]{:S(2)}) collective-permute-start(bf16[88,5120]{1,0:T(8,128)(2,1)S(1)} %get-tuple-element.42), channel_id=1, source_target_pairs={{0,24},{1,7},{2,26},{3,1},{4,28},{5,3},{6,30},{7,5},{8,0},{9,15},{... | collective-permute-start | bytes 2703368 | tf_op jit(solution)/shard_map/ppermute | solution.py:54
  43.3 10.6 %collective-permute-done.3.refs_1_.refs_2_ = bf16[120,5248]{1,0:T(8,128)(2,1)S(1)} collective-permute-done((bf16[120,5248]{1,0:T(8,128)(2,1)S(1)}, bf16[120,5248]{1,0:T(8,128)(2,1)S(1)}, u32[]{:S(2)}, u32[]{:S(2)}) %collective-permute-start.3) | collective-permute-done | bytes 1259552 | tf_op jit(solution)/shard_map/ppermute | solution.py:54
  53.9 1.3 %project_turn.1 = (bf16[128,384]{1,0:T(8,128)(2,1)S(1)}, bf16[128,512]{1,0:T(8,128)(2,1)S(1)}) custom-call(bf16[120,5248]{1,0:T(8,128)(2,1)S(1)} %join_shards.2.refs_0_, bf16[120,5248]{1,0:T(8,128)(2,1)S(1)} %collective-permute-done.3.refs_1_.refs_2_, bf16[120,5248]{1,0:T(8,128)(2,1)S(1)} %collective-permute-done.4.in_ref.refs_2_.refs_4_, ...), custom_call_target="tpu_custom_call" | custom-call | flops 6039797760 | bytes 1048576 | tf_op jit(solution)/shard_map/project_turn/pallas_call | solution.py:189
  55.1 2.8 %collective-permute-start.10 = (bf16[128,384]{1,0:T(8,128)(2,1)S(1)}, bf16[128,384]{1,0:T(8,128)(2,1)S(1)}, u32[]{:S(2)}, u32[]{:S(2)}) collective-permute-start(bf16[128,384]{1,0:T(8,128)(2,1)S(1)} %get-tuple-element.41.q_ref), channel_id=1, source_target_pairs={{0,1},{1,0},{2,3},{3,2},{4,5},{5,4},{6,7},{7,6},{8,9},{9,8},{10,11... | collective-permute-start | bytes 294920 | tf_op jit(solution)/shard_map/ppermute | solution.py:54
  58.0 3.2 %project_cache.1.refs_0_ = bf16[576,512]{1,0:T(8,128)(2,1)S(1)} custom-call(bf16[120,5248]{1,0:T(8,128)(2,1)S(1)} %join_shards.2.refs_0_, bf16[104,5120]{1,0:T(8,128)(2,1)S(1)} %join_shards.3.refs_1_, bf16[120,5248]{1,0:T(8,128)(2,1)S(1)} %collective-permute-done.3.refs_1_.refs_2_, bf16[104,5120]{1,0:T(8,128)(2,1)S(1)} %collective-permute-done.7.refs_3_, ...), custom_call_target="tpu_custom_call" | custom-call | flops 3019898880 | bytes 1048576 | tf_op jit(solution)/shard_map/project_cache/pallas_call | solution.py:207
  61.2 1.1 %attend_begin.1 = (f32[2,256,128]{2,1,0:T(8,128)S(1)}, f32[2,256,128]{2,1,0:T(8,128)S(1)}, f32[2,256,128]{2,1,0:T(8,128)S(1)}) custom-call(bf16[128,384]{1,0:T(8,128)(2,1)S(1)} %get-tuple-element.41.q_ref, bf16[128,384]{1,0:T(8,128)(2,1)S(1)} %collective-permute-done.10.qs_ref, bf16[128,512]{1,0:T(8,128)(2,1)S(1)} %get-tuple-element.44.kvf_ref, ...), custom_call_target="tpu_custom_call" | custom-call | flops 184549376 | bytes 2097152 | tf_op jit(solution)/shard_map/attend_begin/pallas_call | solution.py:258
  62.4 2.9 %collective-permute-done.12.refs_1_ = bf16[104,5120]{1,0:T(8,128)(2,1)S(1)} collective-permute-done((bf16[104,5120]{1,0:T(8,128)(2,1)S(1)}, bf16[104,5120]{1,0:T(8,128)(2,1)S(1)}, u32[]{:S(2)}, u32[]{:S(2)}) %collective-permute-start.12) | collective-permute-done | bytes 1064992 | tf_op jit(solution)/shard_map/ppermute | solution.py:54
  65.3 2.1 %attend_end.1 = bf16[32,8,384]{2,1,0:T(8,128)(2,1)S(1)} custom-call(bf16[128,384]{1,0:T(8,128)(2,1)S(1)} %get-tuple-element.41.q_ref, bf16[128,384]{1,0:T(8,128)(2,1)S(1)} %collective-permute-done.10.qs_ref, f32[2,256,128]{2,1,0:T(8,128)S(1)} %get-tuple-element.48.sum_ref, f32[2,256,128]{2,1,0:T(8,128)S(1)} %get-tuple-element.49.top_ref, ...), custom_call_target="tpu_custom_call" | custom-call | flops 1056964608 | bytes 2097152 | tf_op jit(solution)/shard_map/attend_end/pallas_call | solution.py:303
  67.4 13.6 %all_to_all.5.in_ref = bf16[32,8,384]{2,1,0:T(8,128)(2,1)S(1)} all-to-all(bf16[32,8,384]{2,1,0:T(8,128)(2,1)S(1)} %attend_end.1), channel_id=1, replica_groups=mesh['grp'=8,'seq'=32] {'seq'}, dimensions={0} | all-to-all | bytes 393216 | tf_op jit(solution)/shard_map/all_to_all | solution.py:367
  81.0 0.9 %combine.1 = bf16[8,4096]{1,0:T(8,128)(2,1)} custom-call(bf16[32,8,384]{2,1,0:T(8,128)(2,1)S(1)} %all_to_all.5.in_ref), custom_call_target="tpu_custom_call" | custom-call | flops 262144 | bytes 458752 | tf_op jit(solution)/shard_map/combine/pallas_call | solution.py:334
  (11 shorter events, 0.1 us)
Async XLA Ops:
  2.7 37.7 %collective-permute-start.8 = (bf16[3,5120,128]{2,1,0:T(8,128)(2,1)}, bf16[3,5120,128]{2,1,0:T(8,128)(2,1)S(1)}, u32[]{:S(2)}, u32[]{:S(2)}) collective-permute-start(bf16[3,5120,128]{2,1,0:T(8,128)(2,1)} %bitcast.6), channel_id=1, source_target_pairs={{0,1},{1,0},{2,3},{3,2},{4,5},{5,4},{6,7},{7,6},{8,9},{9,8},{10,11... | collective-permute-start | bytes 11796488 | tf_op jit(solution)/shard_map/ppermute | solution.py:54
  5.9 7.7 %collective-permute-start = (bf16[30,5248]{1,0:T(8,128)(2,1)}, bf16[30,5248]{1,0:T(8,128)(2,1)S(1)}, u32[]{:S(2)}, u32[]{:S(2)}) collective-permute-start(bf16[30,5248]{1,0:T(8,128)(2,1)} %get-tuple-element.32), channel_id=1, source_target_pairs={{0,2},{1,9},{2,4},{3,11},{4,6},{5,13},{6,0},{7,15},{8,10},{9,17},{... | collective-permute-start | bytes 944648 | tf_op jit(solution)/shard_map/ppermute | solution.py:54
  5.9 11.2 %collective-permute-start.1 = (bf16[56,5248]{1,0:T(8,128)(2,1)}, bf16[56,5248]{1,0:T(8,128)(2,1)S(1)}, u32[]{:S(2)}, u32[]{:S(2)}) collective-permute-start(bf16[56,5248]{1,0:T(8,128)(2,1)} %get-tuple-element.33.in_ref), channel_id=1, source_target_pairs={{0,6},{1,25},{2,0},{3,27},{4,2},{5,29},{6,4},{7,31},{8,14},{9,1},{... | collective-permute-start | bytes 1763336 | tf_op jit(solution)/shard_map/ppermute | solution.py:54
  8.6 8.6 %collective-permute-start.5 = (bf16[26,5120]{1,0:T(8,128)(2,1)}, bf16[26,5120]{1,0:T(8,128)(2,1)S(1)}, u32[]{:S(2)}, u32[]{:S(2)}) collective-permute-start(bf16[26,5120]{1,0:T(8,128)(2,1)} %get-tuple-element.36), channel_id=1, source_target_pairs={{0,2},{1,9},{2,4},{3,11},{4,6},{5,13},{6,0},{7,15},{8,10},{9,17},{... | collective-permute-start | bytes 798728 | tf_op jit(solution)/shard_map/ppermute | solution.py:54
  8.6 1.1 %copy-start.1 = (bf16[56,5248]{1,0:T(8,128)(2,1)S(1)}, bf16[56,5248]{1,0:T(8,128)(2,1)}, u32[]{:S(2)}) copy-start(bf16[56,5248]{1,0:T(8,128)(2,1)} %get-tuple-element.33.in_ref) | copy-start | bytes 1763332
  13.6 7.5 %collective-permute-start.2 = (bf16[30,5248]{1,0:T(8,128)(2,1)S(1)}, bf16[30,5248]{1,0:T(8,128)(2,1)S(1)}, u32[]{:S(2)}, u32[]{:S(2)}) collective-permute-start(bf16[30,5248]{1,0:T(8,128)(2,1)S(1)} %collective-permute-done.up), channel_id=1, source_target_pairs={{0,2},{1,9},{2,4},{3,11},{4,6},{5,13},{6,0},{7,15},{8,10},{9,17},{... | collective-permute-start | bytes 944648 | tf_op jit(solution)/shard_map/ppermute | solution.py:54
  17.1 7.5 %collective-permute-start.6 = (bf16[26,5120]{1,0:T(8,128)(2,1)S(1)}, bf16[26,5120]{1,0:T(8,128)(2,1)S(1)}, u32[]{:S(2)}, u32[]{:S(2)}) collective-permute-start(bf16[26,5120]{1,0:T(8,128)(2,1)S(1)} %collective-permute-done.5.up), channel_id=1, source_target_pairs={{0,2},{1,9},{2,4},{3,11},{4,6},{5,13},{6,0},{7,15},{8,10},{9,17},{... | collective-permute-start | bytes 798728 | tf_op jit(solution)/shard_map/ppermute | solution.py:54
  21.4 19.0 %collective-permute-start.4 = (bf16[120,5248]{1,0:T(8,128)(2,1)S(1)}, bf16[120,5248]{1,0:T(8,128)(2,1)S(1)}, u32[]{:S(2)}, u32[]{:S(2)}) collective-permute-start(bf16[120,5248]{1,0:T(8,128)(2,1)S(1)} %join_shards.2.refs_0_), channel_id=1, source_target_pairs={{0,24},{1,7},{2,26},{3,1},{4,28},{5,3},{6,30},{7,5},{8,0},{9,15},{... | collective-permute-start | bytes 3778568 | tf_op jit(solution)/shard_map/ppermute | solution.py:54
  24.7 29.2 %copy-start = (bf16[5120,1,3,128]{3,0,2,1:T(8,128)(2,1)S(1)}, bf16[5120,1,3,128]{3,0,2,1:T(8,128)(2,1)}, u32[]{:S(2)}) copy-start(bf16[5120,1,3,128]{3,0,2,1:T(8,128)(2,1)} %param.8) | copy-start | bytes 11796484
  25.0 15.4 %collective-permute-start.7 = (bf16[104,5120]{1,0:T(8,128)(2,1)S(1)}, bf16[104,5120]{1,0:T(8,128)(2,1)S(1)}, u32[]{:S(2)}, u32[]{:S(2)}) collective-permute-start(bf16[104,5120]{1,0:T(8,128)(2,1)S(1)} %join_shards.3.refs_1_), channel_id=1, source_target_pairs={{0,8},{1,3},{2,10},{3,5},{4,12},{5,7},{6,14},{7,1},{8,16},{9,11},{... | collective-permute-start | bytes 3194888 | tf_op jit(solution)/shard_map/ppermute | solution.py:54
  25.0 28.8 %collective-permute-start.3 = (bf16[120,5248]{1,0:T(8,128)(2,1)S(1)}, bf16[120,5248]{1,0:T(8,128)(2,1)S(1)}, u32[]{:S(2)}, u32[]{:S(2)}) collective-permute-start(bf16[120,5248]{1,0:T(8,128)(2,1)S(1)} %join_shards.2.refs_0_), channel_id=1, source_target_pairs={{0,8},{1,3},{2,10},{3,5},{4,12},{5,7},{6,14},{7,1},{8,16},{9,11},{... | collective-permute-start | bytes 3778568 | tf_op jit(solution)/shard_map/ppermute | solution.py:54
  25.2 32.8 %collective-permute-start.13 = (bf16[104,5120]{1,0:T(8,128)(2,1)S(1)}, bf16[104,5120]{1,0:T(8,128)(2,1)S(1)}, u32[]{:S(2)}, u32[]{:S(2)}) collective-permute-start(bf16[104,5120]{1,0:T(8,128)(2,1)S(1)} %join_shards.3.refs_1_), channel_id=1, source_target_pairs={{0,24},{1,7},{2,26},{3,1},{4,28},{5,3},{6,30},{7,5},{8,0},{9,15},{... | collective-permute-start | bytes 3194888 | tf_op jit(solution)/shard_map/ppermute | solution.py:54
  40.5 13.4 %collective-permute-start.9 = (bf16[32,5248]{1,0:T(8,128)(2,1)S(1)}, bf16[32,5248]{1,0:T(8,128)(2,1)S(1)}, u32[]{:S(2)}, u32[]{:S(2)}) collective-permute-start(bf16[32,5248]{1,0:T(8,128)(2,1)S(1)} %get-tuple-element.39), channel_id=1, source_target_pairs={{0,24},{1,7},{2,26},{3,1},{4,28},{5,3},{6,30},{7,5},{8,0},{9,15},{... | collective-permute-start | bytes 1007624 | tf_op jit(solution)/shard_map/ppermute | solution.py:54
  40.5 24.7 %collective-permute-start.12 = (bf16[104,5120]{1,0:T(8,128)(2,1)S(1)}, bf16[104,5120]{1,0:T(8,128)(2,1)S(1)}, u32[]{:S(2)}, u32[]{:S(2)}) collective-permute-start(bf16[104,5120]{1,0:T(8,128)(2,1)S(1)} %collective-permute-done.7.refs_3_), channel_id=1, source_target_pairs={{0,8},{1,3},{2,10},{3,5},{4,12},{5,7},{6,14},{7,1},{8,16},{9,11},{... | collective-permute-start | bytes 3194888 | tf_op jit(solution)/shard_map/ppermute | solution.py:54
  42.0 20.3 %collective-permute-start.11 = (bf16[88,5120]{1,0:T(8,128)(2,1)S(1)}, bf16[88,5120]{1,0:T(8,128)(2,1)S(1)}, u32[]{:S(2)}, u32[]{:S(2)}) collective-permute-start(bf16[88,5120]{1,0:T(8,128)(2,1)S(1)} %get-tuple-element.42), channel_id=1, source_target_pairs={{0,24},{1,7},{2,26},{3,1},{4,28},{5,3},{6,30},{7,5},{8,0},{9,15},{... | collective-permute-start | bytes 2703368 | tf_op jit(solution)/shard_map/ppermute | solution.py:54
  55.1 6.1 %collective-permute-start.10 = (bf16[128,384]{1,0:T(8,128)(2,1)S(1)}, bf16[128,384]{1,0:T(8,128)(2,1)S(1)}, u32[]{:S(2)}, u32[]{:S(2)}) collective-permute-start(bf16[128,384]{1,0:T(8,128)(2,1)S(1)} %get-tuple-element.41.q_ref), channel_id=1, source_target_pairs={{0,1},{1,0},{2,3},{3,2},{4,5},{5,4},{6,7},{7,6},{8,9},{9,8},{10,11... | collective-permute-start | bytes 294920 | tf_op jit(solution)/shard_map/ppermute | solution.py:54

commit v6 on v5

--- a/solution.py
+++ b/solution.py
@@ -33,8 +33,8 @@
     return pairs
 
 
-A_UP, A_DOWN = ring_pairs(1, True), ring_pairs(-1, True)
-B_UP, B_DOWN = ring_pairs(1, False), ring_pairs(-1, False)
+A_UP, A_DOWN = ring_pairs(1, False), ring_pairs(-1, False)
+B_UP, B_DOWN = ring_pairs(1, True), ring_pairs(-1, True)
 SWAP = [(i, i ^ 1) for i in range(2 * NY * NX)]
 OFFSETS = (0, -1, 1, -2)
 
@@ -42,9 +42,9 @@
 def token_owner(me, group):
     core = lax.rem(me, 2)
     y, x = lax.div(me, 2 * NX), lax.rem(lax.div(me, 2), NX)
-    along_x = core == 0
+    along_x = core == 1
     if group >= NX * NY:
-        core, along_x = 1 - core, core == 1
+        core, along_x = 1 - core, core == 0
     b, a = OFFSETS[group % (NX * NY) // 4], OFFSETS[group % 4]
     dy, dx = jnp.where(along_x, b, a), jnp.where(along_x, a, b)
     return (lax.rem(y + dy + NY, NY) * NX + lax.rem(x + dx + NX, NX)) * 2 + core

time: 82.1 us -> 82.1 us (level)
  no operation moved by 1% of the time
where the time goes in v6:
time: 82.1 us; the launch traced here: 81.9 us
  waiting for transfers between devices  40 us (49%)
  starting transfers between devices  15.2 us (19%)
  blocking collectives  13.6 us (17%)
  Pallas kernels  12 us (15%)
  local copies, waits for them, and re-layouts  1.1 us (1%)
    ppermute x14, waiting for transfers between devices, send(): return lax.ppermute(value, 'seq', pairs)  40 us
    ppermute x14, starting transfers between devices, send(): return lax.ppermute(value, 'seq', pairs)  15.2 us
    all_to_all x1, blocking collectives, shards(): lax.all_to_all(parts, 'seq', split_axis=0, concat_axis=0, tiled=True)  13.6 us
    pallas_call x1, Pallas kernels, cache_project(): pl.pallas_call(cache_kernel, in_specs=[VMEM] * (len(rows) + 2), out_specs...  3.23 us
    pallas_call x1, Pallas kernels, pack(): pl.pallas_call(pack_kernel, in_specs=[VMEM] * 5, out_specs=[VMEM] * 3, ou...  2.66 us
    pallas_call x1, Pallas kernels, end_attention(): pl.pallas_call(end_kernel, in_specs=[VMEM] * len(arrays), out_specs=VMEM,...  2.14 us
  transfers between devices with their start and end apart: 14, of which 7 were waited for; matrix products, arithmetic and copies ran while one was open for 0% of the time, Pallas kernels for 8%

profile of v6, /device:TPU:1, one launch (start us, length us, event | category | flops | bytes accessed | tf_op | source)
XLA Modules:
  0.0 81.9 jit_solution(15836617233057212401)
XLA Ops:
  0.0 2.7 %pack_live.1 = (bf16[30,5248]{1,0:T(8,128)(2,1)}, bf16[26,5120]{1,0:T(8,128)(2,1)}, bf16[56,5248]{1,0:T(8,128)(2,1)}) custom-call(s32[1,64]{1,0:T(1,128)} %bitcast.10, s32[1,32]{1,0:T(1,128)} %bitcast.11, s32[1,8]{1,0:T(1,128)} %bitcast.12, bf16[64,5120]{1,0:T(8,128)(2,1)} %rows_ref.1, bf16[8,5120]{1,0:T(8,128)(2,1)} %turn_ref.1), custom_call_target="tpu_custom_call" | custom-call | flops 31457280 | bytes 1310720 | tf_op jit(solution)/shard_map/pack_live/pallas_call | solution.py:97
  2.7 3.2 %collective-permute-start.8 = (bf16[3,5120,128]{2,1,0:T(8,128)(2,1)}, bf16[3,5120,128]{2,1,0:T(8,128)(2,1)S(1)}, u32[]{:S(2)}, u32[]{:S(2)}) collective-permute-start(bf16[3,5120,128]{2,1,0:T(8,128)(2,1)} %bitcast.6), channel_id=1, source_target_pairs={{0,1},{1,0},{2,3},{3,2},{4,5},{5,4},{6,7},{7,6},{8,9},{9,8},{10,11... | collective-permute-start | bytes 11796488 | tf_op jit(solution)/shard_map/ppermute | solution.py:54
  5.9 2.7 %collective-permute-start.1 = (bf16[56,5248]{1,0:T(8,128)(2,1)}, bf16[56,5248]{1,0:T(8,128)(2,1)S(1)}, u32[]{:S(2)}, u32[]{:S(2)}) collective-permute-start(bf16[56,5248]{1,0:T(8,128)(2,1)} %get-tuple-element.33.in_ref), channel_id=1, source_target_pairs={{0,24},{1,7},{2,26},{3,1},{4,28},{5,3},{6,30},{7,5},{8,0},{9,15},{... | collective-permute-start | bytes 1763336 | tf_op jit(solution)/shard_map/ppermute | solution.py:54
  8.6 0.0 collective-permute-start.5
  8.6 1.1 %copy-done.1 = bf16[56,5248]{1,0:T(8,128)(2,1)S(1)} copy-done((bf16[56,5248]{1,0:T(8,128)(2,1)S(1)}, bf16[56,5248]{1,0:T(8,128)(2,1)}, u32[]{:S(2)}) %copy-start.1) | copy-done | bytes 587800
  9.7 3.9 %collective-permute-done.up = bf16[30,5248]{1,0:T(8,128)(2,1)S(1)} collective-permute-done((bf16[30,5248]{1,0:T(8,128)(2,1)}, bf16[30,5248]{1,0:T(8,128)(2,1)S(1)}, u32[]{:S(2)}, u32[]{:S(2)}) %collective-permute-start) | collective-permute-done | bytes 314912 | tf_op jit(solution)/shard_map/ppermute | solution.py:54
  13.6 0.0 collective-permute-start.2
  13.6 3.5 %collective-permute-done.5.up = bf16[26,5120]{1,0:T(8,128)(2,1)S(1)} collective-permute-done((bf16[26,5120]{1,0:T(8,128)(2,1)}, bf16[26,5120]{1,0:T(8,128)(2,1)S(1)}, u32[]{:S(2)}, u32[]{:S(2)}) %collective-permute-start.5) | collective-permute-done | bytes 266272 | tf_op jit(solution)/shard_map/ppermute | solution.py:54
  17.1 4.0 %collective-permute-done.2.far = bf16[30,5248]{1,0:T(8,128)(2,1)S(1)} collective-permute-done((bf16[30,5248]{1,0:T(8,128)(2,1)S(1)}, bf16[30,5248]{1,0:T(8,128)(2,1)S(1)}, u32[]{:S(2)}, u32[]{:S(2)}) %collective-permute-start.2) | collective-permute-done | bytes 314912 | tf_op jit(solution)/shard_map/ppermute | solution.py:54
  21.1 0.2 join_shards.2.refs_0_
  21.4 0.8 collective-permute-start.4
  22.2 2.5 %collective-permute-done.6.far = bf16[26,5120]{1,0:T(8,128)(2,1)S(1)} collective-permute-done((bf16[26,5120]{1,0:T(8,128)(2,1)S(1)}, bf16[26,5120]{1,0:T(8,128)(2,1)S(1)}, u32[]{:S(2)}, u32[]{:S(2)}) %collective-permute-start.6) | collective-permute-done | bytes 266272 | tf_op jit(solution)/shard_map/ppermute | solution.py:54
  24.7 0.3 join_shards.3.refs_1_
  25.0 0.1 collective-permute-start.7
  25.0 0.3 collective-permute-start.3
  25.3 2.5 %collective-permute-start.13 = (bf16[104,5120]{1,0:T(8,128)(2,1)S(1)}, bf16[104,5120]{1,0:T(8,128)(2,1)S(1)}, u32[]{:S(2)}, u32[]{:S(2)}) collective-permute-start(bf16[104,5120]{1,0:T(8,128)(2,1)S(1)} %join_shards.3.refs_1_), channel_id=1, source_target_pairs={{0,6},{1,25},{2,0},{3,27},{4,2},{5,29},{6,4},{7,31},{8,14},{9,1},{... | collective-permute-start | bytes 3194888 | tf_op jit(solution)/shard_map/ppermute | solution.py:54
  27.8 12.6 %collective-permute-done.7.refs_3_ = bf16[104,5120]{1,0:T(8,128)(2,1)S(1)} collective-permute-done((bf16[104,5120]{1,0:T(8,128)(2,1)S(1)}, bf16[104,5120]{1,0:T(8,128)(2,1)S(1)}, u32[]{:S(2)}, u32[]{:S(2)}) %collective-permute-start.7) | collective-permute-done | bytes 1064992 | tf_op jit(solution)/shard_map/ppermute | solution.py:54
  40.4 0.1 split_block.1
  40.5 0.1 collective-permute-start.9
  40.5 1.5 %collective-permute-start.12 = (bf16[104,5120]{1,0:T(8,128)(2,1)S(1)}, bf16[104,5120]{1,0:T(8,128)(2,1)S(1)}, u32[]{:S(2)}, u32[]{:S(2)}) collective-permute-start(bf16[104,5120]{1,0:T(8,128)(2,1)S(1)} %collective-permute-done.7.refs_3_), channel_id=1, source_target_pairs={{0,2},{1,9},{2,4},{3,11},{4,6},{5,13},{6,0},{7,15},{8,10},{9,17},{... | collective-permute-start | bytes 3194888 | tf_op jit(solution)/shard_map/ppermute | solution.py:54
  42.0 1.3 %collective-permute-start.11 = (bf16[88,5120]{1,0:T(8,128)(2,1)S(1)}, bf16[88,5120]{1,0:T(8,128)(2,1)S(1)}, u32[]{:S(2)}, u32[]{:S(2)}) collective-permute-start(bf16[88,5120]{1,0:T(8,128)(2,1)S(1)} %get-tuple-element.42), channel_id=1, source_target_pairs={{0,6},{1,25},{2,0},{3,27},{4,2},{5,29},{6,4},{7,31},{8,14},{9,1},{... | collective-permute-start | bytes 2703368 | tf_op jit(solution)/shard_map/ppermute | solution.py:54
  43.3 10.6 %collective-permute-done.3.refs_1_.refs_2_ = bf16[120,5248]{1,0:T(8,128)(2,1)S(1)} collective-permute-done((bf16[120,5248]{1,0:T(8,128)(2,1)S(1)}, bf16[120,5248]{1,0:T(8,128)(2,1)S(1)}, u32[]{:S(2)}, u32[]{:S(2)}) %collective-permute-start.3) | collective-permute-done | bytes 1259552 | tf_op jit(solution)/shard_map/ppermute | solution.py:54
  53.9 0.0 collective-permute-done.9.refs_3_
  53.9 1.3 %project_turn.1 = (bf16[128,384]{1,0:T(8,128)(2,1)S(1)}, bf16[128,512]{1,0:T(8,128)(2,1)S(1)}) custom-call(bf16[120,5248]{1,0:T(8,128)(2,1)S(1)} %join_shards.2.refs_0_, bf16[120,5248]{1,0:T(8,128)(2,1)S(1)} %collective-permute-done.3.refs_1_.refs_2_, bf16[120,5248]{1,0:T(8,128)(2,1)S(1)} %collective-permute-done.4.in_ref.refs_2_.refs_4_, ...), custom_call_target="tpu_custom_call" | custom-call | flops 6039797760 | bytes 1048576 | tf_op jit(solution)/shard_map/project_turn/pallas_call | solution.py:189
  55.1 2.8 %collective-permute-start.10 = (bf16[128,384]{1,0:T(8,128)(2,1)S(1)}, bf16[128,384]{1,0:T(8,128)(2,1)S(1)}, u32[]{:S(2)}, u32[]{:S(2)}) collective-permute-start(bf16[128,384]{1,0:T(8,128)(2,1)S(1)} %get-tuple-element.41.q_ref), channel_id=1, source_target_pairs={{0,1},{1,0},{2,3},{3,2},{4,5},{5,4},{6,7},{7,6},{8,9},{9,8},{10,11... | collective-permute-start | bytes 294920 | tf_op jit(solution)/shard_map/ppermute | solution.py:54
  58.0 0.0 collective-permute-done.13.refs_5_
  58.0 3.2 %project_cache.1.refs_0_ = bf16[576,512]{1,0:T(8,128)(2,1)S(1)} custom-call(bf16[120,5248]{1,0:T(8,128)(2,1)S(1)} %join_shards.2.refs_0_, bf16[104,5120]{1,0:T(8,128)(2,1)S(1)} %join_shards.3.refs_1_, bf16[120,5248]{1,0:T(8,128)(2,1)S(1)} %collective-permute-done.3.refs_1_.refs_2_, bf16[104,5120]{1,0:T(8,128)(2,1)S(1)} %collective-permute-done.7.refs_3_, ...), custom_call_target="tpu_custom_call" | custom-call | flops 3019898880 | bytes 1048576 | tf_op jit(solution)/shard_map/project_cache/pallas_call | solution.py:207
  61.2 1.1 %attend_begin.1 = (f32[2,256,128]{2,1,0:T(8,128)S(1)}, f32[2,256,128]{2,1,0:T(8,128)S(1)}, f32[2,256,128]{2,1,0:T(8,128)S(1)}) custom-call(bf16[128,384]{1,0:T(8,128)(2,1)S(1)} %get-tuple-element.41.q_ref, bf16[128,384]{1,0:T(8,128)(2,1)S(1)} %collective-permute-done.10.qs_ref, bf16[128,512]{1,0:T(8,128)(2,1)S(1)} %get-tuple-element.44.kvf_ref, ...), custom_call_target="tpu_custom_call" | custom-call | flops 184549376 | bytes 2097152 | tf_op jit(solution)/shard_map/attend_begin/pallas_call | solution.py:258
  62.4 2.9 %collective-permute-done.12.refs_1_ = bf16[104,5120]{1,0:T(8,128)(2,1)S(1)} collective-permute-done((bf16[104,5120]{1,0:T(8,128)(2,1)S(1)}, bf16[104,5120]{1,0:T(8,128)(2,1)S(1)}, u32[]{:S(2)}, u32[]{:S(2)}) %collective-permute-start.12) | collective-permute-done | bytes 1064992 | tf_op jit(solution)/shard_map/ppermute | solution.py:54
  65.3 2.1 %attend_end.1 = bf16[32,8,384]{2,1,0:T(8,128)(2,1)S(1)} custom-call(bf16[128,384]{1,0:T(8,128)(2,1)S(1)} %get-tuple-element.41.q_ref, bf16[128,384]{1,0:T(8,128)(2,1)S(1)} %collective-permute-done.10.qs_ref, f32[2,256,128]{2,1,0:T(8,128)S(1)} %get-tuple-element.48.sum_ref, f32[2,256,128]{2,1,0:T(8,128)S(1)} %get-tuple-element.49.top_ref, ...), custom_call_target="tpu_custom_call" | custom-call | flops 1056964608 | bytes 2097152 | tf_op jit(solution)/shard_map/attend_end/pallas_call | solution.py:303
  67.4 13.6 %all_to_all.5.in_ref = bf16[32,8,384]{2,1,0:T(8,128)(2,1)S(1)} all-to-all(bf16[32,8,384]{2,1,0:T(8,128)(2,1)S(1)} %attend_end.1), channel_id=1, replica_groups=mesh['grp'=8,'seq'=32] {'seq'}, dimensions={0} | all-to-all | bytes 393216 | tf_op jit(solution)/shard_map/all_to_all | solution.py:367
  81.0 0.9 %combine.1 = bf16[8,4096]{1,0:T(8,128)(2,1)} custom-call(bf16[32,8,384]{2,1,0:T(8,128)(2,1)S(1)} %all_to_all.5.in_ref), custom_call_target="tpu_custom_call" | custom-call | flops 262144 | bytes 458752 | tf_op jit(solution)/shard_map/combine/pallas_call | solution.py:334
  (11 shorter events, 0.1 us)
Async XLA Ops:
  2.7 37.7 %collective-permute-start.8 = (bf16[3,5120,128]{2,1,0:T(8,128)(2,1)}, bf16[3,5120,128]{2,1,0:T(8,128)(2,1)S(1)}, u32[]{:S(2)}, u32[]{:S(2)}) collective-permute-start(bf16[3,5120,128]{2,1,0:T(8,128)(2,1)} %bitcast.6), channel_id=1, source_target_pairs={{0,1},{1,0},{2,3},{3,2},{4,5},{5,4},{6,7},{7,6},{8,9},{9,8},{10,11... | collective-permute-start | bytes 11796488 | tf_op jit(solution)/shard_map/ppermute | solution.py:54
  5.9 7.7 %collective-permute-start = (bf16[30,5248]{1,0:T(8,128)(2,1)}, bf16[30,5248]{1,0:T(8,128)(2,1)S(1)}, u32[]{:S(2)}, u32[]{:S(2)}) collective-permute-start(bf16[30,5248]{1,0:T(8,128)(2,1)} %get-tuple-element.32), channel_id=1, source_target_pairs={{0,8},{1,3},{2,10},{3,5},{4,12},{5,7},{6,14},{7,1},{8,16},{9,11},{... | collective-permute-start | bytes 944648 | tf_op jit(solution)/shard_map/ppermute | solution.py:54
  5.9 11.2 %collective-permute-start.1 = (bf16[56,5248]{1,0:T(8,128)(2,1)}, bf16[56,5248]{1,0:T(8,128)(2,1)S(1)}, u32[]{:S(2)}, u32[]{:S(2)}) collective-permute-start(bf16[56,5248]{1,0:T(8,128)(2,1)} %get-tuple-element.33.in_ref), channel_id=1, source_target_pairs={{0,24},{1,7},{2,26},{3,1},{4,28},{5,3},{6,30},{7,5},{8,0},{9,15},{... | collective-permute-start | bytes 1763336 | tf_op jit(solution)/shard_map/ppermute | solution.py:54
  8.6 8.6 %collective-permute-start.5 = (bf16[26,5120]{1,0:T(8,128)(2,1)}, bf16[26,5120]{1,0:T(8,128)(2,1)S(1)}, u32[]{:S(2)}, u32[]{:S(2)}) collective-permute-start(bf16[26,5120]{1,0:T(8,128)(2,1)} %get-tuple-element.36), channel_id=1, source_target_pairs={{0,8},{1,3},{2,10},{3,5},{4,12},{5,7},{6,14},{7,1},{8,16},{9,11},{... | collective-permute-start | bytes 798728 | tf_op jit(solution)/shard_map/ppermute | solution.py:54
  8.6 1.1 %copy-start.1 = (bf16[56,5248]{1,0:T(8,128)(2,1)S(1)}, bf16[56,5248]{1,0:T(8,128)(2,1)}, u32[]{:S(2)}) copy-start(bf16[56,5248]{1,0:T(8,128)(2,1)} %get-tuple-element.33.in_ref) | copy-start | bytes 1763332
  13.6 7.5 %collective-permute-start.2 = (bf16[30,5248]{1,0:T(8,128)(2,1)S(1)}, bf16[30,5248]{1,0:T(8,128)(2,1)S(1)}, u32[]{:S(2)}, u32[]{:S(2)}) collective-permute-start(bf16[30,5248]{1,0:T(8,128)(2,1)S(1)} %collective-permute-done.up), channel_id=1, source_target_pairs={{0,8},{1,3},{2,10},{3,5},{4,12},{5,7},{6,14},{7,1},{8,16},{9,11},{... | collective-permute-start | bytes 944648 | tf_op jit(solution)/shard_map/ppermute | solution.py:54
  17.1 7.5 %collective-permute-start.6 = (bf16[26,5120]{1,0:T(8,128)(2,1)S(1)}, bf16[26,5120]{1,0:T(8,128)(2,1)S(1)}, u32[]{:S(2)}, u32[]{:S(2)}) collective-permute-start(bf16[26,5120]{1,0:T(8,128)(2,1)S(1)} %collective-permute-done.5.up), channel_id=1, source_target_pairs={{0,8},{1,3},{2,10},{3,5},{4,12},{5,7},{6,14},{7,1},{8,16},{9,11},{... | collective-permute-start | bytes 798728 | tf_op jit(solution)/shard_map/ppermute | solution.py:54
  21.4 19.0 %collective-permute-start.4 = (bf16[120,5248]{1,0:T(8,128)(2,1)S(1)}, bf16[120,5248]{1,0:T(8,128)(2,1)S(1)}, u32[]{:S(2)}, u32[]{:S(2)}) collective-permute-start(bf16[120,5248]{1,0:T(8,128)(2,1)S(1)} %join_shards.2.refs_0_), channel_id=1, source_target_pairs={{0,6},{1,25},{2,0},{3,27},{4,2},{5,29},{6,4},{7,31},{8,14},{9,1},{... | collective-permute-start | bytes 3778568 | tf_op jit(solution)/shard_map/ppermute | solution.py:54
  24.7 29.2 %copy-start = (bf16[5120,1,3,128]{3,0,2,1:T(8,128)(2,1)S(1)}, bf16[5120,1,3,128]{3,0,2,1:T(8,128)(2,1)}, u32[]{:S(2)}) copy-start(bf16[5120,1,3,128]{3,0,2,1:T(8,128)(2,1)} %param.8) | copy-start | bytes 11796484
  25.0 15.4 %collective-permute-start.7 = (bf16[104,5120]{1,0:T(8,128)(2,1)S(1)}, bf16[104,5120]{1,0:T(8,128)(2,1)S(1)}, u32[]{:S(2)}, u32[]{:S(2)}) collective-permute-start(bf16[104,5120]{1,0:T(8,128)(2,1)S(1)} %join_shards.3.refs_1_), channel_id=1, source_target_pairs={{0,2},{1,9},{2,4},{3,11},{4,6},{5,13},{6,0},{7,15},{8,10},{9,17},{... | collective-permute-start | bytes 3194888 | tf_op jit(solution)/shard_map/ppermute | solution.py:54
  25.0 28.8 %collective-permute-start.3 = (bf16[120,5248]{1,0:T(8,128)(2,1)S(1)}, bf16[120,5248]{1,0:T(8,128)(2,1)S(1)}, u32[]{:S(2)}, u32[]{:S(2)}) collective-permute-start(bf16[120,5248]{1,0:T(8,128)(2,1)S(1)} %join_shards.2.refs_0_), channel_id=1, source_target_pairs={{0,2},{1,9},{2,4},{3,11},{4,6},{5,13},{6,0},{7,15},{8,10},{9,17},{... | collective-permute-start | bytes 3778568 | tf_op jit(solution)/shard_map/ppermute | solution.py:54
  25.3 32.7 %collective-permute-start.13 = (bf16[104,5120]{1,0:T(8,128)(2,1)S(1)}, bf16[104,5120]{1,0:T(8,128)(2,1)S(1)}, u32[]{:S(2)}, u32[]{:S(2)}) collective-permute-start(bf16[104,5120]{1,0:T(8,128)(2,1)S(1)} %join_shards.3.refs_1_), channel_id=1, source_target_pairs={{0,6},{1,25},{2,0},{3,27},{4,2},{5,29},{6,4},{7,31},{8,14},{9,1},{... | collective-permute-start | bytes 3194888 | tf_op jit(solution)/shard_map/ppermute | solution.py:54
  40.5 13.4 %collective-permute-start.9 = (bf16[32,5248]{1,0:T(8,128)(2,1)S(1)}, bf16[32,5248]{1,0:T(8,128)(2,1)S(1)}, u32[]{:S(2)}, u32[]{:S(2)}) collective-permute-start(bf16[32,5248]{1,0:T(8,128)(2,1)S(1)} %get-tuple-element.39), channel_id=1, source_target_pairs={{0,6},{1,25},{2,0},{3,27},{4,2},{5,29},{6,4},{7,31},{8,14},{9,1},{... | collective-permute-start | bytes 1007624 | tf_op jit(solution)/shard_map/ppermute | solution.py:54
  40.5 24.7 %collective-permute-start.12 = (bf16[104,5120]{1,0:T(8,128)(2,1)S(1)}, bf16[104,5120]{1,0:T(8,128)(2,1)S(1)}, u32[]{:S(2)}, u32[]{:S(2)}) collective-permute-start(bf16[104,5120]{1,0:T(8,128)(2,1)S(1)} %collective-permute-done.7.refs_3_), channel_id=1, source_target_pairs={{0,2},{1,9},{2,4},{3,11},{4,6},{5,13},{6,0},{7,15},{8,10},{9,17},{... | collective-permute-start | bytes 3194888 | tf_op jit(solution)/shard_map/ppermute | solution.py:54
  42.0 20.3 %collective-permute-start.11 = (bf16[88,5120]{1,0:T(8,128)(2,1)S(1)}, bf16[88,5120]{1,0:T(8,128)(2,1)S(1)}, u32[]{:S(2)}, u32[]{:S(2)}) collective-permute-start(bf16[88,5120]{1,0:T(8,128)(2,1)S(1)} %get-tuple-element.42), channel_id=1, source_target_pairs={{0,6},{1,25},{2,0},{3,27},{4,2},{5,29},{6,4},{7,31},{8,14},{9,1},{... | collective-permute-start | bytes 2703368 | tf_op jit(solution)/shard_map/ppermute | solution.py:54
  55.1 6.1 %collective-permute-start.10 = (bf16[128,384]{1,0:T(8,128)(2,1)S(1)}, bf16[128,384]{1,0:T(8,128)(2,1)S(1)}, u32[]{:S(2)}, u32[]{:S(2)}) collective-permute-start(bf16[128,384]{1,0:T(8,128)(2,1)S(1)} %get-tuple-element.41.q_ref), channel_id=1, source_target_pairs={{0,1},{1,0},{2,3},{3,2},{4,5},{5,4},{6,7},{7,6},{8,9},{9,8},{10,11... | collective-permute-start | bytes 294920 | tf_op jit(solution)/shard_map/ppermute | solution.py:54

commit v7 on v6

--- a/solution.py
+++ b/solution.py
@@ -61,7 +61,7 @@
     return pltpu.CompilerParams(vmem_limit_bytes=mib * 2**20)
 
 
-def pack_kernel(place_ref, len_ref, turn_place_ref, rows_ref, turn_ref, one_ref, two_ref, both_ref):
+def pack_kernel(place_ref, len_ref, turn_place_ref, rows_ref, turn_ref, one_ref, two_ref):
     n, d = rows_ref.shape
     i0 = lax.broadcasted_iota(jnp.int32, (n, n), 0)
     i1 = lax.broadcasted_iota(jnp.int32, (n, n), 1)
@@ -78,16 +78,14 @@
     pick = jnp.where(k0 == rank_row, 1.0, 0.0).astype(BF16)
     live = jnp.dot(pick, rows_ref[...], preferred_element_type=F32)
     two_ref[...] = live[PART:].astype(BF16)
-    rows = jnp.concatenate([turn_ref[...].astype(F32), live], axis=0).astype(BF16)
+    rows = jnp.concatenate([turn_ref[...].astype(F32), live[:PART]], axis=0).astype(BF16)
     m = TURN + PART
-    one_ref[:, :d] = rows[:m]
-    both_ref[:, :d] = rows
-    t0 = lax.broadcasted_iota(jnp.int32, (TURN + LIVE, TURN), 0)
-    t1 = lax.broadcasted_iota(jnp.int32, (TURN + LIVE, TURN), 1)
+    one_ref[:, :d] = rows
+    t0 = lax.broadcasted_iota(jnp.int32, (m, TURN), 0)
+    t1 = lax.broadcasted_iota(jnp.int32, (m, TURN), 1)
     turn_col = jnp.sum(jnp.where(t0 == t1, turn_place_ref[...], 0), axis=1, keepdims=True)
-    places = jnp.broadcast_to(turn_col.astype(F32), (TURN + LIVE, HD)).astype(BF16)
-    one_ref[:, d:] = places[:m]
-    both_ref[:, d:] = places
+    places = jnp.broadcast_to(turn_col.astype(F32), (m, HD)).astype(BF16)
+    one_ref[:, d:] = places
 
 
 def pack(row_place, cache_len, group_place, cache_hidden, group_hidden):
@@ -97,34 +95,33 @@
     return pl.pallas_call(
         pack_kernel,
         in_specs=[VMEM] * 5,
-        out_specs=[VMEM] * 3,
-        out_shape=[jax.ShapeDtypeStruct(s, BF16) for s in ((m, d + HD), (REST, d), (m + REST, d + HD))],
+        out_specs=[VMEM] * 2,
+        out_shape=[jax.ShapeDtypeStruct(s, BF16) for s in ((m, d + HD), (REST, d))],
         compiler_params=limit(56),
         cost_estimate=pl.CostEstimate(flops=2 * n * LIVE * d, bytes_accessed=4 * n * d, transcendentals=0),
         name="pack_live",
     )(*args)
 
 
-def stage_kernel(in_ref, out_ref):
-    out_ref[...] = in_ref[...]
-
-
-def stage(x):
+def stage_kernel(a, b, out_a, out_b):
+    out_a[...] = a[...]
+    out_b[...] = b[...]
+
+
+def stage(*x):
     return pl.pallas_call(
         stage_kernel,
-        in_specs=[VMEM],
-        out_specs=VMEM,
-        out_shape=jax.ShapeDtypeStruct(x.shape, x.dtype),
+        in_specs=[VMEM] * 2,
+        out_specs=[VMEM] * 2,
+        out_shape=[jax.ShapeDtypeStruct(v.shape, v.dtype) for v in x],
         compiler_params=limit(8),
-        cost_estimate=pl.CostEstimate(flops=0, bytes_accessed=4 * x.size, transcendentals=0),
+        cost_estimate=pl.CostEstimate(flops=0, bytes_accessed=4 * sum(v.size for v in x), transcendentals=0),
         name="stage_rows",
-    )(x)
+    )(*x)
 
 
 def join_kernel(turns, own, up, down, far, out_ref):
-    m, w = up.shape
-    half = slice(0, m) if turns else slice(own.shape[0] - m, own.shape[0])
-    x = [own[...].astype(F32)[half, :w], up[...].astype(F32), down[...].astype(F32)[half, :w], far[...].astype(F32)]
+    x = [r[...].astype(F32) for r in (own, up, down, far)]
     n = len(x) * turns
     if turns:
         out_ref[:n] = jnp.concatenate([v[:turns] for v in x], axis=0).astype(BF16)
@@ -344,13 +341,14 @@
     own = jnp.transpose(proj_weight[:, 0], (1, 0, 2))
 
     tie = lax.optimization_barrier
-    one, two, both = pack(row_place, cache_len, group_place, cache_hidden, group_hidden)
-    own, one, two, both = tie((own, one, two, both))
-    one_up, two_up, down = send(one, A_UP), send(two, A_UP), send(both, A_DOWN)
+    one, two = pack(row_place, cache_len, group_place, cache_hidden, group_hidden)
+    own, one, two = tie((own, one, two))
+    one_up, one_down = send(one, A_UP), send(one, A_DOWN)
+    two_up, two_down = send(two, A_UP), send(two, A_DOWN)
     other = send(own, SWAP)
-    one_up, staged = tie((one_up, stage(both)))
-    first = join(TURN, staged, one_up, down, send(one_up, A_UP))
-    second = join(0, staged, two_up, down, send(two_up, A_UP))
+    one_up, one, two = tie((one_up, *stage(one, two)))
+    first = join(TURN, one, one_up, one_down, send(one_up, A_UP))
+    second = join(0, two, two_up, two_down, send(two_down, A_DOWN))
     first_down, second_up = send(first, B_DOWN), send(second, B_UP)
     second_down, first_up = send(second, B_DOWN), send(first, B_UP)
     first_down, second_up, other = tie((first_down, second_up, other))

time: 82.1 us -> 81.9 us (level)
  waiting for transfers between devices: 40 us -> 36.2 us
  starting transfers between devices: 15.2 us -> 18.1 us
    ppermute x14 -> x15, waiting for transfers between devices: 40 us -> 36.2 us  [send(): return lax.ppermute(value, 'seq', pairs)]
    ppermute x14 -> x15, starting transfers between devices: 15.2 us -> 18.1 us  [send(): return lax.ppermute(value, 'seq', pairs)]
  transfers between devices with their start and end apart: 14 -> 15, of which waited for: 7 -> 8; matrix products, arithmetic and copies ran while one was open for 0% -> 0% of each run, Pallas kernels for 8% -> 9%
where the time goes in v7:
time: 81.9 us; the launch traced here: 81.7 us
  waiting for transfers between devices  36.2 us (44%)
  starting transfers between devices  18.1 us (22%)
  blocking collectives  13.6 us (17%)
  Pallas kernels  12.7 us (16%)
  local copies, waits for them, and re-layouts  1.01 us (1%)
    ppermute x15, waiting for transfers between devices, send(): return lax.ppermute(value, 'seq', pairs)  36.2 us
    ppermute x15, starting transfers between devices, send(): return lax.ppermute(value, 'seq', pairs)  18.1 us
    all_to_all x1, blocking collectives, shards(): lax.all_to_all(parts, 'seq', split_axis=0, concat_axis=0, tiled=True)  13.6 us
    pallas_call x1, Pallas kernels, cache_project(): pl.pallas_call(cache_kernel, in_specs=[VMEM] * (len(rows) + 2), out_specs...  3.24 us
    pallas_call x1, Pallas kernels, pack(): pl.pallas_call(pack_kernel, in_specs=[VMEM] * 5, out_specs=[VMEM] * 2, ou...  2.49 us
    pallas_call x1, Pallas kernels, end_attention(): pl.pallas_call(end_kernel, in_specs=[VMEM] * len(arrays), out_specs=VMEM,...  2.14 us
  transfers between devices with their start and end apart: 15, of which 8 were waited for; matrix products, arithmetic and copies ran while one was open for 0% of the time, Pallas kernels for 9%

profile of v7, /device:TPU:1, one launch (start us, length us, event | category | flops | bytes accessed | tf_op | source)
XLA Modules:
  0.0 81.7 jit_solution(16863645725013982898)
XLA Ops:
  0.0 2.5 %pack_live.1 = (bf16[30,5248]{1,0:T(8,128)(2,1)}, bf16[26,5120]{1,0:T(8,128)(2,1)}) custom-call(s32[1,64]{1,0:T(1,128)} %bitcast.10, s32[1,32]{1,0:T(1,128)} %bitcast.11, s32[1,8]{1,0:T(1,128)} %bitcast.12, bf16[64,5120]{1,0:T(8,128)(2,1)} %rows_ref.1, bf16[8,5120]{1,0:T(8,128)(2,1)} %turn_ref.1), custom_call_target="tpu_custom_call" | custom-call | flops 31457280 | bytes 1310720 | tf_op jit(solution)/shard_map/pack_live/pallas_call | solution.py:95
  2.5 3.2 %collective-permute-start.9 = (bf16[3,5120,128]{2,1,0:T(8,128)(2,1)}, bf16[3,5120,128]{2,1,0:T(8,128)(2,1)S(1)}, u32[]{:S(2)}, u32[]{:S(2)}) collective-permute-start(bf16[3,5120,128]{2,1,0:T(8,128)(2,1)} %bitcast.6), channel_id=1, source_target_pairs={{0,1},{1,0},{2,3},{3,2},{4,5},{5,4},{6,7},{7,6},{8,9},{9,8},{10,11... | collective-permute-start | bytes 11796488 | tf_op jit(solution)/shard_map/ppermute | solution.py:54
  5.7 2.7 %collective-permute-start.6 = (bf16[26,5120]{1,0:T(8,128)(2,1)}, bf16[26,5120]{1,0:T(8,128)(2,1)S(1)}, u32[]{:S(2)}, u32[]{:S(2)}) collective-permute-start(bf16[26,5120]{1,0:T(8,128)(2,1)} %get-tuple-element.33.b), channel_id=1, source_target_pairs={{0,24},{1,7},{2,26},{3,1},{4,28},{5,3},{6,30},{7,5},{8,0},{9,15},{... | collective-permute-start | bytes 798728 | tf_op jit(solution)/shard_map/ppermute | solution.py:54
  8.4 0.0 collective-permute-start.1
  8.4 1.0 %copy-done.1 = bf16[30,5248]{1,0:T(8,128)(2,1)S(1)} copy-done((bf16[30,5248]{1,0:T(8,128)(2,1)S(1)}, bf16[30,5248]{1,0:T(8,128)(2,1)}, u32[]{:S(2)}) %copy-start.1) | copy-done | bytes 314904
  9.5 1.0 %stage_rows.1 = (bf16[30,5248]{1,0:T(8,128)(2,1)S(1)}, bf16[26,5120]{1,0:T(8,128)(2,1)S(1)}) custom-call(bf16[30,5248]{1,0:T(8,128)(2,1)S(1)} %copy-done.1, bf16[26,5120]{1,0:T(8,128)(2,1)} %get-tuple-element.33.b), custom_call_target="tpu_custom_call" | custom-call | bytes 1162240 | tf_op jit(solution)/shard_map/stage_rows/pallas_call | solution.py:112
  10.5 3.0 %collective-permute-done.up = bf16[30,5248]{1,0:T(8,128)(2,1)S(1)} collective-permute-done((bf16[30,5248]{1,0:T(8,128)(2,1)}, bf16[30,5248]{1,0:T(8,128)(2,1)S(1)}, u32[]{:S(2)}, u32[]{:S(2)}) %collective-permute-start) | collective-permute-done | bytes 314912 | tf_op jit(solution)/shard_map/ppermute | solution.py:54
  13.5 2.7 %collective-permute-start.7 = (bf16[26,5120]{1,0:T(8,128)(2,1)S(1)}, bf16[26,5120]{1,0:T(8,128)(2,1)S(1)}, u32[]{:S(2)}, u32[]{:S(2)}) collective-permute-start(bf16[26,5120]{1,0:T(8,128)(2,1)S(1)} %collective-permute-done.6.down), channel_id=1, source_target_pairs={{0,24},{1,7},{2,26},{3,1},{4,28},{5,3},{6,30},{7,5},{8,0},{9,15},{... | collective-permute-start | bytes 798728 | tf_op jit(solution)/shard_map/ppermute | solution.py:54
  16.2 0.2 collective-permute-done.1.down
  16.3 4.6 %collective-permute-done.2.far = bf16[30,5248]{1,0:T(8,128)(2,1)S(1)} collective-permute-done((bf16[30,5248]{1,0:T(8,128)(2,1)S(1)}, bf16[30,5248]{1,0:T(8,128)(2,1)S(1)}, u32[]{:S(2)}, u32[]{:S(2)}) %collective-permute-start.2) | collective-permute-done | bytes 314912 | tf_op jit(solution)/shard_map/ppermute | solution.py:54
  21.0 0.2 join_shards.2.refs_0_
  21.2 1.1 %collective-permute-start.4 = (bf16[120,5248]{1,0:T(8,128)(2,1)S(1)}, bf16[120,5248]{1,0:T(8,128)(2,1)S(1)}, u32[]{:S(2)}, u32[]{:S(2)}) collective-permute-start(bf16[120,5248]{1,0:T(8,128)(2,1)S(1)} %join_shards.2.refs_0_), channel_id=1, source_target_pairs={{0,6},{1,25},{2,0},{3,27},{4,2},{5,29},{6,4},{7,31},{8,14},{9,1},{... | collective-permute-start | bytes 3778568 | tf_op jit(solution)/shard_map/ppermute | solution.py:54
  22.3 2.2 %collective-permute-done.5.up = bf16[26,5120]{1,0:T(8,128)(2,1)S(1)} collective-permute-done((bf16[26,5120]{1,0:T(8,128)(2,1)}, bf16[26,5120]{1,0:T(8,128)(2,1)S(1)}, u32[]{:S(2)}, u32[]{:S(2)}) %collective-permute-start.5) | collective-permute-done | bytes 266272 | tf_op jit(solution)/shard_map/ppermute | solution.py:54
  24.5 0.2 join_shards.3.refs_1_
  24.7 0.1 collective-permute-start.8
  24.8 0.3 collective-permute-start.3
  25.1 2.5 %collective-permute-start.14 = (bf16[104,5120]{1,0:T(8,128)(2,1)S(1)}, bf16[104,5120]{1,0:T(8,128)(2,1)S(1)}, u32[]{:S(2)}, u32[]{:S(2)}) collective-permute-start(bf16[104,5120]{1,0:T(8,128)(2,1)S(1)} %join_shards.3.refs_1_), channel_id=1, source_target_pairs={{0,6},{1,25},{2,0},{3,27},{4,2},{5,29},{6,4},{7,31},{8,14},{9,1},{... | collective-permute-start | bytes 3194888 | tf_op jit(solution)/shard_map/ppermute | solution.py:54
  27.6 12.6 %collective-permute-done.8.refs_3_ = bf16[104,5120]{1,0:T(8,128)(2,1)S(1)} collective-permute-done((bf16[104,5120]{1,0:T(8,128)(2,1)S(1)}, bf16[104,5120]{1,0:T(8,128)(2,1)S(1)}, u32[]{:S(2)}, u32[]{:S(2)}) %collective-permute-start.8) | collective-permute-done | bytes 1064992 | tf_op jit(solution)/shard_map/ppermute | solution.py:54
  40.2 0.1 split_block.1
  40.2 0.1 collective-permute-start.10
  40.3 1.5 %collective-permute-start.13 = (bf16[104,5120]{1,0:T(8,128)(2,1)S(1)}, bf16[104,5120]{1,0:T(8,128)(2,1)S(1)}, u32[]{:S(2)}, u32[]{:S(2)}) collective-permute-start(bf16[104,5120]{1,0:T(8,128)(2,1)S(1)} %collective-permute-done.8.refs_3_), channel_id=1, source_target_pairs={{0,2},{1,9},{2,4},{3,11},{4,6},{5,13},{6,0},{7,15},{8,10},{9,17},{... | collective-permute-start | bytes 3194888 | tf_op jit(solution)/shard_map/ppermute | solution.py:54
  41.8 1.3 %collective-permute-start.12 = (bf16[88,5120]{1,0:T(8,128)(2,1)S(1)}, bf16[88,5120]{1,0:T(8,128)(2,1)S(1)}, u32[]{:S(2)}, u32[]{:S(2)}) collective-permute-start(bf16[88,5120]{1,0:T(8,128)(2,1)S(1)} %get-tuple-element.44), channel_id=1, source_target_pairs={{0,6},{1,25},{2,0},{3,27},{4,2},{5,29},{6,4},{7,31},{8,14},{9,1},{... | collective-permute-start | bytes 2703368 | tf_op jit(solution)/shard_map/ppermute | solution.py:54
  43.1 10.6 %collective-permute-done.3.refs_1_.refs_2_ = bf16[120,5248]{1,0:T(8,128)(2,1)S(1)} collective-permute-done((bf16[120,5248]{1,0:T(8,128)(2,1)S(1)}, bf16[120,5248]{1,0:T(8,128)(2,1)S(1)}, u32[]{:S(2)}, u32[]{:S(2)}) %collective-permute-start.3) | collective-permute-done | bytes 1259552 | tf_op jit(solution)/shard_map/ppermute | solution.py:54
  53.6 1.3 %project_turn.1 = (bf16[128,384]{1,0:T(8,128)(2,1)S(1)}, bf16[128,512]{1,0:T(8,128)(2,1)S(1)}) custom-call(bf16[120,5248]{1,0:T(8,128)(2,1)S(1)} %join_shards.2.refs_0_, bf16[120,5248]{1,0:T(8,128)(2,1)S(1)} %collective-permute-done.3.refs_1_.refs_2_, bf16[120,5248]{1,0:T(8,128)(2,1)S(1)} %collective-permute-done.4.in_ref.refs_2_.refs_4_, ...), custom_call_target="tpu_custom_call" | custom-call | flops 6039797760 | bytes 1048576 | tf_op jit(solution)/shard_map/project_turn/pallas_call | solution.py:186
  54.9 2.7 %collective-permute-start.11 = (bf16[128,384]{1,0:T(8,128)(2,1)S(1)}, bf16[128,384]{1,0:T(8,128)(2,1)S(1)}, u32[]{:S(2)}, u32[]{:S(2)}) collective-permute-start(bf16[128,384]{1,0:T(8,128)(2,1)S(1)} %get-tuple-element.43.q_ref), channel_id=1, source_target_pairs={{0,1},{1,0},{2,3},{3,2},{4,5},{5,4},{6,7},{7,6},{8,9},{9,8},{10,11... | collective-permute-start | bytes 294920 | tf_op jit(solution)/shard_map/ppermute | solution.py:54
  57.6 3.2 %project_cache.1.refs_0_ = bf16[576,512]{1,0:T(8,128)(2,1)S(1)} custom-call(bf16[120,5248]{1,0:T(8,128)(2,1)S(1)} %join_shards.2.refs_0_, bf16[104,5120]{1,0:T(8,128)(2,1)S(1)} %join_shards.3.refs_1_, bf16[120,5248]{1,0:T(8,128)(2,1)S(1)} %collective-permute-done.3.refs_1_.refs_2_, bf16[104,5120]{1,0:T(8,128)(2,1)S(1)} %collective-permute-done.8.refs_3_, ...), custom_call_target="tpu_custom_call" | custom-call | flops 3019898880 | bytes 1048576 | tf_op jit(solution)/shard_map/project_cache/pallas_call | solution.py:204
  60.8 1.1 %attend_begin.1 = (f32[2,256,128]{2,1,0:T(8,128)S(1)}, f32[2,256,128]{2,1,0:T(8,128)S(1)}, f32[2,256,128]{2,1,0:T(8,128)S(1)}) custom-call(bf16[128,384]{1,0:T(8,128)(2,1)S(1)} %get-tuple-element.43.q_ref, bf16[128,384]{1,0:T(8,128)(2,1)S(1)} %collective-permute-done.11.qs_ref, bf16[128,512]{1,0:T(8,128)(2,1)S(1)} %get-tuple-element.46.kvf_ref, ...), custom_call_target="tpu_custom_call" | custom-call | flops 184549376 | bytes 2097152 | tf_op jit(solution)/shard_map/attend_begin/pallas_call | solution.py:255
  61.9 0.2 collective-permute-done.12.refs_0_
  62.1 2.9 %collective-permute-done.13.refs_1_ = bf16[104,5120]{1,0:T(8,128)(2,1)S(1)} collective-permute-done((bf16[104,5120]{1,0:T(8,128)(2,1)S(1)}, bf16[104,5120]{1,0:T(8,128)(2,1)S(1)}, u32[]{:S(2)}, u32[]{:S(2)}) %collective-permute-start.13) | collective-permute-done | bytes 1064992 | tf_op jit(solution)/shard_map/ppermute | solution.py:54
  65.1 2.1 %attend_end.1 = bf16[32,8,384]{2,1,0:T(8,128)(2,1)S(1)} custom-call(bf16[128,384]{1,0:T(8,128)(2,1)S(1)} %get-tuple-element.43.q_ref, bf16[128,384]{1,0:T(8,128)(2,1)S(1)} %collective-permute-done.11.qs_ref, f32[2,256,128]{2,1,0:T(8,128)S(1)} %get-tuple-element.50.sum_ref, f32[2,256,128]{2,1,0:T(8,128)S(1)} %get-tuple-element.51.top_ref, ...), custom_call_target="tpu_custom_call" | custom-call | flops 1056964608 | bytes 2097152 | tf_op jit(solution)/shard_map/attend_end/pallas_call | solution.py:300
  67.2 13.6 %all_to_all.5.in_ref = bf16[32,8,384]{2,1,0:T(8,128)(2,1)S(1)} all-to-all(bf16[32,8,384]{2,1,0:T(8,128)(2,1)S(1)} %attend_end.1), channel_id=1, replica_groups=mesh['grp'=8,'seq'=32] {'seq'}, dimensions={0} | all-to-all | bytes 393216 | tf_op jit(solution)/shard_map/all_to_all | solution.py:365
  80.8 0.9 %combine.1 = bf16[8,4096]{1,0:T(8,128)(2,1)} custom-call(bf16[32,8,384]{2,1,0:T(8,128)(2,1)S(1)} %all_to_all.5.in_ref), custom_call_target="tpu_custom_call" | custom-call | flops 262144 | bytes 458752 | tf_op jit(solution)/shard_map/combine/pallas_call | solution.py:331
  (13 shorter events, 0.0 us)
Async XLA Ops:
  2.5 37.7 %collective-permute-start.9 = (bf16[3,5120,128]{2,1,0:T(8,128)(2,1)}, bf16[3,5120,128]{2,1,0:T(8,128)(2,1)S(1)}, u32[]{:S(2)}, u32[]{:S(2)}) collective-permute-start(bf16[3,5120,128]{2,1,0:T(8,128)(2,1)} %bitcast.6), channel_id=1, source_target_pairs={{0,1},{1,0},{2,3},{3,2},{4,5},{5,4},{6,7},{7,6},{8,9},{9,8},{10,11... | collective-permute-start | bytes 11796488 | tf_op jit(solution)/shard_map/ppermute | solution.py:54
  5.7 7.7 %collective-permute-start = (bf16[30,5248]{1,0:T(8,128)(2,1)}, bf16[30,5248]{1,0:T(8,128)(2,1)S(1)}, u32[]{:S(2)}, u32[]{:S(2)}) collective-permute-start(bf16[30,5248]{1,0:T(8,128)(2,1)} %get-tuple-element.32.a), channel_id=1, source_target_pairs={{0,8},{1,3},{2,10},{3,5},{4,12},{5,7},{6,14},{7,1},{8,16},{9,11},{... | collective-permute-start | bytes 944648 | tf_op jit(solution)/shard_map/ppermute | solution.py:54
  5.7 7.7 %collective-permute-start.6 = (bf16[26,5120]{1,0:T(8,128)(2,1)}, bf16[26,5120]{1,0:T(8,128)(2,1)S(1)}, u32[]{:S(2)}, u32[]{:S(2)}) collective-permute-start(bf16[26,5120]{1,0:T(8,128)(2,1)} %get-tuple-element.33.b), channel_id=1, source_target_pairs={{0,24},{1,7},{2,26},{3,1},{4,28},{5,3},{6,30},{7,5},{8,0},{9,15},{... | collective-permute-start | bytes 798728 | tf_op jit(solution)/shard_map/ppermute | solution.py:54
  8.4 7.9 %collective-permute-start.1 = (bf16[30,5248]{1,0:T(8,128)(2,1)}, bf16[30,5248]{1,0:T(8,128)(2,1)S(1)}, u32[]{:S(2)}, u32[]{:S(2)}) collective-permute-start(bf16[30,5248]{1,0:T(8,128)(2,1)} %get-tuple-element.32.a), channel_id=1, source_target_pairs={{0,24},{1,7},{2,26},{3,1},{4,28},{5,3},{6,30},{7,5},{8,0},{9,15},{... | collective-permute-start | bytes 944648 | tf_op jit(solution)/shard_map/ppermute | solution.py:54
  8.4 1.0 %copy-start.1 = (bf16[30,5248]{1,0:T(8,128)(2,1)S(1)}, bf16[30,5248]{1,0:T(8,128)(2,1)}, u32[]{:S(2)}) copy-start(bf16[30,5248]{1,0:T(8,128)(2,1)} %get-tuple-element.32.a) | copy-start | bytes 944644
  13.5 7.5 %collective-permute-start.2 = (bf16[30,5248]{1,0:T(8,128)(2,1)S(1)}, bf16[30,5248]{1,0:T(8,128)(2,1)S(1)}, u32[]{:S(2)}, u32[]{:S(2)}) collective-permute-start(bf16[30,5248]{1,0:T(8,128)(2,1)S(1)} %collective-permute-done.up), channel_id=1, source_target_pairs={{0,8},{1,3},{2,10},{3,5},{4,12},{5,7},{6,14},{7,1},{8,16},{9,11},{... | collective-permute-start | bytes 944648 | tf_op jit(solution)/shard_map/ppermute | solution.py:54
  13.5 11.0 %collective-permute-start.5 = (bf16[26,5120]{1,0:T(8,128)(2,1)}, bf16[26,5120]{1,0:T(8,128)(2,1)S(1)}, u32[]{:S(2)}, u32[]{:S(2)}) collective-permute-start(bf16[26,5120]{1,0:T(8,128)(2,1)} %get-tuple-element.33.b), channel_id=1, source_target_pairs={{0,8},{1,3},{2,10},{3,5},{4,12},{5,7},{6,14},{7,1},{8,16},{9,11},{... | collective-permute-start | bytes 798728 | tf_op jit(solution)/shard_map/ppermute | solution.py:54
  13.5 11.0 %collective-permute-start.7 = (bf16[26,5120]{1,0:T(8,128)(2,1)S(1)}, bf16[26,5120]{1,0:T(8,128)(2,1)S(1)}, u32[]{:S(2)}, u32[]{:S(2)}) collective-permute-start(bf16[26,5120]{1,0:T(8,128)(2,1)S(1)} %collective-permute-done.6.down), channel_id=1, source_target_pairs={{0,24},{1,7},{2,26},{3,1},{4,28},{5,3},{6,30},{7,5},{8,0},{9,15},{... | collective-permute-start | bytes 798728 | tf_op jit(solution)/shard_map/ppermute | solution.py:54
  21.0 32.7 %copy-start = (bf16[5120,1,3,128]{3,0,2,1:T(8,128)(2,1)S(1)}, bf16[5120,1,3,128]{3,0,2,1:T(8,128)(2,1)}, u32[]{:S(2)}) copy-start(bf16[5120,1,3,128]{3,0,2,1:T(8,128)(2,1)} %param.8) | copy-start | bytes 11796484
  21.2 19.0 %collective-permute-start.4 = (bf16[120,5248]{1,0:T(8,128)(2,1)S(1)}, bf16[120,5248]{1,0:T(8,128)(2,1)S(1)}, u32[]{:S(2)}, u32[]{:S(2)}) collective-permute-start(bf16[120,5248]{1,0:T(8,128)(2,1)S(1)} %join_shards.2.refs_0_), channel_id=1, source_target_pairs={{0,6},{1,25},{2,0},{3,27},{4,2},{5,29},{6,4},{7,31},{8,14},{9,1},{... | collective-permute-start | bytes 3778568 | tf_op jit(solution)/shard_map/ppermute | solution.py:54
  24.7 15.4 %collective-permute-start.8 = (bf16[104,5120]{1,0:T(8,128)(2,1)S(1)}, bf16[104,5120]{1,0:T(8,128)(2,1)S(1)}, u32[]{:S(2)}, u32[]{:S(2)}) collective-permute-start(bf16[104,5120]{1,0:T(8,128)(2,1)S(1)} %join_shards.3.refs_1_), channel_id=1, source_target_pairs={{0,2},{1,9},{2,4},{3,11},{4,6},{5,13},{6,0},{7,15},{8,10},{9,17},{... | collective-permute-start | bytes 3194888 | tf_op jit(solution)/shard_map/ppermute | solution.py:54
  24.8 28.8 %collective-permute-start.3 = (bf16[120,5248]{1,0:T(8,128)(2,1)S(1)}, bf16[120,5248]{1,0:T(8,128)(2,1)S(1)}, u32[]{:S(2)}, u32[]{:S(2)}) collective-permute-start(bf16[120,5248]{1,0:T(8,128)(2,1)S(1)} %join_shards.2.refs_0_), channel_id=1, source_target_pairs={{0,2},{1,9},{2,4},{3,11},{4,6},{5,13},{6,0},{7,15},{8,10},{9,17},{... | collective-permute-start | bytes 3778568 | tf_op jit(solution)/shard_map/ppermute | solution.py:54
  25.1 32.5 %collective-permute-start.14 = (bf16[104,5120]{1,0:T(8,128)(2,1)S(1)}, bf16[104,5120]{1,0:T(8,128)(2,1)S(1)}, u32[]{:S(2)}, u32[]{:S(2)}) collective-permute-start(bf16[104,5120]{1,0:T(8,128)(2,1)S(1)} %join_shards.3.refs_1_), channel_id=1, source_target_pairs={{0,6},{1,25},{2,0},{3,27},{4,2},{5,29},{6,4},{7,31},{8,14},{9,1},{... | collective-permute-start | bytes 3194888 | tf_op jit(solution)/shard_map/ppermute | solution.py:54
  40.2 13.4 %collective-permute-start.10 = (bf16[32,5248]{1,0:T(8,128)(2,1)S(1)}, bf16[32,5248]{1,0:T(8,128)(2,1)S(1)}, u32[]{:S(2)}, u32[]{:S(2)}) collective-permute-start(bf16[32,5248]{1,0:T(8,128)(2,1)S(1)} %get-tuple-element.41), channel_id=1, source_target_pairs={{0,6},{1,25},{2,0},{3,27},{4,2},{5,29},{6,4},{7,31},{8,14},{9,1},{... | collective-permute-start | bytes 1007624 | tf_op jit(solution)/shard_map/ppermute | solution.py:54
  40.3 24.7 %collective-permute-start.13 = (bf16[104,5120]{1,0:T(8,128)(2,1)S(1)}, bf16[104,5120]{1,0:T(8,128)(2,1)S(1)}, u32[]{:S(2)}, u32[]{:S(2)}) collective-permute-start(bf16[104,5120]{1,0:T(8,128)(2,1)S(1)} %collective-permute-done.8.refs_3_), channel_id=1, source_target_pairs={{0,2},{1,9},{2,4},{3,11},{4,6},{5,13},{6,0},{7,15},{8,10},{9,17},{... | collective-permute-start | bytes 3194888 | tf_op jit(solution)/shard_map/ppermute | solution.py:54
  41.8 20.4 %collective-permute-start.12 = (bf16[88,5120]{1,0:T(8,128)(2,1)S(1)}, bf16[88,5120]{1,0:T(8,128)(2,1)S(1)}, u32[]{:S(2)}, u32[]{:S(2)}) collective-permute-start(bf16[88,5120]{1,0:T(8,128)(2,1)S(1)} %get-tuple-element.44), channel_id=1, source_target_pairs={{0,6},{1,25},{2,0},{3,27},{4,2},{5,29},{6,4},{7,31},{8,14},{9,1},{... | collective-permute-start | bytes 2703368 | tf_op jit(solution)/shard_map/ppermute | solution.py:54
  54.9 5.9 %collective-permute-start.11 = (bf16[128,384]{1,0:T(8,128)(2,1)S(1)}, bf16[128,384]{1,0:T(8,128)(2,1)S(1)}, u32[]{:S(2)}, u32[]{:S(2)}) collective-permute-start(bf16[128,384]{1,0:T(8,128)(2,1)S(1)} %get-tuple-element.43.q_ref), channel_id=1, source_target_pairs={{0,1},{1,0},{2,3},{3,2},{4,5},{5,4},{6,7},{7,6},{8,9},{9,8},{10,11... | collective-permute-start | bytes 294920 | tf_op jit(solution)/shard_map/ppermute | solution.py:54

commit v8 on v6

--- a/solution.py
+++ b/solution.py
@@ -66,8 +66,8 @@
     i0 = lax.broadcasted_iota(jnp.int32, (n, n), 0)
     i1 = lax.broadcasted_iota(jnp.int32, (n, n), 1)
     place_col = jnp.sum(jnp.where(i0 == i1, place_ref[...], 0), axis=1, keepdims=True)
-    owner = place_col // n
-    inner = place_col - owner * n
+    owner = lax.shift_right_logical(place_col, n.bit_length() - 1)
+    inner = place_col & (n - 1)
     o1 = lax.broadcasted_iota(jnp.int32, (n, len_ref.shape[1]), 1)
     length = jnp.sum(jnp.where(o1 == owner, len_ref[...], 0), axis=1, keepdims=True)
     live_col = (inner < length).astype(jnp.int32)

time: 82.1 us -> 82.1 us (level)
  no operation moved by 1% of the time
where the time goes in v8:
time: 82.1 us; the launch traced here: 81.9 us
  waiting for transfers between devices  40 us (49%)
  starting transfers between devices  15.2 us (19%)
  blocking collectives  13.6 us (17%)
  Pallas kernels  11.9 us (14%)
  local copies, waits for them, and re-layouts  1.1 us (1%)
    ppermute x14, waiting for transfers between devices, send(): return lax.ppermute(value, 'seq', pairs)  40 us
    ppermute x14, starting transfers between devices, send(): return lax.ppermute(value, 'seq', pairs)  15.2 us
    all_to_all x1, blocking collectives, shards(): lax.all_to_all(parts, 'seq', split_axis=0, concat_axis=0, tiled=True)  13.6 us
    pallas_call x1, Pallas kernels, cache_project(): pl.pallas_call(cache_kernel, in_specs=[VMEM] * (len(rows) + 2), out_specs...  3.22 us
    pallas_call x1, Pallas kernels, pack(): pl.pallas_call(pack_kernel, in_specs=[VMEM] * 5, out_specs=[VMEM] * 3, ou...  2.64 us
    pallas_call x1, Pallas kernels, end_attention(): pl.pallas_call(end_kernel, in_specs=[VMEM] * len(arrays), out_specs=VMEM,...  2.14 us
  transfers between devices with their start and end apart: 14, of which 7 were waited for; matrix products, arithmetic and copies ran while one was open for 0% of the time, Pallas kernels for 8%

profile of v8, /device:TPU:1, one launch (start us, length us, event | category | flops | bytes accessed | tf_op | source)
XLA Modules:
  0.0 81.9 jit_solution(5109377099142673682)
XLA Ops:
  0.0 2.6 %pack_live.1 = (bf16[30,5248]{1,0:T(8,128)(2,1)}, bf16[26,5120]{1,0:T(8,128)(2,1)}, bf16[56,5248]{1,0:T(8,128)(2,1)}) custom-call(s32[1,64]{1,0:T(1,128)} %bitcast.10, s32[1,32]{1,0:T(1,128)} %bitcast.11, s32[1,8]{1,0:T(1,128)} %bitcast.12, bf16[64,5120]{1,0:T(8,128)(2,1)} %rows_ref.1, bf16[8,5120]{1,0:T(8,128)(2,1)} %turn_ref.1), custom_call_target="tpu_custom_call" | custom-call | flops 31457280 | bytes 1310720 | tf_op jit(solution)/shard_map/pack_live/pallas_call | solution.py:97
  2.6 3.2 %collective-permute-start.8 = (bf16[3,5120,128]{2,1,0:T(8,128)(2,1)}, bf16[3,5120,128]{2,1,0:T(8,128)(2,1)S(1)}, u32[]{:S(2)}, u32[]{:S(2)}) collective-permute-start(bf16[3,5120,128]{2,1,0:T(8,128)(2,1)} %bitcast.6), channel_id=1, source_target_pairs={{0,1},{1,0},{2,3},{3,2},{4,5},{5,4},{6,7},{7,6},{8,9},{9,8},{10,11... | collective-permute-start | bytes 11796488 | tf_op jit(solution)/shard_map/ppermute | solution.py:54
  5.9 2.7 %collective-permute-start.1 = (bf16[56,5248]{1,0:T(8,128)(2,1)}, bf16[56,5248]{1,0:T(8,128)(2,1)S(1)}, u32[]{:S(2)}, u32[]{:S(2)}) collective-permute-start(bf16[56,5248]{1,0:T(8,128)(2,1)} %get-tuple-element.33.in_ref), channel_id=1, source_target_pairs={{0,24},{1,7},{2,26},{3,1},{4,28},{5,3},{6,30},{7,5},{8,0},{9,15},{... | collective-permute-start | bytes 1763336 | tf_op jit(solution)/shard_map/ppermute | solution.py:54
  8.6 0.0 collective-permute-start.5
  8.6 1.1 %copy-done.1 = bf16[56,5248]{1,0:T(8,128)(2,1)S(1)} copy-done((bf16[56,5248]{1,0:T(8,128)(2,1)S(1)}, bf16[56,5248]{1,0:T(8,128)(2,1)}, u32[]{:S(2)}) %copy-start.1) | copy-done | bytes 587800
  9.7 3.9 %collective-permute-done.up = bf16[30,5248]{1,0:T(8,128)(2,1)S(1)} collective-permute-done((bf16[30,5248]{1,0:T(8,128)(2,1)}, bf16[30,5248]{1,0:T(8,128)(2,1)S(1)}, u32[]{:S(2)}, u32[]{:S(2)}) %collective-permute-start) | collective-permute-done | bytes 314912 | tf_op jit(solution)/shard_map/ppermute | solution.py:54
  13.6 0.0 collective-permute-start.2
  13.6 3.5 %collective-permute-done.5.up = bf16[26,5120]{1,0:T(8,128)(2,1)S(1)} collective-permute-done((bf16[26,5120]{1,0:T(8,128)(2,1)}, bf16[26,5120]{1,0:T(8,128)(2,1)S(1)}, u32[]{:S(2)}, u32[]{:S(2)}) %collective-permute-start.5) | collective-permute-done | bytes 266272 | tf_op jit(solution)/shard_map/ppermute | solution.py:54
  17.1 4.0 %collective-permute-done.2.far = bf16[30,5248]{1,0:T(8,128)(2,1)S(1)} collective-permute-done((bf16[30,5248]{1,0:T(8,128)(2,1)S(1)}, bf16[30,5248]{1,0:T(8,128)(2,1)S(1)}, u32[]{:S(2)}, u32[]{:S(2)}) %collective-permute-start.2) | collective-permute-done | bytes 314912 | tf_op jit(solution)/shard_map/ppermute | solution.py:54
  21.1 0.2 join_shards.2.refs_0_
  21.3 0.8 collective-permute-start.4
  22.1 2.5 %collective-permute-done.6.far = bf16[26,5120]{1,0:T(8,128)(2,1)S(1)} collective-permute-done((bf16[26,5120]{1,0:T(8,128)(2,1)S(1)}, bf16[26,5120]{1,0:T(8,128)(2,1)S(1)}, u32[]{:S(2)}, u32[]{:S(2)}) %collective-permute-start.6) | collective-permute-done | bytes 266272 | tf_op jit(solution)/shard_map/ppermute | solution.py:54
  24.6 0.3 join_shards.3.refs_1_
  24.9 0.1 collective-permute-start.7
  25.0 0.3 collective-permute-start.3
  25.3 2.5 %collective-permute-start.13 = (bf16[104,5120]{1,0:T(8,128)(2,1)S(1)}, bf16[104,5120]{1,0:T(8,128)(2,1)S(1)}, u32[]{:S(2)}, u32[]{:S(2)}) collective-permute-start(bf16[104,5120]{1,0:T(8,128)(2,1)S(1)} %join_shards.3.refs_1_), channel_id=1, source_target_pairs={{0,6},{1,25},{2,0},{3,27},{4,2},{5,29},{6,4},{7,31},{8,14},{9,1},{... | collective-permute-start | bytes 3194888 | tf_op jit(solution)/shard_map/ppermute | solution.py:54
  27.8 12.6 %collective-permute-done.7.refs_3_ = bf16[104,5120]{1,0:T(8,128)(2,1)S(1)} collective-permute-done((bf16[104,5120]{1,0:T(8,128)(2,1)S(1)}, bf16[104,5120]{1,0:T(8,128)(2,1)S(1)}, u32[]{:S(2)}, u32[]{:S(2)}) %collective-permute-start.7) | collective-permute-done | bytes 1064992 | tf_op jit(solution)/shard_map/ppermute | solution.py:54
  40.4 0.1 split_block.1
  40.4 0.1 collective-permute-start.9
  40.5 1.5 %collective-permute-start.12 = (bf16[104,5120]{1,0:T(8,128)(2,1)S(1)}, bf16[104,5120]{1,0:T(8,128)(2,1)S(1)}, u32[]{:S(2)}, u32[]{:S(2)}) collective-permute-start(bf16[104,5120]{1,0:T(8,128)(2,1)S(1)} %collective-permute-done.7.refs_3_), channel_id=1, source_target_pairs={{0,2},{1,9},{2,4},{3,11},{4,6},{5,13},{6,0},{7,15},{8,10},{9,17},{... | collective-permute-start | bytes 3194888 | tf_op jit(solution)/shard_map/ppermute | solution.py:54
  42.0 1.3 %collective-permute-start.11 = (bf16[88,5120]{1,0:T(8,128)(2,1)S(1)}, bf16[88,5120]{1,0:T(8,128)(2,1)S(1)}, u32[]{:S(2)}, u32[]{:S(2)}) collective-permute-start(bf16[88,5120]{1,0:T(8,128)(2,1)S(1)} %get-tuple-element.42), channel_id=1, source_target_pairs={{0,6},{1,25},{2,0},{3,27},{4,2},{5,29},{6,4},{7,31},{8,14},{9,1},{... | collective-permute-start | bytes 2703368 | tf_op jit(solution)/shard_map/ppermute | solution.py:54
  43.3 10.6 %collective-permute-done.3.refs_1_.refs_2_ = bf16[120,5248]{1,0:T(8,128)(2,1)S(1)} collective-permute-done((bf16[120,5248]{1,0:T(8,128)(2,1)S(1)}, bf16[120,5248]{1,0:T(8,128)(2,1)S(1)}, u32[]{:S(2)}, u32[]{:S(2)}) %collective-permute-start.3) | collective-permute-done | bytes 1259552 | tf_op jit(solution)/shard_map/ppermute | solution.py:54
  53.8 0.0 collective-permute-done.9.refs_3_
  53.8 1.3 %project_turn.1 = (bf16[128,384]{1,0:T(8,128)(2,1)S(1)}, bf16[128,512]{1,0:T(8,128)(2,1)S(1)}) custom-call(bf16[120,5248]{1,0:T(8,128)(2,1)S(1)} %join_shards.2.refs_0_, bf16[120,5248]{1,0:T(8,128)(2,1)S(1)} %collective-permute-done.3.refs_1_.refs_2_, bf16[120,5248]{1,0:T(8,128)(2,1)S(1)} %collective-permute-done.4.in_ref.refs_2_.refs_4_, ...), custom_call_target="tpu_custom_call" | custom-call | flops 6039797760 | bytes 1048576 | tf_op jit(solution)/shard_map/project_turn/pallas_call | solution.py:189
  55.1 2.8 %collective-permute-start.10 = (bf16[128,384]{1,0:T(8,128)(2,1)S(1)}, bf16[128,384]{1,0:T(8,128)(2,1)S(1)}, u32[]{:S(2)}, u32[]{:S(2)}) collective-permute-start(bf16[128,384]{1,0:T(8,128)(2,1)S(1)} %get-tuple-element.41.q_ref), channel_id=1, source_target_pairs={{0,1},{1,0},{2,3},{3,2},{4,5},{5,4},{6,7},{7,6},{8,9},{9,8},{10,11... | collective-permute-start | bytes 294920 | tf_op jit(solution)/shard_map/ppermute | solution.py:54
  58.0 0.0 collective-permute-done.13.refs_5_
  58.0 3.2 %project_cache.1.refs_0_ = bf16[576,512]{1,0:T(8,128)(2,1)S(1)} custom-call(bf16[120,5248]{1,0:T(8,128)(2,1)S(1)} %join_shards.2.refs_0_, bf16[104,5120]{1,0:T(8,128)(2,1)S(1)} %join_shards.3.refs_1_, bf16[120,5248]{1,0:T(8,128)(2,1)S(1)} %collective-permute-done.3.refs_1_.refs_2_, bf16[104,5120]{1,0:T(8,128)(2,1)S(1)} %collective-permute-done.7.refs_3_, ...), custom_call_target="tpu_custom_call" | custom-call | flops 3019898880 | bytes 1048576 | tf_op jit(solution)/shard_map/project_cache/pallas_call | solution.py:207
  61.2 1.1 %attend_begin.1 = (f32[2,256,128]{2,1,0:T(8,128)S(1)}, f32[2,256,128]{2,1,0:T(8,128)S(1)}, f32[2,256,128]{2,1,0:T(8,128)S(1)}) custom-call(bf16[128,384]{1,0:T(8,128)(2,1)S(1)} %get-tuple-element.41.q_ref, bf16[128,384]{1,0:T(8,128)(2,1)S(1)} %collective-permute-done.10.qs_ref, bf16[128,512]{1,0:T(8,128)(2,1)S(1)} %get-tuple-element.44.kvf_ref, ...), custom_call_target="tpu_custom_call" | custom-call | flops 184549376 | bytes 2097152 | tf_op jit(solution)/shard_map/attend_begin/pallas_call | solution.py:258
  62.3 2.9 %collective-permute-done.12.refs_1_ = bf16[104,5120]{1,0:T(8,128)(2,1)S(1)} collective-permute-done((bf16[104,5120]{1,0:T(8,128)(2,1)S(1)}, bf16[104,5120]{1,0:T(8,128)(2,1)S(1)}, u32[]{:S(2)}, u32[]{:S(2)}) %collective-permute-start.12) | collective-permute-done | bytes 1064992 | tf_op jit(solution)/shard_map/ppermute | solution.py:54
  65.3 2.1 %attend_end.1 = bf16[32,8,384]{2,1,0:T(8,128)(2,1)S(1)} custom-call(bf16[128,384]{1,0:T(8,128)(2,1)S(1)} %get-tuple-element.41.q_ref, bf16[128,384]{1,0:T(8,128)(2,1)S(1)} %collective-permute-done.10.qs_ref, f32[2,256,128]{2,1,0:T(8,128)S(1)} %get-tuple-element.48.sum_ref, f32[2,256,128]{2,1,0:T(8,128)S(1)} %get-tuple-element.49.top_ref, ...), custom_call_target="tpu_custom_call" | custom-call | flops 1056964608 | bytes 2097152 | tf_op jit(solution)/shard_map/attend_end/pallas_call | solution.py:303
  67.4 13.6 %all_to_all.5.in_ref = bf16[32,8,384]{2,1,0:T(8,128)(2,1)S(1)} all-to-all(bf16[32,8,384]{2,1,0:T(8,128)(2,1)S(1)} %attend_end.1), channel_id=1, replica_groups=mesh['grp'=8,'seq'=32] {'seq'}, dimensions={0} | all-to-all | bytes 393216 | tf_op jit(solution)/shard_map/all_to_all | solution.py:367
  81.0 0.9 %combine.1 = bf16[8,4096]{1,0:T(8,128)(2,1)} custom-call(bf16[32,8,384]{2,1,0:T(8,128)(2,1)S(1)} %all_to_all.5.in_ref), custom_call_target="tpu_custom_call" | custom-call | flops 262144 | bytes 458752 | tf_op jit(solution)/shard_map/combine/pallas_call | solution.py:334
  (11 shorter events, 0.1 us)
Async XLA Ops:
  2.6 37.7 %collective-permute-start.8 = (bf16[3,5120,128]{2,1,0:T(8,128)(2,1)}, bf16[3,5120,128]{2,1,0:T(8,128)(2,1)S(1)}, u32[]{:S(2)}, u32[]{:S(2)}) collective-permute-start(bf16[3,5120,128]{2,1,0:T(8,128)(2,1)} %bitcast.6), channel_id=1, source_target_pairs={{0,1},{1,0},{2,3},{3,2},{4,5},{5,4},{6,7},{7,6},{8,9},{9,8},{10,11... | collective-permute-start | bytes 11796488 | tf_op jit(solution)/shard_map/ppermute | solution.py:54
  5.9 7.7 %collective-permute-start = (bf16[30,5248]{1,0:T(8,128)(2,1)}, bf16[30,5248]{1,0:T(8,128)(2,1)S(1)}, u32[]{:S(2)}, u32[]{:S(2)}) collective-permute-start(bf16[30,5248]{1,0:T(8,128)(2,1)} %get-tuple-element.32), channel_id=1, source_target_pairs={{0,8},{1,3},{2,10},{3,5},{4,12},{5,7},{6,14},{7,1},{8,16},{9,11},{... | collective-permute-start | bytes 944648 | tf_op jit(solution)/shard_map/ppermute | solution.py:54
  5.9 11.2 %collective-permute-start.1 = (bf16[56,5248]{1,0:T(8,128)(2,1)}, bf16[56,5248]{1,0:T(8,128)(2,1)S(1)}, u32[]{:S(2)}, u32[]{:S(2)}) collective-permute-start(bf16[56,5248]{1,0:T(8,128)(2,1)} %get-tuple-element.33.in_ref), channel_id=1, source_target_pairs={{0,24},{1,7},{2,26},{3,1},{4,28},{5,3},{6,30},{7,5},{8,0},{9,15},{... | collective-permute-start | bytes 1763336 | tf_op jit(solution)/shard_map/ppermute | solution.py:54
  8.6 8.6 %collective-permute-start.5 = (bf16[26,5120]{1,0:T(8,128)(2,1)}, bf16[26,5120]{1,0:T(8,128)(2,1)S(1)}, u32[]{:S(2)}, u32[]{:S(2)}) collective-permute-start(bf16[26,5120]{1,0:T(8,128)(2,1)} %get-tuple-element.36), channel_id=1, source_target_pairs={{0,8},{1,3},{2,10},{3,5},{4,12},{5,7},{6,14},{7,1},{8,16},{9,11},{... | collective-permute-start | bytes 798728 | tf_op jit(solution)/shard_map/ppermute | solution.py:54
  8.6 1.1 %copy-start.1 = (bf16[56,5248]{1,0:T(8,128)(2,1)S(1)}, bf16[56,5248]{1,0:T(8,128)(2,1)}, u32[]{:S(2)}) copy-start(bf16[56,5248]{1,0:T(8,128)(2,1)} %get-tuple-element.33.in_ref) | copy-start | bytes 1763332
  13.6 7.5 %collective-permute-start.2 = (bf16[30,5248]{1,0:T(8,128)(2,1)S(1)}, bf16[30,5248]{1,0:T(8,128)(2,1)S(1)}, u32[]{:S(2)}, u32[]{:S(2)}) collective-permute-start(bf16[30,5248]{1,0:T(8,128)(2,1)S(1)} %collective-permute-done.up), channel_id=1, source_target_pairs={{0,8},{1,3},{2,10},{3,5},{4,12},{5,7},{6,14},{7,1},{8,16},{9,11},{... | collective-permute-start | bytes 944648 | tf_op jit(solution)/shard_map/ppermute | solution.py:54
  17.1 7.5 %collective-permute-start.6 = (bf16[26,5120]{1,0:T(8,128)(2,1)S(1)}, bf16[26,5120]{1,0:T(8,128)(2,1)S(1)}, u32[]{:S(2)}, u32[]{:S(2)}) collective-permute-start(bf16[26,5120]{1,0:T(8,128)(2,1)S(1)} %collective-permute-done.5.up), channel_id=1, source_target_pairs={{0,8},{1,3},{2,10},{3,5},{4,12},{5,7},{6,14},{7,1},{8,16},{9,11},{... | collective-permute-start | bytes 798728 | tf_op jit(solution)/shard_map/ppermute | solution.py:54
  21.3 19.0 %collective-permute-start.4 = (bf16[120,5248]{1,0:T(8,128)(2,1)S(1)}, bf16[120,5248]{1,0:T(8,128)(2,1)S(1)}, u32[]{:S(2)}, u32[]{:S(2)}) collective-permute-start(bf16[120,5248]{1,0:T(8,128)(2,1)S(1)} %join_shards.2.refs_0_), channel_id=1, source_target_pairs={{0,6},{1,25},{2,0},{3,27},{4,2},{5,29},{6,4},{7,31},{8,14},{9,1},{... | collective-permute-start | bytes 3778568 | tf_op jit(solution)/shard_map/ppermute | solution.py:54
  24.6 29.2 %copy-start = (bf16[5120,1,3,128]{3,0,2,1:T(8,128)(2,1)S(1)}, bf16[5120,1,3,128]{3,0,2,1:T(8,128)(2,1)}, u32[]{:S(2)}) copy-start(bf16[5120,1,3,128]{3,0,2,1:T(8,128)(2,1)} %param.8) | copy-start | bytes 11796484
  24.9 15.4 %collective-permute-start.7 = (bf16[104,5120]{1,0:T(8,128)(2,1)S(1)}, bf16[104,5120]{1,0:T(8,128)(2,1)S(1)}, u32[]{:S(2)}, u32[]{:S(2)}) collective-permute-start(bf16[104,5120]{1,0:T(8,128)(2,1)S(1)} %join_shards.3.refs_1_), channel_id=1, source_target_pairs={{0,2},{1,9},{2,4},{3,11},{4,6},{5,13},{6,0},{7,15},{8,10},{9,17},{... | collective-permute-start | bytes 3194888 | tf_op jit(solution)/shard_map/ppermute | solution.py:54
  25.0 28.8 %collective-permute-start.3 = (bf16[120,5248]{1,0:T(8,128)(2,1)S(1)}, bf16[120,5248]{1,0:T(8,128)(2,1)S(1)}, u32[]{:S(2)}, u32[]{:S(2)}) collective-permute-start(bf16[120,5248]{1,0:T(8,128)(2,1)S(1)} %join_shards.2.refs_0_), channel_id=1, source_target_pairs={{0,2},{1,9},{2,4},{3,11},{4,6},{5,13},{6,0},{7,15},{8,10},{9,17},{... | collective-permute-start | bytes 3778568 | tf_op jit(solution)/shard_map/ppermute | solution.py:54
  25.3 32.7 %collective-permute-start.13 = (bf16[104,5120]{1,0:T(8,128)(2,1)S(1)}, bf16[104,5120]{1,0:T(8,128)(2,1)S(1)}, u32[]{:S(2)}, u32[]{:S(2)}) collective-permute-start(bf16[104,5120]{1,0:T(8,128)(2,1)S(1)} %join_shards.3.refs_1_), channel_id=1, source_target_pairs={{0,6},{1,25},{2,0},{3,27},{4,2},{5,29},{6,4},{7,31},{8,14},{9,1},{... | collective-permute-start | bytes 3194888 | tf_op jit(solution)/shard_map/ppermute | solution.py:54
  40.4 13.4 %collective-permute-start.9 = (bf16[32,5248]{1,0:T(8,128)(2,1)S(1)}, bf16[32,5248]{1,0:T(8,128)(2,1)S(1)}, u32[]{:S(2)}, u32[]{:S(2)}) collective-permute-start(bf16[32,5248]{1,0:T(8,128)(2,1)S(1)} %get-tuple-element.39), channel_id=1, source_target_pairs={{0,6},{1,25},{2,0},{3,27},{4,2},{5,29},{6,4},{7,31},{8,14},{9,1},{... | collective-permute-start | bytes 1007624 | tf_op jit(solution)/shard_map/ppermute | solution.py:54
  40.5 24.7 %collective-permute-start.12 = (bf16[104,5120]{1,0:T(8,128)(2,1)S(1)}, bf16[104,5120]{1,0:T(8,128)(2,1)S(1)}, u32[]{:S(2)}, u32[]{:S(2)}) collective-permute-start(bf16[104,5120]{1,0:T(8,128)(2,1)S(1)} %collective-permute-done.7.refs_3_), channel_id=1, source_target_pairs={{0,2},{1,9},{2,4},{3,11},{4,6},{5,13},{6,0},{7,15},{8,10},{9,17},{... | collective-permute-start | bytes 3194888 | tf_op jit(solution)/shard_map/ppermute | solution.py:54
  42.0 20.3 %collective-permute-start.11 = (bf16[88,5120]{1,0:T(8,128)(2,1)S(1)}, bf16[88,5120]{1,0:T(8,128)(2,1)S(1)}, u32[]{:S(2)}, u32[]{:S(2)}) collective-permute-start(bf16[88,5120]{1,0:T(8,128)(2,1)S(1)} %get-tuple-element.42), channel_id=1, source_target_pairs={{0,6},{1,25},{2,0},{3,27},{4,2},{5,29},{6,4},{7,31},{8,14},{9,1},{... | collective-permute-start | bytes 2703368 | tf_op jit(solution)/shard_map/ppermute | solution.py:54
  55.1 6.1 %collective-permute-start.10 = (bf16[128,384]{1,0:T(8,128)(2,1)S(1)}, bf16[128,384]{1,0:T(8,128)(2,1)S(1)}, u32[]{:S(2)}, u32[]{:S(2)}) collective-permute-start(bf16[128,384]{1,0:T(8,128)(2,1)S(1)} %get-tuple-element.41.q_ref), channel_id=1, source_target_pairs={{0,1},{1,0},{2,3},{3,2},{4,5},{5,4},{6,7},{7,6},{8,9},{9,8},{10,11... | collective-permute-start | bytes 294920 | tf_op jit(solution)/shard_map/ppermute | solution.py:54
